TPU v7x, 32 devices: a whole 2x2x4 slice. The times are simulated.
32 devices in a mesh: rows: 8 (over z, x), heads: 4 (over y, core).
Axes of the slice: x: 2, y: 2, z: 4, core: 2. Of those that a mesh axis runs over, the one named last changes fastest.
Arguments:
- tokens: bfloat16 [16384, 768], P(('rows', 'heads')), may hold values from -6 to 6
- segment: int32 [16384], P(('rows', 'heads')), may hold values from 0 to 63, as said below
- live_token: int32 [16384], P(('rows', 'heads')), may hold values from 0 to 1, as said below
- prompt_slot: int32 [16384], P(('rows', 'heads')), may hold values from 0 to 50, as said below
- prompts: bfloat16 [50, 768], replicated, may hold values from -6 to 6
- attn_gain: bfloat16 [768], replicated, may hold values from 0.5 to 1.5
- attn_shift: bfloat16 [768], replicated, may hold values from -2.5 to 2.5
- qkv_weight: bfloat16 [768, 3, 768], P('rows', None, 'heads'), may hold values from -0.21875 to 0.21875
- out_weight: bfloat16 [768, 768], P('heads', 'rows'), may hold values from -0.75 to 0.75
- mlp_gain: bfloat16 [768], replicated, may hold values from 0.5 to 1.5
- mlp_shift: bfloat16 [768], replicated, may hold values from -2.5 to 2.5
- up_weight: bfloat16 [768, 3072], P(None, ('rows', 'heads')), may hold values from -0.21875 to 0.21875
- up_bias: bfloat16 [3072], P(('rows', 'heads')), may hold values from -3 to 3
- down_weight: bfloat16 [3072, 768], P(('rows', 'heads')), may hold values from -0.109375 to 0.109375
- cotangent: bfloat16 [16384, 768], P(('rows', 'heads')), may hold values from -6 to 6
Outputs:
- output: bfloat16 [16384, 768], P(('rows', 'heads'))
- grad_tokens: float32 [16384, 768], P(('rows', 'heads'))
- grad_prompts: float32 [50, 768], replicated
- grad_attn_gain: float32 [768], replicated
- grad_attn_shift: float32 [768], replicated
- grad_qkv: float32 [768, 3, 768], P('rows', None, 'heads')
- grad_out: float32 [768, 768], P('heads', 'rows')
- grad_mlp_gain: float32 [768], replicated
- grad_mlp_shift: float32 [768], replicated
- grad_up: float32 [768, 3072], P(None, ('rows', 'heads'))
- grad_up_bias: float32 [3072], P(('rows', 'heads'))
- grad_down: float32 [3072, 768], P(('rows', 'heads'))
Inputs may be any that keep to these rules, and one draw needn't show every extreme that they name: `segment`: numbers images over all packed rows in order: packed row r holds images r * 8 to r * 8 + 7 of 247 consecutive tokens each, in that order, with padding before, between or after them; a padding token carries the number of the image before it in its row (or the row's first image). `live_token`: 1 on the tokens of images, 0 on padding; every packed row has 72 padding tokens. Within an image, token 0 is the class token, tokens 1 to 50 are prompts 0 to 49 in order, the rest are patches; prompt_slot is the prompt's number on prompt tokens and 50 on all others, padding included.
All inputs are finite; a program needn't handle non-finite values.
Results may differ from a plain program's by a relative error of at most 0.017.
Values may be sent and summed in bfloat16 or wider, within the bound.
No kernel may reach another device: no remote copies, remote signals or barrier semaphores. Data moves between devices by JAX's collectives and lax.ppermute only.
A program may use at most 128 MiB of HBM per device.

v0:
```python
import jax
import jax.numpy as jnp
from jax import lax
from jax.sharding import PartitionSpec as P

HEAD = 64
ROW = 2048


EPSILON = 1e-06


def normalize(values, scale_gain, shift_vec):
    center = values - jnp.mean(values, axis=-1, keepdims=True)
    spread = jnp.mean(center * center, axis=-1, keepdims=True)
    inverse = lax.rsqrt(spread + EPSILON)
    scaled = center * inverse
    return (scaled * scale_gain + shift_vec, scaled, inverse)


def norm_back(grad_normed, scaled, inverse, scale_gain):
    incoming = grad_normed * scale_gain
    mean_first = jnp.mean(incoming, axis=-1, keepdims=True)
    mean_second = jnp.mean(incoming * scaled, axis=-1, keepdims=True)
    return inverse * (incoming - mean_first - scaled * mean_second)


def gelu_slope(values):
    normal_cdf = 0.5 * (1.0 + jax.scipy.special.erf(values * 0.7071067811865476))
    normal_pdf = jnp.exp(-0.5 * values * values) * 0.3989422804014327
    return normal_cdf + values * normal_pdf


def block_mask(row_segment, row_live, first_row, block_rows):
    query_segment = lax.dynamic_slice_in_dim(row_segment, first_row, block_rows)
    query_live = lax.dynamic_slice_in_dim(row_live, first_row, block_rows)
    query_place = first_row + jnp.arange(block_rows, dtype=jnp.int32)
    key_place = jnp.arange(row_segment.shape[0], dtype=jnp.int32)
    same_image = (
        (query_segment[:, None] == row_segment[None, :])
        & (query_live[:, None] > 0)
        & (row_live[None, :] > 0)
    )
    return same_image | (query_place[:, None] == key_place[None, :])


def block_scores(queries, keys_row, allowed):
    raw_scores = (
        jnp.einsum("qhe,khe->hqk", queries, keys_row, preferred_element_type=jnp.float32) * 0.125
    )
    return jnp.where(allowed[None], raw_scores, -jnp.inf)


def attend_row(row_qkv, row_segment, row_live, block_rows):
    queries_all = row_qkv[:, 0]
    keys_row = row_qkv[:, 1]
    values_row = row_qkv[:, 2]
    block_count = row_qkv.shape[0] // block_rows

    def one_block(block_index):
        first_row = block_index * block_rows
        queries = lax.dynamic_slice_in_dim(queries_all, first_row, block_rows)
        allowed = block_mask(row_segment, row_live, first_row, block_rows)
        scores = block_scores(queries, keys_row, allowed)
        row_top = jnp.max(scores, axis=-1, keepdims=True)
        exp_scores = jnp.exp(scores - row_top)
        row_total = jnp.sum(exp_scores, axis=-1, keepdims=True)
        probs_low = (exp_scores / row_total).astype(jnp.bfloat16)
        mixed_rows = jnp.einsum(
            "hqk,khe->qhe", probs_low, values_row, preferred_element_type=jnp.float32
        )
        return (mixed_rows.astype(jnp.bfloat16), (row_top + jnp.log(row_total))[..., 0])

    mixed_rows, logsum = lax.map(one_block, jnp.arange(block_count, dtype=jnp.int32))
    return (mixed_rows.reshape(row_qkv.shape[0], -1), logsum)


def attend_back(row_qkv, row_segment, row_live, row_grad, logsum, block_rows):
    queries_all = row_qkv[:, 0]
    keys_row = row_qkv[:, 1]
    values_row = row_qkv[:, 2]
    block_count = row_qkv.shape[0] // block_rows

    def one_block(carried, block_index):
        grad_keys, grad_values = carried
        first_row = block_index * block_rows
        queries = lax.dynamic_slice_in_dim(queries_all, first_row, block_rows)
        grad_rows = lax.dynamic_slice_in_dim(row_grad, first_row, block_rows)
        allowed = block_mask(row_segment, row_live, first_row, block_rows)
        scores = block_scores(queries, keys_row, allowed)
        probs = jnp.exp(scores - logsum[block_index][..., None])
        grad_probs = jnp.einsum(
            "qhe,khe->hqk", grad_rows, values_row, preferred_element_type=jnp.float32
        )
        center = jnp.sum(probs * grad_probs, axis=-1, keepdims=True)
        grad_scores = (probs * (grad_probs - center)).astype(jnp.bfloat16)
        grad_queries = (
            jnp.einsum("hqk,khe->qhe", grad_scores, keys_row, preferred_element_type=jnp.float32)
            * 0.125
        )
        grad_keys = (
            grad_keys
            + jnp.einsum("hqk,qhe->khe", grad_scores, queries, preferred_element_type=jnp.float32)
            * 0.125
        )
        grad_values = grad_values + jnp.einsum(
            "hqk,qhe->khe",
            probs.astype(jnp.bfloat16),
            grad_rows,
            preferred_element_type=jnp.float32,
        )
        return ((grad_keys, grad_values), grad_queries)

    zero_rows = jnp.zeros(keys_row.shape, jnp.float32)
    (grad_keys, grad_values), grad_queries = lax.scan(
        one_block, (zero_rows, zero_rows), jnp.arange(block_count, dtype=jnp.int32)
    )
    grad_queries = grad_queries.reshape(keys_row.shape)
    return jnp.stack([grad_queries, grad_keys, grad_values], axis=1).astype(jnp.bfloat16)


def local(
    tokens,
    segment,
    live_token,
    prompt_slot,
    prompts,
    attn_gain,
    attn_shift,
    qkv_weight,
    out_weight,
    mlp_gain,
    mlp_shift,
    up_weight,
    up_bias,
    down_weight,
    cotangent,
):
    prompt_count = prompts.shape[0]
    picker = prompt_slot[:, None] == jnp.arange(prompt_count, dtype=jnp.int32)[None, :]
    picked = jnp.dot(picker.astype(jnp.bfloat16), prompts, preferred_element_type=jnp.float32)
    is_prompt = (prompt_slot < prompt_count)[:, None]
    inputs = jnp.where(is_prompt, picked, tokens.astype(jnp.float32))
    attn_scale = attn_gain.astype(jnp.float32)
    mlp_scale = mlp_gain.astype(jnp.float32)
    normed, scaled_one, inverse_one = normalize(inputs, attn_scale, attn_shift.astype(jnp.float32))
    normed_low = normed.astype(jnp.bfloat16)
    qkv_part, out_part = (
        lax.all_gather(qkv_weight, "rows", axis=0, tiled=True),
        lax.all_gather(out_weight, "rows", axis=1, tiled=True),
    )
    contract_rows = (((0,), (0,)), ((), ()))
    contract_cols = (((1,), (1,)), ((), ()))
    normed_all, segment_all, live_all = (
        lax.all_gather(normed_low, "heads", axis=0, tiled=True),
        lax.all_gather(segment, "heads", axis=0, tiled=True),
        lax.all_gather(live_token, "heads", axis=0, tiled=True),
    )
    group_rows = normed_all.shape[0]
    local_width = qkv_part.shape[2]
    local_heads = local_width // HEAD
    pack_count = group_rows // ROW
    block_rows = min(512, ROW)
    qkv_low = jnp.einsum(
        "td,dcj->tcj", normed_all, qkv_part, preferred_element_type=jnp.float32
    ).astype(jnp.bfloat16)
    qkv_rows = qkv_low.reshape(pack_count, ROW, 3, local_heads, HEAD)
    segment_rows = segment_all.reshape(pack_count, ROW)
    live_rows = live_all.reshape(pack_count, ROW)

    def forward_pack(row_items):
        return attend_row(row_items[0], row_items[1], row_items[2], block_rows)

    attended, logsum = lax.map(forward_pack, (qkv_rows, segment_rows, live_rows))
    attended = attended.reshape(group_rows, local_width)
    row_part = attended
    projected = lax.psum_scatter(
        jnp.dot(row_part, out_part, preferred_element_type=jnp.float32).astype(jnp.bfloat16),
        "heads",
        scatter_dimension=0,
        tiled=True,
    ).astype(jnp.float32)
    middle = inputs + projected
    normed_two, scaled_two, inverse_two = normalize(
        middle, mlp_scale, mlp_shift.astype(jnp.float32)
    )
    normed_two_low = normed_two.astype(jnp.bfloat16)
    up_full, bias_full, down_full = (
        lax.all_gather(up_weight, ("rows", "heads"), axis=1, tiled=True),
        lax.all_gather(up_bias, ("rows", "heads"), axis=0, tiled=True),
        lax.all_gather(down_weight, ("rows", "heads"), axis=0, tiled=True),
    )
    pre_act = jnp.dot(
        normed_two_low, up_full, preferred_element_type=jnp.float32
    ) + bias_full.astype(jnp.float32)
    activated = jax.nn.gelu(pre_act, approximate=False).astype(jnp.bfloat16)
    output = (middle + jnp.dot(activated, down_full, preferred_element_type=jnp.float32)).astype(
        jnp.bfloat16
    )
    grad_down = lax.dot_general(
        activated, cotangent, contract_rows, preferred_element_type=jnp.float32
    )
    grad_act = lax.dot_general(
        cotangent, down_full, contract_cols, preferred_element_type=jnp.float32
    )
    grad_pre = (grad_act * gelu_slope(pre_act)).astype(jnp.bfloat16)
    grad_bias = jnp.sum(grad_pre.astype(jnp.float32), axis=0)
    grad_up = lax.dot_general(
        normed_two_low, grad_pre, contract_rows, preferred_element_type=jnp.float32
    )
    grad_norm_two = lax.dot_general(
        grad_pre, up_full, contract_cols, preferred_element_type=jnp.float32
    )
    grad_up_all, grad_bias_all, grad_down_all = (
        lax.psum_scatter(grad_up, ("rows", "heads"), scatter_dimension=1, tiled=True),
        lax.psum_scatter(grad_bias, ("rows", "heads"), scatter_dimension=0, tiled=True),
        lax.psum_scatter(grad_down, ("rows", "heads"), scatter_dimension=0, tiled=True),
    )
    mlp_gain_grad = jnp.sum(grad_norm_two * scaled_two, axis=0)
    mlp_shift_grad = jnp.sum(grad_norm_two, axis=0)
    grad_middle = cotangent.astype(jnp.float32) + norm_back(
        grad_norm_two, scaled_two, inverse_two, mlp_scale
    )
    grad_proj_low = grad_middle.astype(jnp.bfloat16)
    grad_proj_all = lax.all_gather(grad_proj_low, "heads", axis=0, tiled=True)
    grad_out = lax.dot_general(
        attended, grad_proj_all, contract_rows, preferred_element_type=jnp.float32
    )
    grad_att = lax.dot_general(
        grad_proj_all, out_part, contract_cols, preferred_element_type=jnp.float32
    ).astype(jnp.bfloat16)
    grad_att_rows = grad_att.reshape(pack_count, ROW, local_heads, HEAD)

    def back_pack(row_items):
        return attend_back(
            row_items[0], row_items[1], row_items[2], row_items[3], row_items[4], block_rows
        )

    grad_qkv_rows = lax.map(back_pack, (qkv_rows, segment_rows, live_rows, grad_att_rows, logsum))
    grad_qkv_low = grad_qkv_rows.reshape(group_rows, 3, local_width)
    grad_qkv_weight = jnp.einsum(
        "td,tcj->dcj", normed_all, grad_qkv_low, preferred_element_type=jnp.float32
    )
    row_part = grad_qkv_low
    grad_norm_one = lax.psum_scatter(
        jnp.einsum("tcj,dcj->td", row_part, qkv_part, preferred_element_type=jnp.float32).astype(
            jnp.bfloat16
        ),
        "heads",
        scatter_dimension=0,
        tiled=True,
    ).astype(jnp.float32)
    grad_qkv_all, grad_out_all = (
        lax.psum_scatter(
            grad_qkv_weight.astype(jnp.bfloat16), "rows", scatter_dimension=0, tiled=True
        ).astype(jnp.float32),
        lax.psum_scatter(
            grad_out.astype(jnp.bfloat16), "rows", scatter_dimension=1, tiled=True
        ).astype(jnp.float32),
    )
    attn_gain_grad = jnp.sum(grad_norm_one * scaled_one, axis=0)
    attn_shift_grad = jnp.sum(grad_norm_one, axis=0)
    grad_inputs = grad_middle + norm_back(grad_norm_one, scaled_one, inverse_one, attn_scale)
    grad_tokens = jnp.where(is_prompt, 0.0, grad_inputs)
    grad_prompts = lax.dot_general(
        picker.astype(jnp.float32),
        grad_inputs,
        contract_rows,
        precision=lax.Precision.HIGHEST,
        preferred_element_type=jnp.float32,
    )
    summed = lax.psum(
        (grad_prompts, attn_gain_grad, attn_shift_grad, mlp_gain_grad, mlp_shift_grad),
        ("rows", "heads"),
    )
    return (
        output,
        grad_tokens,
        summed[0],
        summed[1],
        summed[2],
        grad_qkv_all,
        grad_out_all,
        summed[3],
        summed[4],
        grad_up_all,
        grad_bias_all,
        grad_down_all,
    )


def solution(mesh):
    return jax.shard_map(
        local,
        mesh=mesh,
        in_specs=(
            P(("rows", "heads"), None),
            P(("rows", "heads")),
            P(("rows", "heads")),
            P(("rows", "heads")),
            P(),
            P(),
            P(),
            P("rows", None, "heads"),
            P("heads", "rows"),
            P(),
            P(),
            P(None, ("rows", "heads")),
            P(("rows", "heads")),
            P(("rows", "heads"), None),
            P(("rows", "heads"), None),
        ),
        out_specs=(
            P(("rows", "heads"), None),
            P(("rows", "heads"), None),
            P(),
            P(),
            P(),
            P("rows", None, "heads"),
            P("heads", "rows"),
            P(),
            P(),
            P(None, ("rows", "heads")),
            P(("rows", "heads")),
            P(("rows", "heads"), None),
        ),
        check_vma=False,
    )
```

profile of v0, /device:TPU:0, one launch (start us, length us, event | category | flops | bytes accessed | tf_op | source)
XLA Modules:
  0.0 1018.0 jit_solution(3356947230270631312)
XLA Ops:
  13.8 40.5 %all_gather.30 = bf16[768,3,192]{2,1,0:T(4,128)(2,1)} all-gather(bf16[96,3,192]{2,1,0:T(4,128)(2,1)S(1)} %copy.36), channel_id=1, replica_groups=mesh['rows'=8,'heads'=4] {'rows'}, dimensions={0}, use_global_device_ids=true | all-gather | bytes 995328 | tf_op jit(solution)/shard_map/all_gather | solution.py:149
  67.3 33.1 %all_gather.31 = bf16[192,768]{0,1:T(8,128)(2,1)} all-gather(bf16[192,96]{0,1:T(8,128)(2,1)S(1)} %copy.39), channel_id=1, replica_groups=mesh['rows'=8,'heads'=4] {'rows'}, dimensions={1}, use_global_device_ids=true | all-gather | bytes 331776 | tf_op jit(solution)/shard_map/all_gather | solution.py:150
  105.8 95.8 %while.45 = (s32[]{:T(128)}, bf16[4,512,3,64]{1,3,2,0:T(8,128)(2,1)}, f32[4,3,512]{2,1,0:T(4,128)S(1)}, s32[4]{0:T(128)S(1)}, s32[2048]{0:T(1024)S(1)}, /*index=...) while((s32[]{:T(128)}, ...), condition=%wide.region_5.6_spmd, body=%wide.region_2.5_spmd.sunk | while | flops 848397824 | bytes 43998420 | solution.py:74
  122.4 7.3 fusion.134
  146.3 7.3 fusion.134
  156.8 6.7 fusion.132
  170.3 7.3 fusion.134
  194.3 7.3 fusion.134
  210.0 38.4 %all-reduce = bf16[3072]{0:T(1024)(128)(2,1)S(1)} all-reduce(bf16[3072]{0:T(1024)(128)(2,1)S(1)} %dynamic-update-slice), channel_id=1, replica_groups=mesh['rows'=8,'heads'=4] {'rows','heads'}, use_global_device_ids=true, to_apply=%add | all-reduce | flops 3072 | bytes 12288
  251.4 28.9 %all-gather.9.cloned.1.call-done = bf16[768,3072]{0,1:T(8,128)(2,1)} async-done(((bf16[768,96]{0,1:T(8,128)(2,1)}), bf16[768,3072]{0,1:T(8,128)(2,1)}) %all-gather.9.cloned.1.call-update) | async-done | bytes 4718608 | tf_op jit(solution)/shard_map/all_gather | solution.py:189
  280.3 20.2 %fusion.41 = (bf16[512,3072]{1,0:T(8,128)(2,1)}, f32[512,3072]{1,0:T(8,128)}) fusion(f32[3072]{0:T(1024)S(1)} %convert_element_type.102, bf16[768,3072]{0,1:T(8,128)(2,1)} %all-gather.9.cloned.1.call-done, f32[512,768]{1,0:T(8,128)} %copy-done.10, f32[768]{0:T(1024)S(1)} %convert_element_type.100, f32[768]{0:T(1024)S(1)} %convert_element_type.99, ...), kind=kOutput, calls=%fused_computation.56 | convolution fusion | flops 2521694208 | bytes 15751168 | tf_op jit(solution)/shard_map/dot_general | solution.py:193
  300.5 45.0 %all-gather.11.cloned.1.call-done = bf16[3072,768]{1,0:T(8,128)(2,1)} async-done(((bf16[96,768]{1,0:T(8,128)(2,1)}), bf16[3072,768]{1,0:T(8,128)(2,1)}) %all-gather.11.cloned.1.call-update) | async-done | bytes 4718608 | tf_op jit(solution)/shard_map/all_gather | solution.py:191
  345.5 8.0 convert_reduce_fusion
  359.3 26.9 %all-gather.13.cloned.1.call-done = bf16[2048,768]{1,0:T(8,128)(2,1)} async-done(((bf16[512,768]{1,0:T(8,128)(2,1)}), bf16[2048,768]{1,0:T(8,128)(2,1)}) %all-gather.13.cloned.1.call-update) | async-done | bytes 3145744 | tf_op jit(solution)/shard_map/all_gather | solution.py:225
  389.3 155.3 %while.46 = (s32[]{:T(128)}, f32[2048,3,64]{0,2,1:T(8,128)}, f32[2048,3,64]{0,2,1:T(8,128)}, bf16[4,512,3,64]{1,3,2,0:T(8,128)(2,1)}, s32[4]{0:T(128)S(1)}, /*in...) while((s32[]{:T(128)}, f32[2048,3,64]{0,2,1:T(8,128)}, ...), condition=%wide.region_13.14_spmd.clone, body=%wide.region_11.13_spmd.clone.sunk | while | flops 2067760640 | bytes 156710416 | solution.py:115
  566.0 28.4 %reduce-scatter.11.cloned.1.call-done = bf16[512,768]{1,0:T(8,128)(2,1)} async-done(((bf16[2048,768]{1,0:T(8,128)(2,1)}), bf16[512,768]{1,0:T(8,128)(2,1)}) %reduce-scatter.11.cloned.1.call-update) | async-done | bytes 786448 | tf_op jit(solution)/shard_map/reduce_scatter | solution.py:245
  601.4 8.4 fusion.73
  610.9 8.2 fusion.80
  619.2 6.8 add_convert_fusion
  626.1 32.9 %reduce-scatter.19.cloned.1.call-done = bf16[96,192]{1,0:T(8,128)(2,1)} async-done(((bf16[768,192]{1,0:T(8,128)(2,1)}), bf16[96,192]{1,0:T(8,128)(2,1)}) %reduce-scatter.19.cloned.1.call-update) | async-done | bytes 36880
  660.6 64.7 %reduce-scatter.13.cloned.1.call-done = bf16[96,3,192]{2,0,1:T(8,128)(2,1)} async-done(((bf16[768,3,192]{2,0,1:T(8,128)(2,1)}), bf16[96,3,192]{2,0,1:T(8,128)(2,1)}) %reduce-scatter.13.cloned.1.call-update) | async-done | bytes 110608 | tf_op jit(solution)/shard_map/reduce_scatter | solution.py:254
  727.0 40.9 %all-reduce.2 = (f32[768]{0:T(1024)}, f32[768]{0:T(1024)}, f32[768]{0:T(1024)}, f32[768]{0:T(1024)}, f32[3072]{0:T(1024)S(1)}) all-reduce(f32[768]{0:T(1024)S(1)} %get-tuple-element.209, f32[768]{0:T(1024)S(1)} %get-tuple-element.214, f32[768]{0:T(1024)S(1)} %copy-done.42, ...), channel_id=1, replica_groups=mesh['rows'=8,'heads'=4] {'rows','heads'}, use_global_device_ids=true, to_apply=%region_19.20 | all-reduce | flops 6144 | bytes 49152 | tf_op jit(solution)/shard_map/psum | solution.py:272
  768.5 97.9 %reduce-scatter.15.cloned.1.call-done = f32[768,96]{0,1:T(8,128)} async-done(((f32[768,3072]{0,1:T(8,128)}), f32[768,96]{0,1:T(8,128)}) %reduce-scatter.15.cloned.1.call-update) | async-done | bytes 294928 | tf_op jit(solution)/shard_map/reduce_scatter | solution.py:215
  866.3 142.1 %reduce-scatter.17.cloned.1.call-done = f32[96,768]{1,0:T(8,128)} async-done(((f32[3072,768]{1,0:T(8,128)}), f32[96,768]{1,0:T(8,128)}) %reduce-scatter.17.cloned.1.call-update) | async-done | bytes 294928 | tf_op jit(solution)/shard_map/reduce_scatter | solution.py:217
  (323 shorter events, 270.5 us)
Async XLA Ops:
  8.0 92.3 %all-gather.7.cloned.1.call-start = ((), (), s32[]{:S(2)}) async-start(), calls=%async_computation.6 | async-start | bytes 3932160 | tf_op jit(solution)/shard_map/all_gather | solution.py:155
  8.8 48.1 %copy-start.40 = (pred[512]{0:T(512)(128)(4,1)}, pred[512]{0:T(512)(128)(4,1)S(1)}, u32[]{:S(2)}) copy-start(pred[512]{0:T(512)(128)(4,1)S(1)} %broadcast_compare_fusion.2) | copy-start | bytes 1540
  11.9 236.6 %copy-start.6 = (f32[512,768]{1,0:T(8,128)}, f32[512,768]{1,0:T(8,128)S(1)}, u32[]{:S(2)}) copy-start(f32[512,768]{1,0:T(8,128)S(1)} %get-tuple-element.276) | copy-start | bytes 4718596
  11.9 50.2 %copy-start.47 = (s32[512]{0:T(512)S(1)}, s32[512]{0:T(512)}, u32[]{:S(2)}) copy-start(s32[512]{0:T(512)} %param.21) | copy-start | bytes 6148
  11.9 55.4 %copy-start.27 = (f32[512]{0:T(512)}, f32[512]{0:T(512)S(1)}, u32[]{:S(2)}) copy-start(f32[512]{0:T(512)S(1)} %broadcast_multiply_fusion.5) | copy-start | bytes 6148
  12.2 92.0 %copy-start.30 = (f32[512]{0:T(512)}, f32[512]{0:T(512)S(1)}, u32[]{:S(2)}) copy-start(f32[512]{0:T(512)S(1)} %add_rsqrt_fusion.1) | copy-start | bytes 6148
  13.5 235.0 %reduce-scatter.9.cloned.1.call-start = ((), (), s32[]{:S(2)}) async-start(), calls=%async_computation.7 | async-start | bytes 3932160 | tf_op jit(solution)/shard_map/reduce_scatter | solution.py:177
  208.2 72.1 %all-gather.9.cloned.1.call-start = ((), (), s32[]{:S(2)}) async-start(), calls=%async_computation.8 | async-start | bytes 4866048 | tf_op jit(solution)/shard_map/all_gather | solution.py:189
  208.8 136.8 %all-gather.11.cloned.1.call-start = ((), (), s32[]{:S(2)}) async-start(), calls=%async_computation.9 | async-start | bytes 4866048 | tf_op jit(solution)/shard_map/all_gather | solution.py:191
  209.4 176.8 %all-gather.13.cloned.1.call-start = ((), (), s32[]{:S(2)}) async-start(), calls=%async_computation.10 | async-start | bytes 3932160 | tf_op jit(solution)/shard_map/all_gather | solution.py:225
  209.7 147.4 %copy-start.35 = (f32[768]{0:T(1024)}, f32[768]{0:T(1024)S(1)}, u32[]{:S(2)}) copy-start(f32[768]{0:T(1024)S(1)} %convert_element_type.99) | copy-start | bytes 9220
  209.7 90.8 %copy-start.44 = (f32[768]{0:T(1024)}, f32[768]{0:T(1024)S(1)}, u32[]{:S(2)}) copy-start(f32[768]{0:T(1024)S(1)} %convert_element_type.100) | copy-start | bytes 9220
  249.9 107.2 %copy-start.32 = (f32[512]{0:T(512)}, f32[512]{0:T(512)S(1)}, u32[]{:S(2)}) copy-start(f32[512]{0:T(512)S(1)} %broadcast_multiply_fusion.4) | copy-start | bytes 6148
  251.4 105.7 %copy-start.38 = (f32[512]{0:T(512)}, f32[512]{0:T(512)S(1)}, u32[]{:S(2)}) copy-start(f32[512]{0:T(512)S(1)} %add_rsqrt_fusion) | copy-start | bytes 6148
  359.2 235.2 %reduce-scatter.11.cloned.1.call-start = ((), (), s32[]{:S(2)}) async-start(), calls=%async_computation.11 | async-start | bytes 3932160 | tf_op jit(solution)/shard_map/reduce_scatter | solution.py:245
  556.3 102.7 %reduce-scatter.19.cloned.1.call-start = ((), (), s32[]{:S(2)}) async-start(), calls=%async_computation.16 | async-start | bytes 442368
  559.3 166.0 %reduce-scatter.13.cloned.1.call-start = ((), (), s32[]{:S(2)}) async-start(), calls=%async_computation.13 | async-start | bytes 1327104 | tf_op jit(solution)/shard_map/reduce_scatter | solution.py:254
  566.0 202.5 %all-reduce.5.cloned.1.call-start = ((), (), s32[]{:S(2)}) async-start(), calls=%async_computation.12 | async-start | bytes 344064 | tf_op jit(solution)/shard_map/psum | solution.py:272
  601.3 265.0 %reduce-scatter.15.cloned.1.call-start = ((), (), s32[]{:S(2)}) async-start(), calls=%async_computation.14 | async-start | bytes 9732096 | tf_op jit(solution)/shard_map/reduce_scatter | solution.py:215
  609.8 398.6 %reduce-scatter.17.cloned.1.call-start = ((), (), s32[]{:S(2)}) async-start(), calls=%async_computation.15 | async-start | bytes 9732096 | tf_op jit(solution)/shard_map/reduce_scatter | solution.py:217
  619.2 107.8 %copy-start.37 = (f32[3072]{0:T(1024)S(1)}, f32[3072]{0:T(1024)}, u32[]{:S(2)}) copy-start(f32[3072]{0:T(1024)} %get-tuple-element.280) | copy-start | bytes 36868
  619.2 107.8 %copy-start.42 = (f32[768]{0:T(1024)S(1)}, f32[768]{0:T(1024)}, u32[]{:S(2)}) copy-start(f32[768]{0:T(1024)} %get-tuple-element.207) | copy-start | bytes 9220
  619.2 107.8 %copy-start.43 = (f32[768]{0:T(1024)S(1)}, f32[768]{0:T(1024)}, u32[]{:S(2)}) copy-start(f32[768]{0:T(1024)} %get-tuple-element.212) | copy-start | bytes 9220
  619.2 390.8 %copy-start.1 = (bf16[50,768]{1,0:T(8,128)(2,1)S(1)}, bf16[50,768]{1,0:T(8,128)(2,1)}, u32[]{:S(2)}) copy-start(bf16[50,768]{1,0:T(8,128)(2,1)} %param.23) | copy-start | bytes 230404
  (64 other events, 632.0 us)
Sparse Core Ops, SparseCore 0:
  13.6 31.2 all-gather.6
  208.3 37.7 reduce-scatter.8
  359.3 26.7 all-gather.12
  556.4 37.9 reduce-scatter.10
  597.5 61.4 reduce-scatter.18
  662.2 63.0 reduce-scatter.12
  731.8 134.5 reduce-scatter.14
  873.8 134.5 reduce-scatter.16
Sparse Core Ops, SparseCore 1:
  212.0 68.2 all-gather.8
  283.5 62.0 all-gather.10
  601.4 124.0 all-reduce.4
where the time goes:
time: 1030 us; the launch traced here: 1020 us
  waiting for transfers between devices  468 us (45%)
  matrix products  237 us (23%)
  blocking collectives  163 us (16%)
  other arithmetic  85.2 us (8%)
  local copies, waits for them, and re-layouts  23.3 us (2%)
  loops' own time  23.3 us (2%)
  between operations  16.9 us (2%)
    reduce_scatter x1, waiting for transfers between devices, local(): lax.psum_scatter(grad_down, ('rows', 'heads'), scatter_dimension=0, tiled...  142 us
    reduce_scatter x1, waiting for transfers between devices, local(): lax.psum_scatter(grad_up, ('rows', 'heads'), scatter_dimension=1, tiled=T...  97.9 us
    reduce_scatter x1, waiting for transfers between devices, local(): lax.psum_scatter(grad_qkv_weight.astype(jnp.bfloat16), 'rows', scatter_di...  64.7 us
    all_gather x1, waiting for transfers between devices, local(): lax.all_gather(down_weight, ('rows', 'heads'), axis=0, tiled=True)  45 us
    psum x1, blocking collectives, local(): lax.psum((grad_prompts, attn_gain_grad, attn_shift_grad, mlp_gain_grad, m...  40.9 us
    all_gather x1, blocking collectives, local(): lax.all_gather(qkv_weight, 'rows', axis=0, tiled=True)  40.5 us
    dot_general x8, matrix products, block_scores(): jnp.einsum('qhe,khe->hqk', queries, keys_row, preferred_element_type=jnp....  39 us
    unnamed x1, blocking collectives  38.4 us
  transfers between devices with their start and end apart: 11, of which 8 were waited for; matrix products, arithmetic and copies ran while one was open for 7% of the time, Pallas kernels for 0%

commit v1 on v0

v1 whole, which is shorter than its diff:
```python
import functools

import jax
import jax.numpy as jnp
from jax import lax
from jax.experimental import pallas as pl
from jax.experimental.pallas import tpu as pltpu
from jax.sharding import PartitionSpec as P

HEAD = 64
ROW = 2048
IMG = 247
IMGS_ROW = 8
PROMPTS = 50
SLOT = 272
CORE = 256
HALO = 48
EPSILON = 1e-06
AXES = ("rows", "heads")
F32 = jnp.float32
BF16 = jnp.bfloat16
VMEM_LIMIT = 56 * 1024 * 1024

NN = (((1,), (0,)), ((), ()))
NT = (((1,), (1,)), ((), ()))
TN = (((0,), (0,)), ((), ()))


def dot(left, right, dims=NN):
    return lax.dot_general(left, right, dims, preferred_element_type=F32)


def whole(shape):
    return pl.BlockSpec(shape, lambda *_: (0,) * len(shape))


def params(**more):
    return pltpu.CompilerParams(vmem_limit_bytes=VMEM_LIMIT, **more)


def cost(flops, moved, trans=0):
    return pl.CostEstimate(flops=int(flops), bytes_accessed=int(moved), transcendentals=int(trans))


SMEM = pl.BlockSpec(memory_space=pltpu.SMEM)
ANY = pl.BlockSpec(memory_space=pl.ANY)


def stats(values):
    center = values - jnp.mean(values, axis=-1, keepdims=True)
    inverse = lax.rsqrt(jnp.mean(center * center, axis=-1, keepdims=True) + EPSILON)
    return center * inverse, inverse


def norm_back(grad, hat, inverse, gain):
    inner = grad * gain
    first = jnp.mean(inner, axis=-1, keepdims=True)
    second = jnp.mean(inner * hat, axis=-1, keepdims=True)
    return inverse * (inner - first - hat * second)


def prep_kernel(
    place, own, other, halo, prom, gain, shift, x_out, n_out, cot_out, dest_own, dest_halo, d_oth
):
    step = pl.program_id(0)
    count = d_oth.shape[1]
    slots = pl.num_programs(0)
    y_at, c_at = place[2], place[3]

    @pl.when(step == 0)
    def _():
        big = 1 << 20
        spans = (
            (own[2 * count : 2 * count + 16, :count], 2 * count * y_at + count * c_at, True),
            (other[2 * count : 2 * count + 16, :count], 2 * count * y_at + count * (1 - c_at), True),
            (halo[2 * HALO : 2 * HALO + 16, :HALO], 2 * count - HALO * y_at, False),
        )
        parts = []
        for marks, base, home in spans:
            code = marks.astype(F32)[0:1].astype(jnp.int32)
            live = (code & 1) > 0
            slot = (code >> 1) - slots * y_at
            pos = base + lax.broadcasted_iota(jnp.int32, code.shape, 1)
            parts.append((live, slot, pos, home))
        starts = []
        for k in range(slots):
            low = None
            for live, slot, pos, home in parts:
                here = jnp.min(jnp.where(live & (slot == k), pos, big), axis=1, keepdims=True)
                low = here if low is None else jnp.minimum(low, here)
            starts.append(low)
        pads_own, pads_other = [
            jnp.sum(jnp.where(part[0], 0, 1), axis=1, keepdims=True) for part in parts[:2]
        ]
        befores = (c_at * pads_other, (1 - c_at) * pads_own, None)
        results = []
        for (live, slot, pos, home), before in zip(parts, befores):
            dest = jnp.full(pos.shape, -1, jnp.int32)
            for k in range(slots):
                dest = jnp.where(live & (slot == k), pos - starts[k] + k * SLOT, dest)
            if home:
                pads = jnp.where(live, 0.0, 1.0).astype(BF16)
                size = pads.shape[1]
                earlier = (
                    lax.broadcasted_iota(jnp.int32, (size, size), 0)
                    < lax.broadcasted_iota(jnp.int32, (size, size), 1)
                )
                wide = jnp.broadcast_to(pads, (16, size))
                rank = dot(wide, earlier.astype(BF16))[0:1].astype(jnp.int32) + before
                spare = (rank & (slots - 1)) * SLOT + IMG + (rank >> (slots.bit_length() - 1))
                dest = jnp.where(live, dest, spare)
            results.append(dest)
        dest_own[...] = results[0]
        d_oth[...] = results[1]
        dest_halo[...] = results[2]

    rows = step * SLOT
    tokens = cots = None
    for dest, ref, size in (
        (dest_own, own, count),
        (d_oth, other, count),
        (dest_halo, halo, HALO),
    ):
        at = rows + lax.broadcasted_iota(jnp.int32, (SLOT, size), 0)
        pick = (at == dest[...]).astype(BF16)
        one = dot(pick, ref[0:size])
        two = dot(pick, ref[size : 2 * size])
        tokens = one if tokens is None else tokens + one
        cots = two if cots is None else cots + two
    at = lax.broadcasted_iota(jnp.int32, (SLOT, 1), 0)
    inputs = jnp.where((at >= 1) & (at <= PROMPTS), prom[...].astype(F32), tokens)
    hat, _ = stats(inputs)
    x_out[...] = inputs.astype(BF16)
    n_out[...] = (hat * gain[...] + shift[...]).astype(BF16)
    cot_out[...] = cots.astype(BF16)


def prep(place, own, other, halo, prom, gain, shift, slots):
    count = own.shape[0] // 2 - 8
    wide = own.shape[1]
    rows = slots * SLOT
    tile = pl.BlockSpec((SLOT, wide), lambda t: (t, 0))
    array = jax.ShapeDtypeStruct((rows, wide), BF16)
    return pl.pallas_call(
        prep_kernel,
        grid=(slots,),
        in_specs=[SMEM] + [whole(v.shape) for v in (own, other, halo, prom, gain, shift)],
        out_specs=[tile, tile, tile, whole((1, count)), whole((1, HALO))],
        out_shape=[
            array,
            array,
            array,
            jax.ShapeDtypeStruct((1, count), jnp.int32),
            jax.ShapeDtypeStruct((1, HALO), jnp.int32),
        ],
        scratch_shapes=[pltpu.VMEM((1, count), jnp.int32)],
        compiler_params=params(),
        cost_estimate=cost(4 * rows * (2 * count + HALO) * wide, 12 * rows * wide),
        name="prep",
    )(place, own, other, halo, prom, gain, shift)


def attend_kernel(normed, weight, qkv_out, prob_out, att_out, part_out):
    third = weight.shape[2] // 4
    rows = lax.broadcasted_iota(jnp.int32, (CORE, CORE), 0)
    cols = lax.broadcasted_iota(jnp.int32, (CORE, CORE), 1)
    allowed = ((rows < IMG) & (cols < IMG)) | (rows == cols)
    total = None
    for group in range(weight.shape[0]):
        qkv_out[group] = dot(normed[...], weight[group, :, : 3 * third]).astype(BF16)
        for head in range(third // HEAD):
            at = head * HEAD
            queries = qkv_out[group, :CORE, at : at + HEAD]
            keys = qkv_out[group, :CORE, third + at : third + at + HEAD]
            values = qkv_out[group, :, 2 * third + at : 2 * third + at + HEAD]
            scores = jnp.where(allowed, dot(queries, keys, NT) * 0.125, -1e30)
            exp_scores = jnp.exp(scores - jnp.max(scores, axis=-1, keepdims=True))
            probs = (exp_scores / jnp.sum(exp_scores, axis=-1, keepdims=True)).astype(BF16)
            prob_out[0, group, head] = probs
            att_out[group, :CORE, at : at + HEAD] = dot(probs, values[:CORE]).astype(BF16)
            att_out[group, CORE:, at : at + HEAD] = values[CORE:]
        part = dot(att_out[group], weight[group, :, 3 * third :], NT)
        total = part if total is None else total + part
    part_out[...] = total.astype(BF16)


def attend(normed, weight, slots):
    groups, deep, wide = weight.shape
    third = wide // 4
    heads = third // HEAD
    rows = slots * SLOT
    return pl.pallas_call(
        attend_kernel,
        grid=(slots,),
        in_specs=[pl.BlockSpec((SLOT, deep), lambda t: (t, 0)), whole(weight.shape)],
        out_specs=[
            pl.BlockSpec((groups, SLOT, 3 * third), lambda t: (0, t, 0)),
            pl.BlockSpec((1, groups, heads, CORE, CORE), lambda t: (t, 0, 0, 0, 0)),
            pl.BlockSpec((groups, SLOT, third), lambda t: (0, t, 0)),
            pl.BlockSpec((SLOT, deep), lambda t: (t, 0)),
        ],
        out_shape=[
            jax.ShapeDtypeStruct((groups, rows, 3 * third), BF16),
            jax.ShapeDtypeStruct((slots, groups, heads, CORE, CORE), BF16),
            jax.ShapeDtypeStruct((groups, rows, third), BF16),
            jax.ShapeDtypeStruct((rows, deep), BF16),
        ],
        compiler_params=params(),
        cost_estimate=cost(2 * rows * deep * groups * wide * 1.6, 12 * rows * deep),
        name="attend",
    )(normed, weight)


def mid_kernel(x_in, one, two, gain, shift, middle_out, n_out):
    middle = x_in[...].astype(F32) + one[...].astype(F32) + two[...].astype(F32)
    middle_out[...] = middle
    hat, _ = stats(middle)
    n_out[...] = (hat * gain[...] + shift[...]).astype(BF16)


def mid(x_in, one, two, gain, shift, slots):
    rows, wide = x_in.shape
    tile = pl.BlockSpec((SLOT, wide), lambda t: (t, 0))
    return pl.pallas_call(
        mid_kernel,
        grid=(slots,),
        in_specs=[tile, tile, tile, whole(gain.shape), whole(shift.shape)],
        out_specs=[tile, tile],
        out_shape=[jax.ShapeDtypeStruct(x_in.shape, F32), jax.ShapeDtypeStruct(x_in.shape, BF16)],
        compiler_params=params(),
        cost_estimate=cost(20 * rows * wide, 12 * rows * wide),
        name="mid",
    )(x_in, one, two, gain, shift)


def mlp_kernel(more, *refs):
    if more:
        (a_in, b_in, normed, cot, bias, o_acc, g_acc, *refs) = refs
    else:
        (a_in, b_in, normed, cot, bias, *refs) = refs
    (o_out, g_out, a_out, b_out, bias_out, weight, act, grad, result, in_sem, out_sem) = refs
    step = pl.program_id(0)
    lead, count, _, span, _ = a_in.shape
    hidden = weight.shape[1]

    def pieces(first, second):
        for source, ref in enumerate((first, second)):
            for i in range(lead):
                for j in range(count):
                    for kind in range(2):
                        place = ((source * lead + i) * count + j) * span
                        index = ((source * lead + i) * count + j) * 2 + kind
                        yield ref.at[i, j, kind], kind, place, index

    @pl.when(step == 0)
    def _():
        copies = [
            pltpu.make_async_copy(ref, weight.at[kind, pl.ds(place, span)], in_sem.at[index])
            for ref, kind, place, index in pieces(a_in, b_in)
        ]
        for copy in copies:
            copy.start()
        bias_out[...] = jnp.zeros_like(bias_out)
        for copy in copies:
            copy.wait()

    rows = pl.ds(pl.multiple_of(step * SLOT, 16), SLOT)
    tile_n = normed[rows]
    tile_c = cot[rows]
    cut = 256
    o_sum = o_acc[...] if more else None
    g_sum = g_acc[...] if more else None
    for at in range(0, hidden, cut):
        up = weight[0, at : at + cut]
        down = weight[1, at : at + cut]
        pre = dot(tile_n, up, NT) + bias[:, at : at + cut]
        cdf = 0.5 * (1.0 + lax.erf(pre * 0.7071067811865476))
        pdf = jnp.exp(-0.5 * pre * pre) * 0.3989422804014327
        low = (pre * cdf).astype(BF16)
        grad_low = (dot(tile_c, down, NT) * (cdf + pre * pdf)).astype(BF16)
        act[rows, at : at + cut] = low
        grad[rows, at : at + cut] = grad_low
        bias_out[:, at : at + cut] += jnp.sum(grad_low.astype(F32), axis=0, keepdims=True)
        o_part = dot(low, down)
        g_part = dot(grad_low, up)
        o_sum = o_part if o_sum is None else o_sum + o_part
        g_sum = g_part if g_sum is None else g_sum + g_part
    o_out[...] = o_sum.astype(o_out.dtype)
    g_out[...] = g_sum.astype(g_out.dtype)

    @pl.when(step == pl.num_programs(0) - 1)
    def _():
        def tile(i, _):
            at = pl.ds(pl.multiple_of(i * cut, cut), cut)
            result[0, at] = dot(grad[:, at], normed[...], TN).astype(BF16)
            result[1, at] = dot(act[:, at], cot[...], TN).astype(BF16)
            return 0

        lax.fori_loop(0, hidden // cut, tile, 0)
        copies = [
            pltpu.make_async_copy(result.at[kind, pl.ds(place, span)], ref, out_sem.at[index])
            for ref, kind, place, index in pieces(a_out, b_out)
        ]
        for copy in copies:
            copy.start()
        for copy in copies:
            copy.wait()


def mlp(a_in, b_in, normed, cot, bias, slots, sums=None):
    rows, wide = normed.shape
    hidden = bias.shape[1]
    more = sums is not None
    tile = pl.BlockSpec((SLOT, wide), lambda t: (t, 0))
    kept = BF16 if more else F32
    count = 4 * a_in.shape[0] * a_in.shape[1]
    return pl.pallas_call(
        functools.partial(mlp_kernel, more),
        grid=(slots,),
        in_specs=[ANY, ANY, whole(normed.shape), whole(cot.shape), whole(bias.shape)]
        + ([tile, tile] if more else []),
        out_specs=[tile, tile, ANY, ANY, whole(bias.shape)],
        out_shape=[
            jax.ShapeDtypeStruct((rows, wide), kept),
            jax.ShapeDtypeStruct((rows, wide), kept),
            jax.ShapeDtypeStruct(a_in.shape, BF16),
            jax.ShapeDtypeStruct(b_in.shape, BF16),
            jax.ShapeDtypeStruct(bias.shape, F32),
        ],
        scratch_shapes=[
            pltpu.VMEM((2, hidden, wide), BF16),
            pltpu.VMEM((rows, hidden), BF16),
            pltpu.VMEM((rows, hidden), BF16),
            pltpu.VMEM((2, hidden, wide), BF16),
            pltpu.SemaphoreType.DMA((count,)),
            pltpu.SemaphoreType.DMA((count,)),
        ],
        compiler_params=params(),
        cost_estimate=cost(12 * rows * hidden * wide, 14 * rows * wide, 2 * rows * hidden),
        name="mlp",
    )(a_in, b_in, normed, cot, bias, *(sums or ()))


def finish_kernel(middle, one, two, dest_own, dest_halo, own_out, halo_out, total, total_halo):
    step = pl.program_id(0)
    value = middle[...] + one[...].astype(F32) + two[...].astype(F32)
    spread_rows(step, value.astype(BF16), dest_own, dest_halo, total, total_halo)

    @pl.when(step == pl.num_programs(0) - 1)
    def _():
        own_out[...] = total[...].astype(own_out.dtype)
        halo_out[...] = total_halo[...].astype(halo_out.dtype)


def spread_rows(step, value, dest_own, dest_halo, total, total_halo):
    for dest, sum_ref in ((dest_own, total), (dest_halo, total_halo)):
        at = step * SLOT + lax.broadcasted_iota(jnp.int32, (SLOT, dest.shape[1]), 0)
        part = dot((at == dest[...]).astype(BF16), value, TN)
        sum_ref[...] = jnp.where(step == 0, part, sum_ref[...] + part)


def finish(middle, one, two, dest_own, dest_halo, slots):
    rows, wide = middle.shape
    count = dest_own.shape[1]
    tile = pl.BlockSpec((SLOT, wide), lambda t: (t, 0))
    return pl.pallas_call(
        finish_kernel,
        grid=(slots,),
        in_specs=[tile, tile, tile, whole(dest_own.shape), whole(dest_halo.shape)],
        out_specs=[whole((count, wide)), whole((HALO, wide))],
        out_shape=[
            jax.ShapeDtypeStruct((count, wide), BF16),
            jax.ShapeDtypeStruct((HALO, wide), BF16),
        ],
        scratch_shapes=[pltpu.VMEM((count, wide), F32), pltpu.VMEM((HALO, wide), F32)],
        compiler_params=params(),
        cost_estimate=cost(2 * rows * (count + HALO) * wide, 10 * rows * wide),
        name="finish",
    )(middle, one, two, dest_own, dest_halo)


def back_kernel(
    middle, one, two, cot, gain, weight, qkv, prob, gm_out, gp_out, dq_out, part_out, sums_out
):
    step = pl.program_id(0)
    third = weight.shape[2] // 4

    @pl.when(step == 0)
    def _():
        sums_out[...] = jnp.zeros_like(sums_out)

    grad = one[...].astype(F32) + two[...].astype(F32)
    hat, inverse = stats(middle[...])
    sums_out[0:1] += jnp.sum(grad * hat, axis=0, keepdims=True)
    sums_out[1:2] += jnp.sum(grad, axis=0, keepdims=True)
    grad_middle = cot[...].astype(F32) + norm_back(grad, hat, inverse, gain[...])
    gm_out[...] = grad_middle
    grad_proj = grad_middle.astype(BF16)
    gp_out[...] = grad_proj
    total = None
    for group in range(weight.shape[0]):
        grad_att = dot(grad_proj, weight[group, :, 3 * third :]).astype(BF16)
        for head in range(third // HEAD):
            at = head * HEAD
            queries = qkv[group, :CORE, at : at + HEAD]
            keys = qkv[group, :CORE, third + at : third + at + HEAD]
            values = qkv[group, :CORE, 2 * third + at : 2 * third + at + HEAD]
            grad_head = grad_att[:, at : at + HEAD]
            grad_core = grad_head[:CORE]
            probs = prob[0, group, head]
            probs_wide = probs.astype(F32)
            grad_probs = dot(grad_core, values, NT)
            center = jnp.sum(probs_wide * grad_probs, axis=-1, keepdims=True)
            grad_scores = (probs_wide * (grad_probs - center)).astype(BF16)
            grad_q = (dot(grad_scores, keys) * 0.125).astype(BF16)
            grad_k = (dot(grad_scores, queries, TN) * 0.125).astype(BF16)
            grad_v = dot(probs, grad_core, TN).astype(BF16)
            blank = jnp.zeros((SLOT - CORE, HEAD), BF16)
            dq_out[group, :CORE, at : at + HEAD] = grad_q
            dq_out[group, CORE:, at : at + HEAD] = blank
            dq_out[group, :CORE, third + at : third + at + HEAD] = grad_k
            dq_out[group, CORE:, third + at : third + at + HEAD] = blank
            dq_out[group, :CORE, 2 * third + at : 2 * third + at + HEAD] = grad_v
            dq_out[group, CORE:, 2 * third + at : 2 * third + at + HEAD] = grad_head[CORE:]
        part = dot(dq_out[group], weight[group, :, : 3 * third], NT)
        total = part if total is None else total + part
    part_out[...] = total.astype(BF16)


def back(middle, one, two, cot, gain, weight, qkv, prob, slots):
    rows, wide = middle.shape
    groups, third = weight.shape[0], weight.shape[2] // 4
    tile = pl.BlockSpec((SLOT, wide), lambda t: (t, 0))
    tile_q = pl.BlockSpec((groups, SLOT, 3 * third), lambda t: (0, t, 0))
    return pl.pallas_call(
        back_kernel,
        grid=(slots,),
        in_specs=[
            tile,
            tile,
            tile,
            tile,
            whole(gain.shape),
            whole(weight.shape),
            tile_q,
            pl.BlockSpec((1,) + prob.shape[1:], lambda t: (t, 0, 0, 0, 0)),
        ],
        out_specs=[tile, tile, tile_q, tile, whole((8, wide))],
        out_shape=[
            jax.ShapeDtypeStruct((rows, wide), F32),
            jax.ShapeDtypeStruct((rows, wide), BF16),
            jax.ShapeDtypeStruct(qkv.shape, BF16),
            jax.ShapeDtypeStruct((rows, wide), BF16),
            jax.ShapeDtypeStruct((8, wide), F32),
        ],
        compiler_params=params(),
        cost_estimate=cost(2 * rows * wide * groups * 4 * third * 2, 24 * rows * wide),
        name="back",
    )(middle, one, two, cot, gain, weight, qkv, prob)


def weight_kernel(normed, grad_proj, grad_qkv, att, out):
    third = att.shape[2]
    out[0, :, : 3 * third] = dot(normed[...], grad_qkv[0], TN).astype(BF16)
    out[0, :, 3 * third :] = dot(grad_proj[...], att[0], TN).astype(BF16)


def weight_grads(normed, grad_proj, grad_qkv, att):
    rows, wide = normed.shape
    groups, _, third = att.shape
    cut = 256
    tall = pl.BlockSpec((rows, cut), lambda d, g: (0, d))
    return pl.pallas_call(
        weight_kernel,
        grid=(wide // cut, groups),
        in_specs=[
            tall,
            tall,
            pl.BlockSpec((1, rows, 3 * third), lambda d, g: (g, 0, 0)),
            pl.BlockSpec((1, rows, third), lambda d, g: (g, 0, 0)),
        ],
        out_specs=pl.BlockSpec((1, cut, 4 * third), lambda d, g: (g, d, 0)),
        out_shape=jax.ShapeDtypeStruct((groups, wide, 4 * third), BF16),
        compiler_params=params(),
        cost_estimate=cost(2 * rows * wide * groups * 4 * third, 20 * rows * wide),
        name="weight_grads",
    )(normed, grad_proj, grad_qkv, att)


def last_kernel(
    x_in, gm, one, two, gain, dest_own, dest_halo, own_out, halo_out, prompt_out, sums_out, halo_sum
):
    step = pl.program_id(0)

    @pl.when(step == 0)
    def _():
        sums_out[...] = jnp.zeros_like(sums_out)
        prompt_out[...] = jnp.zeros_like(prompt_out)

    grad = one[...].astype(F32) + two[...].astype(F32)
    hat, inverse = stats(x_in[...].astype(F32))
    sums_out[0:1] += jnp.sum(grad * hat, axis=0, keepdims=True)
    sums_out[1:2] += jnp.sum(grad, axis=0, keepdims=True)
    grad_in = gm[...] + norm_back(grad, hat, inverse, gain[...])
    prompt_out[...] += grad_in[: prompt_out.shape[0]]
    at = lax.broadcasted_iota(jnp.int32, (SLOT, 1), 0)
    value = jnp.where((at >= 1) & (at <= PROMPTS), 0.0, grad_in).astype(BF16)
    spread_rows(step, value, dest_own, dest_halo, own_out, halo_sum)

    @pl.when(step == pl.num_programs(0) - 1)
    def _():
        halo_out[...] = halo_sum[...].astype(BF16)


def last(x_in, gm, one, two, gain, dest_own, dest_halo, slots):
    rows, wide = x_in.shape
    count = dest_own.shape[1]
    tile = pl.BlockSpec((SLOT, wide), lambda t: (t, 0))
    return pl.pallas_call(
        last_kernel,
        grid=(slots,),
        in_specs=[tile] * 4 + [whole(gain.shape), whole(dest_own.shape), whole(dest_halo.shape)],
        out_specs=[whole((count, wide)), whole((HALO, wide)), whole((56, wide)), whole((8, wide))],
        out_shape=[
            jax.ShapeDtypeStruct((count, wide), F32),
            jax.ShapeDtypeStruct((HALO, wide), BF16),
            jax.ShapeDtypeStruct((56, wide), F32),
            jax.ShapeDtypeStruct((8, wide), F32),
        ],
        scratch_shapes=[pltpu.VMEM((HALO, wide), F32)],
        compiler_params=params(),
        cost_estimate=cost(2 * rows * (count + HALO) * wide, 10 * rows * wide),
        name="last",
    )(x_in, gm, one, two, gain, dest_own, dest_halo)


class Grid:
    def __init__(self, rows, heads):
        self.deep = rows // 2
        self.size = rows * heads
        row = lax.axis_index("rows")
        col = lax.axis_index("heads")
        self.z = row // 2
        self.x = row % 2
        self.y = col // 2
        self.c = col % 2

    def send(self, value, move):
        pairs = []
        for i in range(self.size):
            z, x, y, c = move(i // 8, (i // 4) % 2, (i // 2) % 2, i % 2)
            pairs.append((i, ((z * 2 + x) * 2 + y) * 2 + c))
        return lax.ppermute(value, AXES, pairs)

    def by_x(self, value):
        return self.send(value, lambda z, x, y, c: (z, 1 - x, y, c))

    def by_y(self, value):
        return self.send(value, lambda z, x, y, c: (z, x, 1 - y, c))

    def by_core(self, value):
        return self.send(value, lambda z, x, y, c: (z, x, y, 1 - c))

    def by_z(self, value, shift):
        return self.send(value, lambda z, x, y, c: ((z + shift) % self.deep, x, y, c))

    def gather_z(self, value):
        return [value] + [self.by_z(value, k) for k in range(1, self.deep)]

    def scatter_z(self, values):
        got = [self.by_z(values[k], self.deep - k) for k in range(1, self.deep)]
        total = values[0].astype(F32)
        for item in got:
            total = total + item.astype(F32)
        return total

    def spread(self, first, second):
        a_next, b_next = tie(self.by_y(first), self.by_x(second))
        a_zero = jnp.stack([first, a_next])
        b_zero = jnp.stack([second, b_next])
        return a_zero, b_zero

    def spread_more(self, a_zero, b_zero):
        return self.by_x(a_zero), self.by_y(b_zero)

    def fold(self, a_zero, b_zero, a_one, b_one):
        a_got, b_got = tie(self.by_x(a_one), self.by_y(b_one))
        a_last, b_last = tie(
            self.by_y(plus(a_zero[1], a_got[1])), self.by_x(plus(b_zero[1], b_got[1]))
        )
        return plus(a_zero[0], a_got[0], a_last), plus(b_zero[0], b_got[0], b_last)

    def to_absolute(self, blocks, z_axis, x_axis):
        size = self.deep
        turned = jnp.take(blocks, jnp.asarray([-m % size for m in range(size)]), axis=z_axis)
        turned = jnp.roll(turned, self.z, axis=z_axis)
        return jnp.where(self.x == 0, turned, jnp.flip(turned, axis=x_axis))

    def to_relative(self, blocks, z_axis, x_axis):
        size = self.deep
        turned = jnp.where(self.x == 0, blocks, jnp.flip(blocks, axis=x_axis))
        turned = jnp.roll(turned, -self.z, axis=z_axis)
        return jnp.take(turned, jnp.asarray([-m % size for m in range(size)]), axis=z_axis)


def tie(*values):
    return lax.optimization_barrier(values)


def plus(*values):
    total = values[0].astype(F32)
    for item in values[1:]:
        total = total + item.astype(F32)
    return total.astype(values[0].dtype)


def local(
    rows,
    heads,
    tokens,
    segment,
    live_token,
    prompt_slot,
    prompts,
    attn_gain,
    attn_shift,
    qkv_weight,
    out_weight,
    mlp_gain,
    mlp_shift,
    up_weight,
    up_bias,
    down_weight,
    cotangent,
):
    grid = Grid(rows, heads)
    deep = grid.deep
    count, wide = tokens.shape
    slots = IMGS_ROW * 2 * count // ROW
    place = jnp.stack([grid.z, grid.x, grid.y, grid.c]).astype(jnp.int32)

    def row_of(vec):
        return vec.astype(F32).reshape(1, -1)

    depth = qkv_weight.shape[0]
    third = qkv_weight.shape[2]
    shard = jnp.concatenate(
        [qkv_weight.reshape(depth, 3 * third), out_weight.swapaxes(0, 1)], axis=1
    ).reshape(2, depth // 2, 4 * third)
    got = grid.gather_z(shard)
    got = list(tie(*got))
    a_zero, b_zero = grid.spread(jnp.stack([g[0] for g in got]), jnp.stack([g[1] for g in got]))
    a_one, b_one = grid.spread_more(a_zero, b_zero)

    code = ((segment % IMGS_ROW) * 2 + live_token).astype(BF16)
    marks = jnp.pad(code[None], ((0, 15), (0, wide - count)))
    own = jnp.concatenate([tokens, cotangent, marks])
    other = grid.by_core(own)
    edge_source = jnp.where(grid.c == 1 - grid.y, 1, 0)
    first_row = jnp.where(grid.y == 0, count - HALO, 0)
    edge_parts = []
    for base, size in ((0, HALO), (count, HALO)):
        mine = lax.dynamic_slice_in_dim(own, base + first_row, size)
        theirs = lax.dynamic_slice_in_dim(other, base + first_row, size)
        edge_parts.append(jnp.where(edge_source == 1, mine, theirs))
    code_source = jnp.where(edge_source == 1, own[2 * count], other[2 * count])
    edge_code = lax.dynamic_slice_in_dim(code_source, first_row, HALO)
    edge_parts.append(jnp.pad(edge_code[None], ((0, 15), (0, wide - HALO))))
    halo = grid.by_y(jnp.concatenate(edge_parts))
    prom = jnp.pad(prompts, ((1, SLOT - PROMPTS - 1), (0, 0)))
    x_in, normed, cot, dest_own, dest_halo = prep(
        place, own, other, halo, prom, row_of(attn_gain), row_of(attn_shift), slots
    )

    hidden = up_weight.shape[1]
    span = hidden // 2
    shard = jnp.stack(
        [up_weight.swapaxes(0, 1).reshape(2, span, wide), down_weight.reshape(2, span, wide)],
        axis=1,
    )
    shard, got[0] = tie(shard, got[0])
    held = grid.gather_z(shard)
    bias = jnp.stack(grid.gather_z(up_bias.reshape(2, span)))
    bias = jnp.stack([bias, grid.by_x(bias)])
    bias = jnp.stack([bias, grid.by_y(bias)])
    mlp_a0, mlp_b0 = grid.spread(jnp.stack([h[0] for h in held]), jnp.stack([h[1] for h in held]))
    mlp_a1, mlp_b1 = grid.spread_more(mlp_a0, mlp_b0)
    bias_a = jnp.stack([bias[0, 0, :, 0], bias[1, 0, :, 0], bias[0, 0, :, 1], bias[0, 1, :, 1]])
    bias_b = jnp.stack([bias[0, 1, :, 0], bias[1, 1, :, 0], bias[1, 0, :, 1], bias[1, 1, :, 1]])

    blocks = jnp.stack(
        [
            jnp.concatenate(
                [(a_zero, a_one)[dx][dy], (b_zero, b_one)[dy][dx]], axis=1
            )
            for dy in range(2)
            for dx in range(2)
        ]
    ).reshape(2, 2, deep, depth, 4 * third)
    blocks = grid.to_absolute(blocks, 2, 1).swapaxes(1, 2)
    weight = blocks.reshape(2, 2 * deep * depth, 4 * third)
    qkv, prob, att, part = attend(normed, weight, slots)
    middle, normed_two = mid(
        x_in, part, grid.by_core(part), row_of(mlp_gain), row_of(mlp_shift), slots
    )

    fine = span % 16 == 0

    def enter(value):
        if fine:
            return value
        return value.swapaxes(1, 2).reshape(2, 1, 2, deep * span, wide)

    def leave(value):
        if fine:
            return value
        return value.reshape(2, 2, deep, span, wide).swapaxes(1, 2)

    o_sum, g_sum, grad_a0, grad_b0, grad_bias_a = mlp(
        enter(mlp_a0), enter(mlp_b0), normed_two, cot, row_of(bias_a), slots
    )
    o_part, g_part, grad_a1, grad_b1, grad_bias_b = mlp(
        enter(mlp_a1), enter(mlp_b1), normed_two, cot, row_of(bias_b), slots, (o_sum, g_sum)
    )
    g_other = grid.by_core(g_part)
    grad_a, grad_b = grid.fold(leave(grad_a0), leave(grad_b0), leave(grad_a1), leave(grad_b1))
    grad_shard = grid.scatter_z([jnp.stack([grad_a[k], grad_b[k]]) for k in range(deep)])
    grad_up = grad_shard[:, 0].reshape(hidden, wide).swapaxes(0, 1)
    grad_down = grad_shard[:, 1].reshape(hidden, wide)
    o_other = grid.by_core(o_part)
    out_own, out_halo = finish(middle, o_part, o_other, dest_own, dest_halo, slots)
    out_edge = grid.by_y(out_halo)

    grad_middle, grad_proj, grad_qkv, g_one, sums_two = back(
        middle, g_part, g_other, cot, row_of(mlp_gain), weight, qkv, prob, slots
    )
    g_one_other = grid.by_core(g_one)
    grad_weight = weight_grads(normed, grad_proj, grad_qkv, att)
    blocks = grad_weight.reshape(2, deep, 2, depth, 4 * third).swapaxes(1, 2)
    blocks = grid.to_relative(blocks, 2, 1)
    blocks = blocks.reshape(2, 2, deep, 2, depth // 2, 4 * third)
    att_a, att_b = grid.fold(
        blocks[:, 0, :, 0], blocks[0, :, :, 1], blocks[:, 1, :, 0], blocks[1, :, :, 1]
    )
    att_shard = grid.scatter_z([jnp.stack([att_a[k], att_b[k]]) for k in range(deep)])
    att_shard = att_shard.reshape(depth, 4 * third)
    grad_qkv_weight = att_shard[:, : 3 * third].reshape(depth, 3, third)
    grad_out_weight = att_shard[:, 3 * third :].swapaxes(0, 1)

    tok_own, tok_halo, prompt_sum, sums_one = last(
        x_in, grad_middle, g_one, g_one_other, row_of(attn_gain), dest_own, dest_halo, slots
    )
    tok_edge = grid.by_y(tok_halo)

    def merge(value, edge):
        edge = edge.astype(value.dtype)
        ends = jnp.where((grid.y == 0) & (grid.c == 1), edge, 0)
        begins = jnp.where((grid.y == 1) & (grid.c == 0), edge, 0)
        value = value.at[count - HALO :].add(ends)
        return value.at[:HALO].add(begins)

    g_a = grad_bias_a.reshape(4, deep, span)
    g_b = grad_bias_b.reshape(4, deep, span)
    bias_blocks = jnp.stack(
        [
            jnp.stack([jnp.stack([g_a[0], g_a[2]], 1), jnp.stack([g_b[0], g_a[3]], 1)]),
            jnp.stack([jnp.stack([g_a[1], g_b[2]], 1), jnp.stack([g_b[1], g_b[3]], 1)]),
        ]
    )
    bias_blocks = grid.to_absolute(bias_blocks, 2, 1)
    bias_blocks = jnp.where(grid.y == 0, bias_blocks, jnp.flip(bias_blocks, axis=0))
    small = jnp.concatenate(
        [prompt_sum, sums_one[:2], sums_two[:2], bias_blocks.reshape(-1, wide)]
    )
    small = small + grid.by_x(small)
    small = small + grid.by_y(small)
    stride = 1
    while stride < deep:
        small = small + grid.send(
            small, lambda z, x, y, c, stride=stride: (z ^ stride, x, y, c)
        )
        stride *= 2
    bias_all = small[60:].reshape(2, 2, deep, hidden)
    grad_bias = lax.dynamic_slice(
        bias_all, (grid.y, grid.x, grid.z, jnp.int32(0)), (1, 1, 1, hidden)
    ).reshape(hidden)
    return (
        merge(out_own, out_edge),
        merge(tok_own, tok_edge),
        small[1 : 1 + PROMPTS],
        small[56],
        small[57],
        grad_qkv_weight,
        grad_out_weight,
        small[58],
        small[59],
        grad_up,
        grad_bias,
        grad_down,
    )


def solution(mesh):
    both = P(AXES)
    lead = P(AXES, None)
    return jax.shard_map(
        functools.partial(local, mesh.shape["rows"], mesh.shape["heads"]),
        mesh=mesh,
        in_specs=(
            lead,
            both,
            both,
            both,
            P(),
            P(),
            P(),
            P("rows", None, "heads"),
            P("heads", "rows"),
            P(),
            P(),
            P(None, AXES),
            both,
            lead,
            lead,
        ),
        out_specs=(
            lead,
            lead,
            P(),
            P(),
            P(),
            P("rows", None, "heads"),
            P("heads", "rows"),
            P(),
            P(),
            P(None, AXES),
            both,
            lead,
        ),
        check_vma=False,
    )
```

time: 1030 us -> 344 us (0.33); the launches traced: 1020 us -> 343 us
  waiting for transfers between devices: 468 us -> 111 us
  matrix products: 237 us -> 0 us
  blocking collectives: 163 us -> 0 us
  Pallas kernels: 0 us -> 112 us
  other arithmetic: 85.2 us -> 31.5 us
  starting transfers between devices: 0.97 us -> 47.4 us
  loops' own time: 23.3 us -> 0 us
  local copies, waits for them, and re-layouts: 23.3 us -> 39 us
  between operations: 16.9 us -> 1.38 us
    reduce_scatter x5 -> x0, waiting for transfers between devices: 333 us -> none  [the longest x1 142 us: local(): lax.psum_scatter(grad_down, ('rows', 'heads'), scatter_dimension=0, tiled...]
    dot_general x41 -> x0, matrix products: 233 us -> none  [the longest x8 39 us: block_scores(): jnp.einsum('qhe,khe->hqk', queries, keys_row, preferred_element_type=jnp....]
    pallas_call x0 -> x9, Pallas kernels: none -> 112 us  [the longest x2 36.5 us: mlp(): pl.pallas_call(functools.partial(mlp_kernel, more), grid=(slots,), in_spe...]
    ppermute x0 -> x45, waiting for transfers between devices: none -> 111 us  [send(): return lax.ppermute(value, AXES, pairs)]
    all_gather x4 -> x0, waiting for transfers between devices: 101 us -> none  [the longest x1 45 us: local(): lax.all_gather(down_weight, ('rows', 'heads'), axis=0, tiled=True)]
    all_gather x4 -> x0, blocking collectives: 83.9 us -> none  [the longest x1 40.5 us: local(): lax.all_gather(qkv_weight, 'rows', axis=0, tiled=True)]
    ppermute x0 -> x45, starting transfers between devices: none -> 47.4 us  [send(): return lax.ppermute(value, AXES, pairs)]
    psum x1 -> x0, blocking collectives: 40.9 us -> none  [local(): lax.psum((grad_prompts, attn_gain_grad, attn_shift_grad, mlp_gain_grad, m...]
  transfers between devices with their start and end apart: 11 -> 45, of which waited for: 8 -> 19; matrix products, arithmetic and copies ran while one was open for 7% -> 18% of each run, Pallas kernels for 0% -> 27%
where the time goes in v1:
time: 344 us; the launch traced here: 343 us
  Pallas kernels  112 us (33%)
  waiting for transfers between devices  111 us (32%)
  starting transfers between devices  47.4 us (14%)
  local copies, waits for them, and re-layouts  39 us (11%)
  other arithmetic  31.5 us (9%)
    ppermute x45, waiting for transfers between devices, send(): return lax.ppermute(value, AXES, pairs)  111 us
    ppermute x45, starting transfers between devices, send(): return lax.ppermute(value, AXES, pairs)  47.4 us
    pallas_call x2, Pallas kernels, mlp(): pl.pallas_call(functools.partial(mlp_kernel, more), grid=(slots,), in_spe...  36.5 us
    pallas_call x1, Pallas kernels, back(): pl.pallas_call(back_kernel, grid=(slots,), in_specs=[tile, tile, tile, ti...  21.4 us
    pallas_call x1, Pallas kernels, attend(): pl.pallas_call(attend_kernel, grid=(slots,), in_specs=[pl.BlockSpec((SLOT...  15.2 us
    pallas_call x1, Pallas kernels, weight_grads(): pl.pallas_call(weight_kernel, grid=(wide // cut, groups), in_specs=[tall,...  10.6 us
    pallas_call x1, Pallas kernels, prep(): pl.pallas_call(prep_kernel, grid=(slots,), in_specs=[SMEM] + [whole(v.sha...  9.11 us
    unnamed x48, local copies, waits for them, and re-layouts  9.07 us
  transfers between devices with their start and end apart: 45, of which 19 were waited for; matrix products, arithmetic and copies ran while one was open for 18% of the time, Pallas kernels for 27%

profile of v1, /device:TPU:0, one launch (start us, length us, event | category | flops | bytes accessed | tf_op | source)
XLA Modules:
  0.0 342.8 jit_solution(12759419579324140662)
XLA Ops:
  1.6 5.0 %collective-permute-start.19 = (bf16[2,48]{1,0:T(2,128)(2,1)S(1)}, bf16[2,48]{1,0:T(2,128)(2,1)S(1)}, u32[]{:S(2)}, u32[]{:S(2)}) collective-permute-start(bf16[2,48]{1,0:T(2,128)(2,1)S(1)} %reshape.282), channel_id=1, source_target_pairs={{0,24},{1,25},{2,26},{3,27},{4,28},{5,29},{6,30},{7,31},{8,0},{9,1... | collective-permute-start | bytes 584 | tf_op jit(solution)/shard_map/ppermute | solution.py:553
  32.7 3.4 collective-permute-start.12
  39.1 4.9 %collective-permute-done.6 = bf16[4,48,768]{2,1,0:T(8,128)(2,1)S(1)} collective-permute-done((bf16[4,48,768]{2,1,0:T(8,128)(2,1)S(1)}, bf16[4,48,768]{2,1,0:T(8,128)(2,1)S(1)}, u32[]{:S(2)}, u32[]{:S(2)}) %collective-permute-start.6) | collective-permute-done | bytes 294944 | tf_op jit(solution)/shard_map/ppermute | solution.py:553
  47.2 15.5 %collective-permute-done.11 = bf16[2,2,48,768]{3,2,1,0:T(8,128)(2,1)S(1)} collective-permute-done((bf16[2,2,48,768]{3,2,1,0:T(8,128)(2,1)S(1)}, bf16[2,2,48,768]{3,2,1,0:T(8,128)(2,1)S(1)}, u32[]{:S(2)}, u32[]{:S(2)}) %collective-permute-start.11) | collective-permute-done | bytes 294944 | tf_op jit(solution)/shard_map/ppermute | solution.py:553
  65.9 12.1 %collective-permute-done.8 = bf16[2,4,48,768]{3,2,1,0:T(8,128)(2,1)S(1)} collective-permute-done((bf16[2,4,48,768]{3,2,1,0:T(8,128)(2,1)S(1)}, bf16[2,4,48,768]{3,2,1,0:T(8,128)(2,1)S(1)}, u32[]{:S(2)}, u32[]{:S(2)}) %collective-permute-start.8) | collective-permute-done | bytes 589856 | tf_op jit(solution)/shard_map/ppermute | solution.py:553
  88.1 3.2 collective-permute-done.1.halo
  92.0 9.1 %prep.1 = (bf16[1088,768]{1,0:T(8,128)(2,1)}, bf16[1088,768]{1,0:T(8,128)(2,1)}, bf16[1088,768]{1,0:T(8,128)(2,1)}, s32[1,512]{1,0:T(1,128)}, s32[1,48]{1,0:T(1,128)}) custom-call(s32[4]{0:T(128)} %pad_add_fusion.place, bf16[1040,768]{1,0:T(8,128)(2,1)} %pad_maximum_fusion.1.own, bf16[1040,768]{1,0:T(8,128)(2,1)} %collective-permute-done.other, ...), custom_call_target="tpu_custom_call" | custom-call | flops 3582984192 | bytes 10027008 | tf_op jit(solution)/shard_map/prep/pallas_call | solution.py:144
  101.1 15.2 %attend.1 = (bf16[2,1088,576]{2,1,0:T(8,128)(2,1)}, bf16[4,2,3,256,256]{4,3,2,1,0:T(8,128)(2,1)}, bf16[2,1088,192]{2,1,0:T(8,128)(2,1)}, bf16[1088,768]{1,0:T(8,128)(2,1)}) custom-call(bf16[1088,768]{1,0:T(8,128)(2,1)} %get-tuple-element.112.normed, bf16[2,768,768]{2,1,0:T(8,128)(2,1)} %bitcast.171), custom_call_target="tpu_custom_call" | custom-call | flops 4107062528 | bytes 10027008 | tf_op jit(solution)/shard_map/attend/pallas_call | solution.py:192
  118.3 14.0 %collective-permute-done.13 = bf16[4,2,48,768]{3,2,1,0:T(8,128)(2,1)S(1)} collective-permute-done((bf16[4,2,48,768]{3,2,1,0:T(8,128)(2,1)S(1)}, bf16[4,2,48,768]{3,2,1,0:T(8,128)(2,1)S(1)}, u32[]{:S(2)}, u32[]{:S(2)}) %collective-permute-start.13) | collective-permute-done | bytes 589856 | tf_op jit(solution)/shard_map/ppermute | solution.py:553
  139.3 5.2 %mid.1 = (f32[1088,768]{1,0:T(8,128)}, bf16[1088,768]{1,0:T(8,128)(2,1)}) custom-call(bf16[1088,768]{1,0:T(8,128)(2,1)} %get-tuple-element.111.x_in, bf16[1088,768]{1,0:T(8,128)(2,1)} %get-tuple-element.119.one, bf16[1088,768]{1,0:T(8,128)(2,1)} %copy-done.3, f32[1,768]{1,0:T(1,128)} %reshape.295.gain, f32[1,768]{1,0:T(1,128)} %reshape.297.shift), custom_call_target="tpu_custom_call" | custom-call | flops 16711680 | bytes 10027008 | tf_op jit(solution)/shard_map/mid/pallas_call | solution.py:224
  144.5 17.8 %mlp.2 = (f32[1088,768]{1,0:T(8,128)}, f32[1088,768]{1,0:T(8,128)}, bf16[2,4,2,48,768]{4,3,2,1,0:T(8,128)(2,1)}, bf16[2,4,2,48,768]{4,3,2,1,0:T(8,128)(2,1)}, f32[1,768]{1,0:T(1,128)}) custom-call(bf16[2,4,2,48,768]{4,3,2,1,0:T(8,128)(2,1)} %pad_maximum_fusion.2.refs_0_, bf16[2,4,2,48,768]{4,3,2,1,0:T(8,128)(2,1)} %copy-done.6, ...), custom_call_target="tpu_custom_call" | custom-call | flops 7700742144 | bytes 11698176 | tf_op jit(solution)/shard_map/mlp/pallas_call | solution.py:317
  162.8 18.7 %mlp.3 = (bf16[1088,768]{1,0:T(8,128)(2,1)}, bf16[1088,768]{1,0:T(8,128)(2,1)}, bf16[2,4,2,48,768]{4,3,2,1,0:T(8,128)(2,1)}, bf16[2,4,2,48,768]{4,3,2,1,0:T(8,128)(2,1)}, f32[1,768]{1,0:T(1,128)}) custom-call(bf16[2,4,2,48,768]{4,3,2,1,0:T(8,128)(2,1)} %collective-permute-done.15.refs_0_, bf16[2,4,2,48,768]{4,3,2,1,0:T(8,128)(2,1)} %collective-permute-done.16.refs_1_, ...), custom_call_target="tpu_custom_call" | custom-call | flops 7700742144 | bytes 11698176 | tf_op jit(solution)/shard_map/mlp/pallas_call | solution.py:317
  187.6 22.1 %collective-permute-done.38 = bf16[2,4,2,48,768]{4,3,2,1,0:T(8,128)(2,1)} collective-permute-done((bf16[2,4,2,48,768]{4,3,2,1,0:T(8,128)(2,1)}, bf16[2,4,2,48,768]{4,3,2,1,0:T(8,128)(2,1)}, u32[]{:S(2)}, u32[]{:S(2)}) %collective-permute-start.38) | collective-permute-done | bytes 1179680 | tf_op jit(solution)/shard_map/ppermute | solution.py:553
  218.4 6.0 %finish.1 = (bf16[512,768]{1,0:T(8,128)(2,1)}, bf16[48,768]{1,0:T(8,128)(2,1)}) custom-call(f32[1088,768]{1,0:T(8,128)} %get-tuple-element.120.middle, bf16[1088,768]{1,0:T(8,128)(2,1)} %get-tuple-element.128.one, bf16[1088,768]{1,0:T(8,128)(2,1)} %copy-done, s32[1,512]{1,0:T(1,128)} %get-tuple-element.129.dest_own, s32[1,48]{1,0:T(1,128)} %get-tuple-element.130.dest_halo), custom_call_target="tpu_custom_call" | custom-call | flops 935854080 | bytes 8355840 | tf_op jit(solution)/shard_map/finish/pallas_call | solution.py:366
  224.9 21.4 %back.1 = (f32[1088,768]{1,0:T(8,128)}, bf16[1088,768]{1,0:T(8,128)(2,1)}, bf16[2,1088,576]{2,1,0:T(8,128)(2,1)}, bf16[1088,768]{1,0:T(8,128)(2,1)}, f32[8,768]{1,0:T(8,128)}) custom-call(f32[1088,768]{1,0:T(8,128)} %get-tuple-element.120.middle, bf16[1088,768]{1,0:T(8,128)(2,1)} %get-tuple-element.133.one, bf16[1088,768]{1,0:T(8,128)(2,1)} %collective-permute-done.24.two, ...), custom_call_target="tpu_custom_call" | custom-call | flops 5133828096 | bytes 20054016 | tf_op jit(solution)/shard_map/back/pallas_call | solution.py:435
  246.3 10.6 %weight_grads.1 = bf16[2,768,768]{2,1,0:T(8,128)(2,1)} custom-call(bf16[1088,768]{1,0:T(8,128)(2,1)} %get-tuple-element.112.normed, bf16[1088,768]{1,0:T(8,128)(2,1)} %get-tuple-element.145.grad_proj, bf16[2,1088,576]{2,1,0:T(8,128)(2,1)} %get-tuple-element.146.grad_qkv, bf16[2,1088,192]{2,1,0:T(8,128)(2,1)} %get-tuple-element.147.att), custom_call_target="tpu_custom_call" | custom-call | flops 2566914048 | bytes 16711680 | tf_op jit(solution)/shard_map/weight_grads/pallas_call | solution.py:473
  278.7 4.6 %collective-permute-done.42 = bf16[2,2,48,768]{3,2,1,0:T(8,128)(2,1)S(1)} collective-permute-done((bf16[2,2,48,768]{3,2,1,0:T(8,128)(2,1)S(1)}, bf16[2,2,48,768]{3,2,1,0:T(8,128)(2,1)S(1)}, u32[]{:S(2)}, u32[]{:S(2)}) %collective-permute-start.42) | collective-permute-done | bytes 294944 | tf_op jit(solution)/shard_map/ppermute | solution.py:553
  283.9 10.2 %collective-permute-done.43 = bf16[2,2,48,768]{3,2,1,0:T(8,128)(2,1)S(1)} collective-permute-done((bf16[2,2,48,768]{3,2,1,0:T(8,128)(2,1)S(1)}, bf16[2,2,48,768]{3,2,1,0:T(8,128)(2,1)S(1)}, u32[]{:S(2)}, u32[]{:S(2)}) %collective-permute-start.43) | collective-permute-done | bytes 294944 | tf_op jit(solution)/shard_map/ppermute | solution.py:553
  295.4 5.0 %collective-permute-start.36 = (bf16[2,48,768]{2,1,0:T(8,128)(2,1)S(1)}, bf16[2,48,768]{2,1,0:T(8,128)(2,1)S(1)}, u32[]{:S(2)}, u32[]{:S(2)}) collective-permute-start(bf16[2,48,768]{2,1,0:T(8,128)(2,1)S(1)} %pad_maximum_fusion.17), channel_id=1, source_target_pairs={{0,16},{1,17},{2,18},{3,19},{4,20},{5,21},{6,22},{7,23},{8,24},{9,... | collective-permute-start | bytes 442376 | tf_op jit(solution)/shard_map/ppermute | solution.py:553
  303.7 8.1 %last.1 = (f32[512,768]{1,0:T(8,128)}, bf16[48,768]{1,0:T(8,128)(2,1)}, f32[56,768]{1,0:T(8,128)}, f32[8,768]{1,0:T(8,128)}) custom-call(bf16[1088,768]{1,0:T(8,128)(2,1)} %get-tuple-element.111.x_in, f32[1088,768]{1,0:T(8,128)} %get-tuple-element.136.gm, bf16[1088,768]{1,0:T(8,128)(2,1)} %get-tuple-element.137.one, bf16[1088,768]{1,0:T(8,128)(2,1)} %copy-done.2, ...), custom_call_target="tpu_custom_call" | custom-call | flops 935854080 | bytes 8355840 | tf_op jit(solution)/shard_map/last/pallas_call | solution.py:519
  315.1 4.4 %collective-permute-done.27 = f32[62,768]{1,0:T(8,128)S(1)} collective-permute-done((f32[62,768]{1,0:T(8,128)S(1)}, f32[62,768]{1,0:T(8,128)S(1)}, u32[]{:S(2)}, u32[]{:S(2)}) %collective-permute-start.27) | collective-permute-done | bytes 190496 | tf_op jit(solution)/shard_map/ppermute | solution.py:553
  323.0 3.2 collective-permute-done.28
  328.2 4.3 %collective-permute-done.29 = f32[62,768]{1,0:T(8,128)S(1)} collective-permute-done((f32[62,768]{1,0:T(8,128)S(1)}, f32[62,768]{1,0:T(8,128)S(1)}, u32[]{:S(2)}, u32[]{:S(2)}) %collective-permute-start.29) | collective-permute-done | bytes 190496 | tf_op jit(solution)/shard_map/ppermute | solution.py:553
  334.8 6.1 %collective-permute-done.30 = f32[62,768]{1,0:T(8,128)S(1)} collective-permute-done((f32[62,768]{1,0:T(8,128)S(1)}, f32[62,768]{1,0:T(8,128)S(1)}, u32[]{:S(2)}, u32[]{:S(2)}) %collective-permute-start.30) | collective-permute-done | bytes 190496 | tf_op jit(solution)/shard_map/ppermute | solution.py:553
  (246 shorter events, 111.5 us)
Async XLA Ops:
  1.6 24.2 %collective-permute-start.19 = (bf16[2,48]{1,0:T(2,128)(2,1)S(1)}, bf16[2,48]{1,0:T(2,128)(2,1)S(1)}, u32[]{:S(2)}, u32[]{:S(2)}) collective-permute-start(bf16[2,48]{1,0:T(2,128)(2,1)S(1)} %reshape.282), channel_id=1, source_target_pairs={{0,24},{1,25},{2,26},{3,27},{4,28},{5,29},{6,30},{7,31},{8,0},{9,1... | collective-permute-start | bytes 584 | tf_op jit(solution)/shard_map/ppermute | solution.py:553
  6.6 19.2 %collective-permute-start.18 = (bf16[2,48]{1,0:T(2,128)(2,1)S(1)}, bf16[2,48]{1,0:T(2,128)(2,1)S(1)}, u32[]{:S(2)}, u32[]{:S(2)}) collective-permute-start(bf16[2,48]{1,0:T(2,128)(2,1)S(1)} %reshape.282), channel_id=1, source_target_pairs={{0,16},{1,17},{2,18},{3,19},{4,20},{5,21},{6,22},{7,23},{8,24},{9,... | collective-permute-start | bytes 584 | tf_op jit(solution)/shard_map/ppermute | solution.py:553
  6.6 19.3 %collective-permute-start.17 = (bf16[2,48]{1,0:T(2,128)(2,1)S(1)}, bf16[2,48]{1,0:T(2,128)(2,1)S(1)}, u32[]{:S(2)}, u32[]{:S(2)}) collective-permute-start(bf16[2,48]{1,0:T(2,128)(2,1)S(1)} %reshape.282), channel_id=1, source_target_pairs={{0,8},{1,9},{2,10},{3,11},{4,12},{5,13},{6,14},{7,15},{8,16},{9,17... | collective-permute-start | bytes 584 | tf_op jit(solution)/shard_map/ppermute | solution.py:553
  9.8 22.5 %collective-permute-start.4 = (bf16[2,48,768]{2,1,0:T(8,128)(2,1)S(1)}, bf16[2,48,768]{2,1,0:T(8,128)(2,1)S(1)}, u32[]{:S(2)}, u32[]{:S(2)}) collective-permute-start(bf16[2,48,768]{2,1,0:T(8,128)(2,1)S(1)} %pad_maximum_fusion.15), channel_id=1, source_target_pairs={{0,24},{1,25},{2,26},{3,27},{4,28},{5,29},{6,30},{7,31},{8,0},{9,1... | collective-permute-start | bytes 442376 | tf_op jit(solution)/shard_map/ppermute | solution.py:553
  12.7 19.6 %collective-permute-start.3 = (bf16[2,48,768]{2,1,0:T(8,128)(2,1)S(1)}, bf16[2,48,768]{2,1,0:T(8,128)(2,1)S(1)}, u32[]{:S(2)}, u32[]{:S(2)}) collective-permute-start(bf16[2,48,768]{2,1,0:T(8,128)(2,1)S(1)} %pad_maximum_fusion.15), channel_id=1, source_target_pairs={{0,16},{1,17},{2,18},{3,19},{4,20},{5,21},{6,22},{7,23},{8,24},{9,... | collective-permute-start | bytes 442376 | tf_op jit(solution)/shard_map/ppermute | solution.py:553
  25.8 57.4 %collective-permute-start = (bf16[1040,768]{1,0:T(8,128)(2,1)}, bf16[1040,768]{1,0:T(8,128)(2,1)}, u32[]{:S(2)}, u32[]{:S(2)}) collective-permute-start(bf16[1040,768]{1,0:T(8,128)(2,1)} %pad_maximum_fusion.1.own), channel_id=1, source_target_pairs={{0,1},{1,0},{2,3},{3,2},{4,5},{5,4},{6,7},{7,6},{8,9},{9,8},{10,11... | collective-permute-start | bytes 4792328 | tf_op jit(solution)/shard_map/ppermute | solution.py:553
  30.2 88.1 %collective-permute-start.21 = (bf16[2,4,2,48]{3,2,1,0:T(2,128)(2,1)}, bf16[2,4,2,48]{3,2,1,0:T(2,128)(2,1)S(1)}, u32[]{:S(2)}, u32[]{:S(2)}) collective-permute-start(bf16[2,4,2,48]{3,2,1,0:T(2,128)(2,1)} %pad_maximum_fusion.20), channel_id=1, source_target_pairs={{0,2},{1,3},{2,0},{3,1},{4,6},{5,7},{6,4},{7,5},{8,10},{9,11},{10,... | collective-permute-start | bytes 4616 | tf_op jit(solution)/shard_map/ppermute | solution.py:553
  45.4 20.4 %collective-permute-start.7 = (bf16[2,4,48,768]{3,2,1,0:T(8,128)(2,1)S(1)}, bf16[2,4,48,768]{3,2,1,0:T(8,128)(2,1)S(1)}, u32[]{:S(2)}, u32[]{:S(2)}) collective-permute-start(bf16[2,4,48,768]{3,2,1,0:T(8,128)(2,1)S(1)} %pad_maximum_fusion.4), channel_id=1, source_target_pairs={{0,4},{1,5},{2,6},{3,7},{4,0},{5,1},{6,2},{7,3},{8,12},{9,13},{10,... | collective-permute-start | bytes 1769480 | tf_op jit(solution)/shard_map/ppermute | solution.py:553
  64.2 54.1 %collective-permute-start.14 = (bf16[4,2,48,768]{3,2,1,0:T(8,128)(2,1)S(1)}, bf16[4,2,48,768]{3,2,1,0:T(8,128)(2,1)}, u32[]{:S(2)}, u32[]{:S(2)}) collective-permute-start(bf16[4,2,48,768]{3,2,1,0:T(8,128)(2,1)S(1)} %get-tuple-element.249), channel_id=1, source_target_pairs={{0,4},{1,5},{2,6},{3,7},{4,0},{5,1},{6,2},{7,3},{8,12},{9,13},{10,... | collective-permute-start | bytes 1769480 | tf_op jit(solution)/shard_map/ppermute | solution.py:553
  116.3 21.8 %collective-permute-start.9 = (bf16[1088,768]{1,0:T(8,128)(2,1)}, bf16[1088,768]{1,0:T(8,128)(2,1)S(1)}, u32[]{:S(2)}, u32[]{:S(2)}) collective-permute-start(bf16[1088,768]{1,0:T(8,128)(2,1)} %get-tuple-element.119.one), channel_id=1, source_target_pairs={{0,1},{1,0},{2,3},{3,2},{4,5},{5,4},{6,7},{7,6},{8,9},{9,8},{10,11... | collective-permute-start | bytes 5013512 | tf_op jit(solution)/shard_map/ppermute | solution.py:553
  133.5 28.8 %collective-permute-start.16 = (bf16[2,4,2,48,768]{4,3,2,1,0:T(8,128)(2,1)S(1)}, bf16[2,4,2,48,768]{4,3,2,1,0:T(8,128)(2,1)}, u32[]{:S(2)}, u32[]{:S(2)}) collective-permute-start(bf16[2,4,2,48,768]{4,3,2,1,0:T(8,128)(2,1)S(1)} %pad_maximum_fusion.3.refs_1_), channel_id=1, source_target_pairs={{0,2},{1,3},{2,0},{3,1},{4,6},{5,7},{6,4},{7,5},{8,10},{9,11},{10,... | collective-permute-start | bytes 3538952 | tf_op jit(solution)/shard_map/ppermute | solution.py:553
  135.2 27.6 %collective-permute-start.15 = (bf16[2,4,2,48,768]{4,3,2,1,0:T(8,128)(2,1)}, bf16[2,4,2,48,768]{4,3,2,1,0:T(8,128)(2,1)}, u32[]{:S(2)}, u32[]{:S(2)}) collective-permute-start(bf16[2,4,2,48,768]{4,3,2,1,0:T(8,128)(2,1)} %pad_maximum_fusion.2.refs_0_), channel_id=1, source_target_pairs={{0,4},{1,5},{2,6},{3,7},{4,0},{5,1},{6,2},{7,3},{8,12},{9,13},{10,... | collective-permute-start | bytes 3538952 | tf_op jit(solution)/shard_map/ppermute | solution.py:553
  182.9 26.8 %collective-permute-start.38 = (bf16[2,4,2,48,768]{4,3,2,1,0:T(8,128)(2,1)}, bf16[2,4,2,48,768]{4,3,2,1,0:T(8,128)(2,1)}, u32[]{:S(2)}, u32[]{:S(2)}) collective-permute-start(bf16[2,4,2,48,768]{4,3,2,1,0:T(8,128)(2,1)} %get-tuple-element.153), channel_id=1, source_target_pairs={{0,4},{1,5},{2,6},{3,7},{4,0},{5,1},{6,2},{7,3},{8,12},{9,13},{10,... | collective-permute-start | bytes 3538952 | tf_op jit(solution)/shard_map/ppermute | solution.py:553
  184.4 26.4 %collective-permute-start.39 = (bf16[2,4,2,48,768]{4,3,2,1,0:T(8,128)(2,1)}, bf16[2,4,2,48,768]{4,3,2,1,0:T(8,128)(2,1)}, u32[]{:S(2)}, u32[]{:S(2)}) collective-permute-start(bf16[2,4,2,48,768]{4,3,2,1,0:T(8,128)(2,1)} %get-tuple-element.154), channel_id=1, source_target_pairs={{0,2},{1,3},{2,0},{3,1},{4,6},{5,7},{6,4},{7,5},{8,10},{9,11},{10,... | collective-permute-start | bytes 3538952 | tf_op jit(solution)/shard_map/ppermute | solution.py:553
  185.8 31.3 %collective-permute-start.22 = (bf16[1088,768]{1,0:T(8,128)(2,1)}, bf16[1088,768]{1,0:T(8,128)(2,1)S(1)}, u32[]{:S(2)}, u32[]{:S(2)}) collective-permute-start(bf16[1088,768]{1,0:T(8,128)(2,1)} %get-tuple-element.128.one), channel_id=1, source_target_pairs={{0,1},{1,0},{2,3},{3,2},{4,5},{5,4},{6,7},{7,6},{8,9},{9,8},{10,11... | collective-permute-start | bytes 5013512 | tf_op jit(solution)/shard_map/ppermute | solution.py:553
  185.8 39.1 %collective-permute-start.24 = (bf16[1088,768]{1,0:T(8,128)(2,1)}, bf16[1088,768]{1,0:T(8,128)(2,1)}, u32[]{:S(2)}, u32[]{:S(2)}) collective-permute-start(bf16[1088,768]{1,0:T(8,128)(2,1)} %get-tuple-element.133.one), channel_id=1, source_target_pairs={{0,1},{1,0},{2,3},{3,2},{4,5},{5,4},{6,7},{7,6},{8,9},{9,8},{10,11... | collective-permute-start | bytes 5013512 | tf_op jit(solution)/shard_map/ppermute | solution.py:553
  212.9 56.3 %collective-permute-start.41 = (bf16[4,2,48,768]{3,2,1,0:T(8,128)(2,1)}, bf16[4,2,48,768]{3,2,1,0:T(8,128)(2,1)}, u32[]{:S(2)}, u32[]{:S(2)}) collective-permute-start(bf16[4,2,48,768]{3,2,1,0:T(8,128)(2,1)} %fusion.6), channel_id=1, source_target_pairs={{0,4},{1,5},{2,6},{3,7},{4,0},{5,1},{6,2},{7,3},{8,12},{9,13},{10,... | collective-permute-start | bytes 1769480 | tf_op jit(solution)/shard_map/ppermute | solution.py:553
  215.7 53.5 %collective-permute-start.40 = (bf16[4,2,48,768]{3,2,1,0:T(8,128)(2,1)}, bf16[4,2,48,768]{3,2,1,0:T(8,128)(2,1)}, u32[]{:S(2)}, u32[]{:S(2)}) collective-permute-start(bf16[4,2,48,768]{3,2,1,0:T(8,128)(2,1)} %fusion.5), channel_id=1, source_target_pairs={{0,2},{1,3},{2,0},{3,1},{4,6},{5,7},{6,4},{7,5},{8,10},{9,11},{10,... | collective-permute-start | bytes 1769480 | tf_op jit(solution)/shard_map/ppermute | solution.py:553
  224.3 43.3 %collective-permute-start.23 = (bf16[48,768]{1,0:T(8,128)(2,1)}, bf16[48,768]{1,0:T(8,128)(2,1)}, u32[]{:S(2)}, u32[]{:S(2)}) collective-permute-start(bf16[48,768]{1,0:T(8,128)(2,1)} %get-tuple-element.132), channel_id=1, source_target_pairs={{0,2},{1,3},{2,0},{3,1},{4,6},{5,7},{6,4},{7,5},{8,10},{9,11},{10,... | collective-permute-start | bytes 221192 | tf_op jit(solution)/shard_map/ppermute | solution.py:553
  272.4 21.6 %collective-permute-start.43 = (bf16[2,2,48,768]{3,2,1,0:T(8,128)(2,1)S(1)}, bf16[2,2,48,768]{3,2,1,0:T(8,128)(2,1)S(1)}, u32[]{:S(2)}, u32[]{:S(2)}) collective-permute-start(bf16[2,2,48,768]{3,2,1,0:T(8,128)(2,1)S(1)} %pad_maximum_fusion.12), channel_id=1, source_target_pairs={{0,16},{1,17},{2,18},{3,19},{4,20},{5,21},{6,22},{7,23},{8,24},{9,... | collective-permute-start | bytes 884744 | tf_op jit(solution)/shard_map/ppermute | solution.py:553
  272.5 21.5 %collective-permute-start.44 = (bf16[2,2,48,768]{3,2,1,0:T(8,128)(2,1)S(1)}, bf16[2,2,48,768]{3,2,1,0:T(8,128)(2,1)S(1)}, u32[]{:S(2)}, u32[]{:S(2)}) collective-permute-start(bf16[2,2,48,768]{3,2,1,0:T(8,128)(2,1)S(1)} %pad_maximum_fusion.13), channel_id=1, source_target_pairs={{0,8},{1,9},{2,10},{3,11},{4,12},{5,13},{6,14},{7,15},{8,16},{9,17... | collective-permute-start | bytes 884744 | tf_op jit(solution)/shard_map/ppermute | solution.py:553
  276.7 25.8 %collective-permute-start.25 = (bf16[1088,768]{1,0:T(8,128)(2,1)S(1)}, bf16[1088,768]{1,0:T(8,128)(2,1)S(1)}, u32[]{:S(2)}, u32[]{:S(2)}) collective-permute-start(bf16[1088,768]{1,0:T(8,128)(2,1)S(1)} %copy-done.1), channel_id=1, source_target_pairs={{0,1},{1,0},{2,3},{3,2},{4,5},{5,4},{6,7},{7,6},{8,9},{9,8},{10,11... | collective-permute-start | bytes 5013512 | tf_op jit(solution)/shard_map/ppermute | solution.py:553
  295.3 19.1 %collective-permute-start.35 = (bf16[2,48,768]{2,1,0:T(8,128)(2,1)S(1)}, bf16[2,48,768]{2,1,0:T(8,128)(2,1)S(1)}, u32[]{:S(2)}, u32[]{:S(2)}) collective-permute-start(bf16[2,48,768]{2,1,0:T(8,128)(2,1)S(1)} %pad_maximum_fusion.16), channel_id=1, source_target_pairs={{0,24},{1,25},{2,26},{3,27},{4,28},{5,29},{6,30},{7,31},{8,0},{9,1... | collective-permute-start | bytes 442376 | tf_op jit(solution)/shard_map/ppermute | solution.py:553
  295.4 19.0 %collective-permute-start.36 = (bf16[2,48,768]{2,1,0:T(8,128)(2,1)S(1)}, bf16[2,48,768]{2,1,0:T(8,128)(2,1)S(1)}, u32[]{:S(2)}, u32[]{:S(2)}) collective-permute-start(bf16[2,48,768]{2,1,0:T(8,128)(2,1)S(1)} %pad_maximum_fusion.17), channel_id=1, source_target_pairs={{0,16},{1,17},{2,18},{3,19},{4,20},{5,21},{6,22},{7,23},{8,24},{9,... | collective-permute-start | bytes 442376 | tf_op jit(solution)/shard_map/ppermute | solution.py:553
  (41 other events, 467.5 us)

commit v2 on v1

--- a/solution.py
+++ b/solution.py
@@ -38,8 +38,7 @@
     return pltpu.CompilerParams(vmem_limit_bytes=VMEM_LIMIT, **more)
 
 
-def cost(flops, moved, trans=0):
-    return pl.CostEstimate(flops=int(flops), bytes_accessed=int(moved), transcendentals=int(trans))
+COST = pl.CostEstimate(flops=1, bytes_accessed=1, transcendentals=0)
 
 
 SMEM = pl.BlockSpec(memory_space=pltpu.SMEM)
@@ -60,7 +59,7 @@
 
 
 def prep_kernel(
-    place, own, other, halo, prom, gain, shift, x_out, n_out, cot_out, dest_own, dest_halo, d_oth
+    place, own, other, halo, prom, norms, x_out, n_out, cot_out, dest_own, dest_halo, d_oth
 ):
     step = pl.program_id(0)
     count = d_oth.shape[1]
@@ -128,14 +127,17 @@
         tokens = one if tokens is None else tokens + one
         cots = two if cots is None else cots + two
     at = lax.broadcasted_iota(jnp.int32, (SLOT, 1), 0)
-    inputs = jnp.where((at >= 1) & (at <= PROMPTS), prom[...].astype(F32), tokens)
+    slot_row = lax.broadcasted_iota(jnp.int32, (SLOT, PROMPTS), 0)
+    which = lax.broadcasted_iota(jnp.int32, (SLOT, PROMPTS), 1)
+    prompted = dot((slot_row == which + 1).astype(BF16), prom[...])
+    inputs = jnp.where((at >= 1) & (at <= PROMPTS), prompted, tokens)
     hat, _ = stats(inputs)
     x_out[...] = inputs.astype(BF16)
-    n_out[...] = (hat * gain[...] + shift[...]).astype(BF16)
+    n_out[...] = (hat * norms[0:1] + norms[1:2]).astype(BF16)
     cot_out[...] = cots.astype(BF16)
 
 
-def prep(place, own, other, halo, prom, gain, shift, slots):
+def prep(place, own, other, halo, prom, norms, slots):
     count = own.shape[0] // 2 - 8
     wide = own.shape[1]
     rows = slots * SLOT
@@ -144,7 +146,7 @@
     return pl.pallas_call(
         prep_kernel,
         grid=(slots,),
-        in_specs=[SMEM] + [whole(v.shape) for v in (own, other, halo, prom, gain, shift)],
+        in_specs=[SMEM] + [whole(v.shape) for v in (own, other, halo, prom, norms)],
         out_specs=[tile, tile, tile, whole((1, count)), whole((1, HALO))],
         out_shape=[
             array,
@@ -155,12 +157,52 @@
         ],
         scratch_shapes=[pltpu.VMEM((1, count), jnp.int32)],
         compiler_params=params(),
-        cost_estimate=cost(4 * rows * (2 * count + HALO) * wide, 12 * rows * wide),
+        cost_estimate=COST,
         name="prep",
-    )(place, own, other, halo, prom, gain, shift)
-
-
-def attend_kernel(normed, weight, qkv_out, prob_out, att_out, part_out):
+    )(place, own, other, halo, prom, norms)
+
+
+def weight_pieces(place, refs):
+    if len(refs) == 1:
+        for group in range(2):
+            yield refs[0].at[group], group, 0, refs[0].shape[1]
+        return
+    a_zero, a_one, b_zero, b_one = refs
+    deep, half = a_zero.shape[1], a_zero.shape[2]
+    for dx in range(2):
+        col = place[1] if dx == 0 else 1 - place[1]
+        for dy in range(2):
+            for k in range(deep):
+                row = lax.rem(place[0] + deep - k, deep)
+                for part in range(2):
+                    ref = ((a_zero, a_one)[dx].at[dy, k], (b_zero, b_one)[dy].at[dx, k])[part]
+                    first = ((row * 2 + col) * 2 + part) * half
+                    yield ref, dy, pl.multiple_of(first, 16), half
+
+
+def piece_count(held):
+    return 2 if len(held) == 1 else 8 * held[0].shape[1]
+
+
+def load_weight(place, held, weight, sem):
+    copies = [
+        pltpu.make_async_copy(ref, weight.at[group, pl.ds(first, size)], sem.at[i])
+        for i, (ref, group, first, size) in enumerate(weight_pieces(place, held))
+    ]
+    for copy in copies:
+        copy.start()
+    for copy in copies:
+        copy.wait()
+
+
+def attend_kernel(held_count, place, normed, *refs):
+    held = refs[:held_count]
+    qkv_out, prob_out, att_out, part_out, weight, sem = refs[held_count:]
+
+    @pl.when(pl.program_id(0) == 0)
+    def _():
+        load_weight(place, held, weight, sem)
+
     third = weight.shape[2] // 4
     rows = lax.broadcasted_iota(jnp.int32, (CORE, CORE), 0)
     cols = lax.broadcasted_iota(jnp.int32, (CORE, CORE), 1)
@@ -184,15 +226,15 @@
     part_out[...] = total.astype(BF16)
 
 
-def attend(normed, weight, slots):
-    groups, deep, wide = weight.shape
+def attend(place, normed, held, slots):
+    rows, deep = normed.shape
+    groups, wide = 2, held[0].shape[-1]
     third = wide // 4
     heads = third // HEAD
-    rows = slots * SLOT
     return pl.pallas_call(
-        attend_kernel,
+        functools.partial(attend_kernel, len(held)),
         grid=(slots,),
-        in_specs=[pl.BlockSpec((SLOT, deep), lambda t: (t, 0)), whole(weight.shape)],
+        in_specs=[SMEM, pl.BlockSpec((SLOT, deep), lambda t: (t, 0))] + [ANY] * len(held),
         out_specs=[
             pl.BlockSpec((groups, SLOT, 3 * third), lambda t: (0, t, 0)),
             pl.BlockSpec((1, groups, heads, CORE, CORE), lambda t: (t, 0, 0, 0, 0)),
@@ -205,39 +247,21 @@
             jax.ShapeDtypeStruct((groups, rows, third), BF16),
             jax.ShapeDtypeStruct((rows, deep), BF16),
         ],
+        scratch_shapes=[
+            pltpu.VMEM((groups, deep, wide), BF16),
+            pltpu.SemaphoreType.DMA((piece_count(held),)),
+        ],
         compiler_params=params(),
-        cost_estimate=cost(2 * rows * deep * groups * wide * 1.6, 12 * rows * deep),
+        cost_estimate=COST,
         name="attend",
-    )(normed, weight)
-
-
-def mid_kernel(x_in, one, two, gain, shift, middle_out, n_out):
-    middle = x_in[...].astype(F32) + one[...].astype(F32) + two[...].astype(F32)
-    middle_out[...] = middle
-    hat, _ = stats(middle)
-    n_out[...] = (hat * gain[...] + shift[...]).astype(BF16)
-
-
-def mid(x_in, one, two, gain, shift, slots):
-    rows, wide = x_in.shape
-    tile = pl.BlockSpec((SLOT, wide), lambda t: (t, 0))
-    return pl.pallas_call(
-        mid_kernel,
-        grid=(slots,),
-        in_specs=[tile, tile, tile, whole(gain.shape), whole(shift.shape)],
-        out_specs=[tile, tile],
-        out_shape=[jax.ShapeDtypeStruct(x_in.shape, F32), jax.ShapeDtypeStruct(x_in.shape, BF16)],
-        compiler_params=params(),
-        cost_estimate=cost(20 * rows * wide, 12 * rows * wide),
-        name="mid",
-    )(x_in, one, two, gain, shift)
+    )(place, normed, *held)
 
 
 def mlp_kernel(more, *refs):
     if more:
         (a_in, b_in, normed, cot, bias, o_acc, g_acc, *refs) = refs
     else:
-        (a_in, b_in, normed, cot, bias, *refs) = refs
+        (a_in, b_in, x_in, one, two, norms, cot, bias, middle_out, normed, *refs) = refs
     (o_out, g_out, a_out, b_out, bias_out, weight, act, grad, result, in_sem, out_sem) = refs
     step = pl.program_id(0)
     lead, count, _, span, _ = a_in.shape
@@ -265,6 +289,11 @@
             copy.wait()
 
     rows = pl.ds(pl.multiple_of(step * SLOT, 16), SLOT)
+    if not more:
+        middle = x_in[...].astype(F32) + one[...].astype(F32) + two[...].astype(F32)
+        middle_out[...] = middle
+        hat, _ = stats(middle)
+        normed[rows] = (hat * norms[2:3] + norms[3:4]).astype(BF16)
     tile_n = normed[rows]
     tile_c = cot[rows]
     cut = 256
@@ -307,22 +336,31 @@
             copy.wait()
 
 
-def mlp(a_in, b_in, normed, cot, bias, slots, sums=None):
-    rows, wide = normed.shape
+def mlp(a_in, b_in, cot, bias, slots, start=None, sums=None):
+    rows, wide = cot.shape
     hidden = bias.shape[1]
     more = sums is not None
     tile = pl.BlockSpec((SLOT, wide), lambda t: (t, 0))
-    kept = BF16 if more else F32
+    wide_f32, wide_bf16 = (jax.ShapeDtypeStruct((rows, wide), kind) for kind in (F32, BF16))
+    kept = wide_bf16 if more else wide_f32
     count = 4 * a_in.shape[0] * a_in.shape[1]
+    full = whole(cot.shape)
+    if more:
+        operands = (a_in, b_in, start, cot, bias, *sums)
+        specs = [ANY, ANY, full, full, whole(bias.shape), tile, tile]
+    else:
+        x_in, one, two, norms = start
+        operands = (a_in, b_in, x_in, one, two, norms, cot, bias)
+        specs = [ANY, ANY, tile, tile, tile, whole(norms.shape), full, whole(bias.shape)]
     return pl.pallas_call(
         functools.partial(mlp_kernel, more),
         grid=(slots,),
-        in_specs=[ANY, ANY, whole(normed.shape), whole(cot.shape), whole(bias.shape)]
-        + ([tile, tile] if more else []),
-        out_specs=[tile, tile, ANY, ANY, whole(bias.shape)],
-        out_shape=[
-            jax.ShapeDtypeStruct((rows, wide), kept),
-            jax.ShapeDtypeStruct((rows, wide), kept),
+        in_specs=specs,
+        out_specs=([] if more else [tile, full]) + [tile, tile, ANY, ANY, whole(bias.shape)],
+        out_shape=([] if more else [wide_f32, wide_bf16])
+        + [
+            kept,
+            kept,
             jax.ShapeDtypeStruct(a_in.shape, BF16),
             jax.ShapeDtypeStruct(b_in.shape, BF16),
             jax.ShapeDtypeStruct(bias.shape, F32),
@@ -336,9 +374,53 @@
             pltpu.SemaphoreType.DMA((count,)),
         ],
         compiler_params=params(),
-        cost_estimate=cost(12 * rows * hidden * wide, 14 * rows * wide, 2 * rows * hidden),
+        cost_estimate=COST,
         name="mlp",
-    )(a_in, b_in, normed, cot, bias, *(sums or ()))
+    )(*operands)
+
+
+def add_kernel(a_zero, a_got, b_zero, b_got, a_out, b_out):
+    for zero, got, out in ((a_zero, a_got, a_out), (b_zero, b_got, b_out)):
+        out[...] = (zero[0].astype(F32) + got[0].astype(F32)).astype(BF16)
+
+
+def add_second(a_zero, a_got, b_zero, b_got):
+    shape = a_zero.shape[1:]
+    block = pl.BlockSpec((1, 1) + shape[1:], lambda k: (1, k) + (0,) * (len(shape) - 1))
+    out = pl.BlockSpec((1,) + shape[1:], lambda k: (k,) + (0,) * (len(shape) - 1))
+    return pl.pallas_call(
+        add_kernel,
+        grid=(shape[0],),
+        in_specs=[block] * 4,
+        out_specs=[out] * 2,
+        out_shape=[jax.ShapeDtypeStruct(shape, BF16)] * 2,
+        compiler_params=params(),
+        cost_estimate=COST,
+        name="add_second",
+    )(a_zero, a_got, b_zero, b_got)
+
+
+def fold_kernel(a_zero, a_got, a_last, b_zero, b_got, b_last, *outs):
+    for part, (zero, got, last_got) in enumerate(((a_zero, a_got, a_last), (b_zero, b_got, b_last))):
+        for k, out in enumerate(outs):
+            total = zero[0, k].astype(F32) + got[0, k].astype(F32) + last_got[k].astype(F32)
+            out[part] = total.astype(BF16)
+
+
+def fold_first(a_zero, a_got, a_last, b_zero, b_got, b_last):
+    shape = a_last.shape
+    first = whole((1,) + shape)
+    out = (2,) + shape[1:]
+    return pl.pallas_call(
+        fold_kernel,
+        grid=(1,),
+        in_specs=[first, first, whole(shape)] * 2,
+        out_specs=[whole(out)] * shape[0],
+        out_shape=[jax.ShapeDtypeStruct(out, BF16)] * shape[0],
+        compiler_params=params(),
+        cost_estimate=COST,
+        name="fold_first",
+    )(a_zero, a_got, a_last, b_zero, b_got, b_last)
 
 
 def finish_kernel(middle, one, two, dest_own, dest_halo, own_out, halo_out, total, total_halo):
@@ -374,26 +456,27 @@
         ],
         scratch_shapes=[pltpu.VMEM((count, wide), F32), pltpu.VMEM((HALO, wide), F32)],
         compiler_params=params(),
-        cost_estimate=cost(2 * rows * (count + HALO) * wide, 10 * rows * wide),
+        cost_estimate=COST,
         name="finish",
     )(middle, one, two, dest_own, dest_halo)
 
 
-def back_kernel(
-    middle, one, two, cot, gain, weight, qkv, prob, gm_out, gp_out, dq_out, part_out, sums_out
-):
+def back_kernel(held_count, place, middle, one, two, cot, norms, qkv, prob, *refs):
+    held = refs[:held_count]
+    gm_out, gp_out, dq_out, part_out, sums_out, weight, sem = refs[held_count:]
     step = pl.program_id(0)
     third = weight.shape[2] // 4
 
     @pl.when(step == 0)
     def _():
         sums_out[...] = jnp.zeros_like(sums_out)
+        load_weight(place, held, weight, sem)
 
     grad = one[...].astype(F32) + two[...].astype(F32)
     hat, inverse = stats(middle[...])
     sums_out[0:1] += jnp.sum(grad * hat, axis=0, keepdims=True)
     sums_out[1:2] += jnp.sum(grad, axis=0, keepdims=True)
-    grad_middle = cot[...].astype(F32) + norm_back(grad, hat, inverse, gain[...])
+    grad_middle = cot[...].astype(F32) + norm_back(grad, hat, inverse, norms[2:3])
     gm_out[...] = grad_middle
     grad_proj = grad_middle.astype(BF16)
     gp_out[...] = grad_proj
@@ -427,24 +510,25 @@
     part_out[...] = total.astype(BF16)
 
 
-def back(middle, one, two, cot, gain, weight, qkv, prob, slots):
+def back(place, middle, one, two, cot, norms, held, qkv, prob, slots):
     rows, wide = middle.shape
-    groups, third = weight.shape[0], weight.shape[2] // 4
+    groups, third = qkv.shape[0], qkv.shape[2] // 3
     tile = pl.BlockSpec((SLOT, wide), lambda t: (t, 0))
     tile_q = pl.BlockSpec((groups, SLOT, 3 * third), lambda t: (0, t, 0))
     return pl.pallas_call(
-        back_kernel,
+        functools.partial(back_kernel, len(held)),
         grid=(slots,),
         in_specs=[
+            SMEM,
             tile,
             tile,
             tile,
             tile,
-            whole(gain.shape),
-            whole(weight.shape),
+            whole(norms.shape),
             tile_q,
             pl.BlockSpec((1,) + prob.shape[1:], lambda t: (t, 0, 0, 0, 0)),
-        ],
+        ]
+        + [ANY] * len(held),
         out_specs=[tile, tile, tile_q, tile, whole((8, wide))],
         out_shape=[
             jax.ShapeDtypeStruct((rows, wide), F32),
@@ -453,42 +537,61 @@
             jax.ShapeDtypeStruct((rows, wide), BF16),
             jax.ShapeDtypeStruct((8, wide), F32),
         ],
+        scratch_shapes=[
+            pltpu.VMEM((groups, wide, 4 * third), BF16),
+            pltpu.SemaphoreType.DMA((piece_count(held),)),
+        ],
         compiler_params=params(),
-        cost_estimate=cost(2 * rows * wide * groups * 4 * third * 2, 24 * rows * wide),
+        cost_estimate=COST,
         name="back",
-    )(middle, one, two, cot, gain, weight, qkv, prob)
-
-
-def weight_kernel(normed, grad_proj, grad_qkv, att, out):
+    )(place, middle, one, two, cot, norms, qkv, prob, *held)
+
+
+def weight_kernel(held_count, place, normed, grad_proj, grad_qkv, att, *refs):
+    held = refs[:held_count]
+    result, sem = refs[held_count:]
     third = att.shape[2]
-    out[0, :, : 3 * third] = dot(normed[...], grad_qkv[0], TN).astype(BF16)
-    out[0, :, 3 * third :] = dot(grad_proj[...], att[0], TN).astype(BF16)
-
-
-def weight_grads(normed, grad_proj, grad_qkv, att):
+    cut = normed.shape[1]
+    at = pl.ds(pl.multiple_of(pl.program_id(0) * cut, cut), cut)
+    for group in range(2):
+        result[group, at, : 3 * third] = dot(normed[...], grad_qkv[group], TN).astype(BF16)
+        result[group, at, 3 * third :] = dot(grad_proj[...], att[group], TN).astype(BF16)
+
+    @pl.when(pl.program_id(0) == pl.num_programs(0) - 1)
+    def _():
+        copies = [
+            pltpu.make_async_copy(result.at[group, pl.ds(first, size)], ref, sem.at[i])
+            for i, (ref, group, first, size) in enumerate(weight_pieces(place, held))
+        ]
+        for copy in copies:
+            copy.start()
+        for copy in copies:
+            copy.wait()
+
+
+def weight_grads(place, normed, grad_proj, grad_qkv, att, held):
     rows, wide = normed.shape
     groups, _, third = att.shape
     cut = 256
-    tall = pl.BlockSpec((rows, cut), lambda d, g: (0, d))
+    tall = pl.BlockSpec((rows, cut), lambda d: (0, d))
     return pl.pallas_call(
-        weight_kernel,
-        grid=(wide // cut, groups),
-        in_specs=[
-            tall,
-            tall,
-            pl.BlockSpec((1, rows, 3 * third), lambda d, g: (g, 0, 0)),
-            pl.BlockSpec((1, rows, third), lambda d, g: (g, 0, 0)),
-        ],
-        out_specs=pl.BlockSpec((1, cut, 4 * third), lambda d, g: (g, d, 0)),
-        out_shape=jax.ShapeDtypeStruct((groups, wide, 4 * third), BF16),
+        functools.partial(weight_kernel, len(held)),
+        grid=(wide // cut,),
+        in_specs=[SMEM, tall, tall, whole(grad_qkv.shape), whole(att.shape)],
+        out_specs=[ANY] * len(held),
+        out_shape=[jax.ShapeDtypeStruct(v.shape, BF16) for v in held],
+        scratch_shapes=[
+            pltpu.VMEM((groups, wide, 4 * third), BF16),
+            pltpu.SemaphoreType.DMA((piece_count(held),)),
+        ],
         compiler_params=params(),
-        cost_estimate=cost(2 * rows * wide * groups * 4 * third, 20 * rows * wide),
+        cost_estimate=COST,
         name="weight_grads",
-    )(normed, grad_proj, grad_qkv, att)
+    )(place, normed, grad_proj, grad_qkv, att)
 
 
 def last_kernel(
-    x_in, gm, one, two, gain, dest_own, dest_halo, own_out, halo_out, prompt_out, sums_out, halo_sum
+    x_in, gm, one, two, norms, dest_own, dest_halo, own_out, halo_out, prompt_out, sums_out, halo_sum
 ):
     step = pl.program_id(0)
 
@@ -501,7 +604,7 @@
     hat, inverse = stats(x_in[...].astype(F32))
     sums_out[0:1] += jnp.sum(grad * hat, axis=0, keepdims=True)
     sums_out[1:2] += jnp.sum(grad, axis=0, keepdims=True)
-    grad_in = gm[...] + norm_back(grad, hat, inverse, gain[...])
+    grad_in = gm[...] + norm_back(grad, hat, inverse, norms[0:1])
     prompt_out[...] += grad_in[: prompt_out.shape[0]]
     at = lax.broadcasted_iota(jnp.int32, (SLOT, 1), 0)
     value = jnp.where((at >= 1) & (at <= PROMPTS), 0.0, grad_in).astype(BF16)
@@ -512,14 +615,14 @@
         halo_out[...] = halo_sum[...].astype(BF16)
 
 
-def last(x_in, gm, one, two, gain, dest_own, dest_halo, slots):
+def last(x_in, gm, one, two, norms, dest_own, dest_halo, slots):
     rows, wide = x_in.shape
     count = dest_own.shape[1]
     tile = pl.BlockSpec((SLOT, wide), lambda t: (t, 0))
     return pl.pallas_call(
         last_kernel,
         grid=(slots,),
-        in_specs=[tile] * 4 + [whole(gain.shape), whole(dest_own.shape), whole(dest_halo.shape)],
+        in_specs=[tile] * 4 + [whole(norms.shape), whole(dest_own.shape), whole(dest_halo.shape)],
         out_specs=[whole((count, wide)), whole((HALO, wide)), whole((56, wide)), whole((8, wide))],
         out_shape=[
             jax.ShapeDtypeStruct((count, wide), F32),
@@ -529,9 +632,9 @@
         ],
         scratch_shapes=[pltpu.VMEM((HALO, wide), F32)],
         compiler_params=params(),
-        cost_estimate=cost(2 * rows * (count + HALO) * wide, 10 * rows * wide),
+        cost_estimate=COST,
         name="last",
-    )(x_in, gm, one, two, gain, dest_own, dest_halo)
+    )(x_in, gm, one, two, norms, dest_own, dest_halo)
 
 
 class Grid:
@@ -567,8 +670,9 @@
     def gather_z(self, value):
         return [value] + [self.by_z(value, k) for k in range(1, self.deep)]
 
-    def scatter_z(self, values):
+    def scatter_z(self, values, earlier):
         got = [self.by_z(values[k], self.deep - k) for k in range(1, self.deep)]
+        got = tie(*got, earlier)[:-1]
         total = values[0].astype(F32)
         for item in got:
             total = total + item.astype(F32)
@@ -583,13 +687,6 @@
     def spread_more(self, a_zero, b_zero):
         return self.by_x(a_zero), self.by_y(b_zero)
 
-    def fold(self, a_zero, b_zero, a_one, b_one):
-        a_got, b_got = tie(self.by_x(a_one), self.by_y(b_one))
-        a_last, b_last = tie(
-            self.by_y(plus(a_zero[1], a_got[1])), self.by_x(plus(b_zero[1], b_got[1]))
-        )
-        return plus(a_zero[0], a_got[0], a_last), plus(b_zero[0], b_got[0], b_last)
-
     def to_absolute(self, blocks, z_axis, x_axis):
         size = self.deep
         turned = jnp.take(blocks, jnp.asarray([-m % size for m in range(size)]), axis=z_axis)
@@ -607,11 +704,8 @@
     return lax.optimization_barrier(values)
 
 
-def plus(*values):
-    total = values[0].astype(F32)
-    for item in values[1:]:
-        total = total + item.astype(F32)
-    return total.astype(values[0].dtype)
+def after(value, *earlier):
+    return lax.optimization_barrier((value, *earlier))[0]
 
 
 def local(
@@ -642,67 +736,71 @@
     def row_of(vec):
         return vec.astype(F32).reshape(1, -1)
 
+    norms = jnp.stack([attn_gain, attn_shift, mlp_gain, mlp_shift]).astype(F32)
+
     depth = qkv_weight.shape[0]
     third = qkv_weight.shape[2]
     shard = jnp.concatenate(
         [qkv_weight.reshape(depth, 3 * third), out_weight.swapaxes(0, 1)], axis=1
     ).reshape(2, depth // 2, 4 * third)
-    got = grid.gather_z(shard)
-    got = list(tie(*got))
-    a_zero, b_zero = grid.spread(jnp.stack([g[0] for g in got]), jnp.stack([g[1] for g in got]))
-    a_one, b_one = grid.spread_more(a_zero, b_zero)
+    hidden = up_weight.shape[1]
+    span = hidden // 2
+    bias = jnp.stack(grid.gather_z(up_bias.reshape(2, span)))
+    bias = jnp.stack([bias, grid.by_x(bias)])
+    bias = jnp.stack([bias, grid.by_y(bias)])
+    *got, bias = tie(*grid.gather_z(shard), bias)
 
     code = ((segment % IMGS_ROW) * 2 + live_token).astype(BF16)
     marks = jnp.pad(code[None], ((0, 15), (0, wide - count)))
-    own = jnp.concatenate([tokens, cotangent, marks])
+    own = after(jnp.concatenate([tokens, cotangent, marks]), shard)
     other = grid.by_core(own)
-    edge_source = jnp.where(grid.c == 1 - grid.y, 1, 0)
+    mine = grid.c == 1 - grid.y
     first_row = jnp.where(grid.y == 0, count - HALO, 0)
     edge_parts = []
-    for base, size in ((0, HALO), (count, HALO)):
-        mine = lax.dynamic_slice_in_dim(own, base + first_row, size)
-        theirs = lax.dynamic_slice_in_dim(other, base + first_row, size)
-        edge_parts.append(jnp.where(edge_source == 1, mine, theirs))
-    code_source = jnp.where(edge_source == 1, own[2 * count], other[2 * count])
-    edge_code = lax.dynamic_slice_in_dim(code_source, first_row, HALO)
-    edge_parts.append(jnp.pad(edge_code[None], ((0, 15), (0, wide - HALO))))
-    halo = grid.by_y(jnp.concatenate(edge_parts))
-    prom = jnp.pad(prompts, ((1, SLOT - PROMPTS - 1), (0, 0)))
-    x_in, normed, cot, dest_own, dest_halo = prep(
-        place, own, other, halo, prom, row_of(attn_gain), row_of(attn_shift), slots
-    )
-
-    hidden = up_weight.shape[1]
-    span = hidden // 2
+    for base in (0, count):
+        edge_parts.append(
+            jnp.where(
+                mine,
+                lax.dynamic_slice_in_dim(own, base + first_row, HALO),
+                lax.dynamic_slice_in_dim(other, base + first_row, HALO),
+            )
+        )
+    edge_code = jnp.where(mine, own[2 * count :], other[2 * count :])
+    edge_code = jnp.where(grid.y == 0, edge_code[:, count - HALO : count], edge_code[:, :HALO])
+    edge_parts.append(jnp.pad(edge_code, ((0, 0), (0, wide - HALO))))
+    edge = jnp.concatenate(edge_parts)
+    halo = grid.by_y(edge)
+
+    a_zero, b_zero = grid.spread(jnp.stack([g[0] for g in got]), jnp.stack([g[1] for g in got]))
+    a_zero, b_zero, _ = tie(a_zero, b_zero, edge)
+    a_one, b_one = grid.spread_more(a_zero, b_zero)
+    x_in, normed, cot, dest_own, dest_halo = prep(place, own, other, halo, prompts, norms, slots)
+
     shard = jnp.stack(
         [up_weight.swapaxes(0, 1).reshape(2, span, wide), down_weight.reshape(2, span, wide)],
         axis=1,
     )
-    shard, got[0] = tie(shard, got[0])
-    held = grid.gather_z(shard)
-    bias = jnp.stack(grid.gather_z(up_bias.reshape(2, span)))
-    bias = jnp.stack([bias, grid.by_x(bias)])
-    bias = jnp.stack([bias, grid.by_y(bias)])
-    mlp_a0, mlp_b0 = grid.spread(jnp.stack([h[0] for h in held]), jnp.stack([h[1] for h in held]))
+    shard = after(shard, got[0])
+    held = tie(*grid.gather_z(shard), normed)[:deep]
+    mlp_a = jnp.stack([h[0] for h in held])
+    mlp_b = jnp.stack([h[1] for h in held])
+    mlp_a0, mlp_b0 = grid.spread(mlp_a, mlp_b)
     mlp_a1, mlp_b1 = grid.spread_more(mlp_a0, mlp_b0)
     bias_a = jnp.stack([bias[0, 0, :, 0], bias[1, 0, :, 0], bias[0, 0, :, 1], bias[0, 1, :, 1]])
     bias_b = jnp.stack([bias[0, 1, :, 0], bias[1, 1, :, 0], bias[1, 0, :, 1], bias[1, 1, :, 1]])
 
-    blocks = jnp.stack(
-        [
-            jnp.concatenate(
-                [(a_zero, a_one)[dx][dy], (b_zero, b_one)[dy][dx]], axis=1
-            )
-            for dy in range(2)
-            for dx in range(2)
-        ]
-    ).reshape(2, 2, deep, depth, 4 * third)
-    blocks = grid.to_absolute(blocks, 2, 1).swapaxes(1, 2)
-    weight = blocks.reshape(2, 2 * deep * depth, 4 * third)
-    qkv, prob, att, part = attend(normed, weight, slots)
-    middle, normed_two = mid(
-        x_in, part, grid.by_core(part), row_of(mlp_gain), row_of(mlp_shift), slots
-    )
+    weights = [a_zero, a_one, b_zero, b_one]
+    if (depth // 2) % 16:
+        blocks = jnp.stack(
+            [
+                jnp.concatenate([(a_zero, a_one)[dx][dy], (b_zero, b_one)[dy][dx]], axis=1)
+                for dy in range(2)
+                for dx in range(2)
+            ]
+        ).reshape(2, 2, deep, depth, 4 * third)
+        blocks = grid.to_absolute(blocks, 2, 1).swapaxes(1, 2)
+        weights = [blocks.reshape(2, 2 * deep * depth, 4 * third)]
+    qkv, prob, att, part = attend(place, normed, weights, slots)
 
     fine = span % 16 == 0
 
@@ -716,41 +814,63 @@
             return value
         return value.reshape(2, 2, deep, span, wide).swapaxes(1, 2)
 
-    o_sum, g_sum, grad_a0, grad_b0, grad_bias_a = mlp(
-        enter(mlp_a0), enter(mlp_b0), normed_two, cot, row_of(bias_a), slots
+    start = (x_in, part, grid.by_core(part), norms)
+    middle, normed_two, o_sum, g_sum, grad_a0, grad_b0, grad_bias_a = mlp(
+        enter(mlp_a0), enter(mlp_b0), cot, row_of(bias_a), slots, start
     )
     o_part, g_part, grad_a1, grad_b1, grad_bias_b = mlp(
-        enter(mlp_a1), enter(mlp_b1), normed_two, cot, row_of(bias_b), slots, (o_sum, g_sum)
-    )
+        enter(mlp_a1), enter(mlp_b1), cot, row_of(bias_b), slots, normed_two, (o_sum, g_sum)
+    )
+    grad_a0, grad_b0 = leave(grad_a0), leave(grad_b0)
+    a_got, b_got = grid.by_x(leave(grad_a1)), grid.by_y(leave(grad_b1))
     g_other = grid.by_core(g_part)
-    grad_a, grad_b = grid.fold(leave(grad_a0), leave(grad_b0), leave(grad_a1), leave(grad_b1))
-    grad_shard = grid.scatter_z([jnp.stack([grad_a[k], grad_b[k]]) for k in range(deep)])
+    o_other = grid.by_core(after(o_part, g_other))
+
+    grad_middle, grad_proj, grad_qkv, g_one, sums_two = back(
+        place, middle, g_part, g_other, cot, norms, weights, qkv, prob, slots
+    )
+    g_one_other = grid.by_core(g_one)
+    a_got, b_got, _ = tie(a_got, b_got, g_one)
+    a_send, b_send = add_second(grad_a0, a_got, grad_b0, b_got)
+    a_last, b_last = grid.by_y(a_send), grid.by_x(b_send)
+    weight_blocks = weight_grads(
+        place, after(normed, a_send), grad_proj, grad_qkv, att, weights
+    )
+    if len(weight_blocks) == 1:
+        blocks = weight_blocks[0].reshape(2, deep, 2, depth, 4 * third).swapaxes(1, 2)
+        blocks = grid.to_relative(blocks, 2, 1)
+        blocks = blocks.reshape(2, 2, deep, 2, depth // 2, 4 * third)
+        weight_blocks = [
+            blocks[:, 0, :, 0],
+            blocks[:, 1, :, 0],
+            blocks[0, :, :, 1],
+            blocks[1, :, :, 1],
+        ]
+    att_a0, att_a1, att_b0, att_b1 = weight_blocks
+    att_a_got, att_b_got = grid.by_x(att_a1), grid.by_y(att_b1)
+    a_last, b_last, _ = tie(a_last, b_last, att_a1)
+    pieces = fold_first(grad_a0, a_got, a_last, grad_b0, b_got, b_last)
+
+    att_a_got, att_b_got, _ = tie(att_a_got, att_b_got, pieces[0])
+    a_send, b_send = add_second(att_a0, att_a_got, att_b0, att_b_got)
+    att_a_last, att_b_last = grid.by_y(a_send), grid.by_x(b_send)
+    tok_own, tok_halo, prompt_sum, sums_one = last(
+        x_in, grad_middle, g_one, after(g_one_other, a_send), norms, dest_own, dest_halo, slots
+    )
+    tok_edge = grid.by_y(tok_halo)
+    att_a_last, att_b_last, _ = tie(att_a_last, att_b_last, tok_halo)
+    att_pieces = fold_first(att_a0, att_a_got, att_a_last, att_b0, att_b_got, att_b_last)
+    out_own, out_halo = finish(
+        middle, o_part, after(o_other, att_pieces[0]), dest_own, dest_halo, slots
+    )
+    out_edge = grid.by_y(out_halo)
+    grad_shard = grid.scatter_z(pieces, out_halo)
     grad_up = grad_shard[:, 0].reshape(hidden, wide).swapaxes(0, 1)
     grad_down = grad_shard[:, 1].reshape(hidden, wide)
-    o_other = grid.by_core(o_part)
-    out_own, out_halo = finish(middle, o_part, o_other, dest_own, dest_halo, slots)
-    out_edge = grid.by_y(out_halo)
-
-    grad_middle, grad_proj, grad_qkv, g_one, sums_two = back(
-        middle, g_part, g_other, cot, row_of(mlp_gain), weight, qkv, prob, slots
-    )
-    g_one_other = grid.by_core(g_one)
-    grad_weight = weight_grads(normed, grad_proj, grad_qkv, att)
-    blocks = grad_weight.reshape(2, deep, 2, depth, 4 * third).swapaxes(1, 2)
-    blocks = grid.to_relative(blocks, 2, 1)
-    blocks = blocks.reshape(2, 2, deep, 2, depth // 2, 4 * third)
-    att_a, att_b = grid.fold(
-        blocks[:, 0, :, 0], blocks[0, :, :, 1], blocks[:, 1, :, 0], blocks[1, :, :, 1]
-    )
-    att_shard = grid.scatter_z([jnp.stack([att_a[k], att_b[k]]) for k in range(deep)])
+    att_shard = grid.scatter_z(att_pieces, out_halo)
     att_shard = att_shard.reshape(depth, 4 * third)
     grad_qkv_weight = att_shard[:, : 3 * third].reshape(depth, 3, third)
     grad_out_weight = att_shard[:, 3 * third :].swapaxes(0, 1)
-
-    tok_own, tok_halo, prompt_sum, sums_one = last(
-        x_in, grad_middle, g_one, g_one_other, row_of(attn_gain), dest_own, dest_halo, slots
-    )
-    tok_edge = grid.by_y(tok_halo)
 
     def merge(value, edge):
         edge = edge.astype(value.dtype)

time: 344 us -> 264 us (0.77)
  waiting for transfers between devices: 111 us -> 49.4 us
  other arithmetic: 31.5 us -> 11.9 us
  local copies, waits for them, and re-layouts: 39 us -> 21.9 us
  Pallas kernels: 112 us -> 123 us
  starting transfers between devices: 47.4 us -> 55.5 us
    ppermute x45, waiting for transfers between devices: 111 us -> 49.4 us  [send(): return lax.ppermute(value, AXES, pairs)]
    pallas_call x5 -> x8, Pallas kernels: 60.5 us -> 69.3 us  [the longest x1 23.1 us: back(): pl.pallas_call(functools.partial(back_kernel, len(held)), grid=(slots,),...]
    ppermute x45, starting transfers between devices: 47.4 us -> 55.5 us  [send(): return lax.ppermute(value, AXES, pairs)]
    convert_element_type x6 -> x1, other arithmetic: 7.49 us -> 0.61 us  [local(): norms = jnp.stack([attn_gain, attn_shift, mlp_gain, mlp_shift]).astype(F32)]
    reshape x5 -> x0, local copies, waits for them, and re-layouts: 6.88 us -> none  [the longest x4 5.06 us: row_of(): return vec.astype(F32).reshape(1, -1)]
    slice x12 -> x4, local copies, waits for them, and re-layouts: 4.75 us -> 0.75 us  [the longest x1 0.59 us: local(): bias[0, 1, :, 0]]
    unnamed x48 -> x72, local copies, waits for them, and re-layouts: 9.07 us -> 8.66 us
  transfers between devices with their start and end apart: 45 -> 45, of which waited for: 19 -> 18; matrix products, arithmetic and copies ran while one was open for 18% -> 10% of each run, Pallas kernels for 27% -> 40%
where the time goes in v2:
time: 264 us; the launch traced here: 263 us
  Pallas kernels  123 us (47%)
  starting transfers between devices  55.5 us (21%)
  waiting for transfers between devices  49.4 us (19%)
  local copies, waits for them, and re-layouts  21.9 us (8%)
  other arithmetic  11.9 us (5%)
    ppermute x45, starting transfers between devices, send(): return lax.ppermute(value, AXES, pairs)  55.5 us
    ppermute x45, waiting for transfers between devices, send(): return lax.ppermute(value, AXES, pairs)  49.4 us
    pallas_call x2, Pallas kernels, mlp(): pl.pallas_call(functools.partial(mlp_kernel, more), grid=(slots,), in_spe...  38.1 us
    pallas_call x1, Pallas kernels, back(): pl.pallas_call(functools.partial(back_kernel, len(held)), grid=(slots,),...  23.1 us
    pallas_call x1, Pallas kernels, attend(): pl.pallas_call(functools.partial(attend_kernel, len(held)), grid=(slots,)...  16.3 us
    pallas_call x1, Pallas kernels, prep(): pl.pallas_call(prep_kernel, grid=(slots,), in_specs=[SMEM] + [whole(v.sha...  9.43 us
    pallas_call x1, Pallas kernels, weight_grads(): pl.pallas_call(functools.partial(weight_kernel, len(held)), grid=(wide //...  8.96 us
    unnamed x72, local copies, waits for them, and re-layouts  8.66 us
  transfers between devices with their start and end apart: 45, of which 18 were waited for; matrix products, arithmetic and copies ran while one was open for 10% of the time, Pallas kernels for 40%

profile of v2, /device:TPU:0, one launch (start us, length us, event | category | flops | bytes accessed | tf_op | source)
XLA Modules:
  0.0 262.9 jit_solution(4222754335658127526)
XLA Ops:
  1.5 5.0 %collective-permute-start.5 = (bf16[2,48]{1,0:T(2,128)(2,1)S(1)}, bf16[2,48]{1,0:T(2,128)(2,1)S(1)}, u32[]{:S(2)}, u32[]{:S(2)}) collective-permute-start(bf16[2,48]{1,0:T(2,128)(2,1)S(1)} %reshape.191), channel_id=1, source_target_pairs={{0,24},{1,25},{2,26},{3,27},{4,28},{5,29},{6,30},{7,31},{8,0},{9,1... | collective-permute-start | bytes 584 | tf_op jit(solution)/shard_map/ppermute | solution.py:656
  9.7 2.9 %collective-permute-start.2 = (bf16[2,48,768]{2,1,0:T(8,128)(2,1)S(1)}, bf16[2,48,768]{2,1,0:T(8,128)(2,1)S(1)}, u32[]{:S(2)}, u32[]{:S(2)}) collective-permute-start(bf16[2,48,768]{2,1,0:T(8,128)(2,1)S(1)} %pad_maximum_fusion.10), channel_id=1, source_target_pairs={{0,24},{1,25},{2,26},{3,27},{4,28},{5,29},{6,30},{7,31},{8,0},{9,1... | collective-permute-start | bytes 442376 | tf_op jit(solution)/shard_map/ppermute | solution.py:656
  31.3 3.8 %collective-permute-start.10 = (bf16[2,2,48,768]{3,2,1,0:T(8,128)(2,1)S(1)}, bf16[2,2,48,768]{3,2,1,0:T(8,128)(2,1)S(1)}, u32[]{:S(2)}, u32[]{:S(2)}) collective-permute-start(bf16[2,2,48,768]{3,2,1,0:T(8,128)(2,1)S(1)} %pad_maximum_fusion.6), channel_id=1, source_target_pairs={{0,24},{1,25},{2,26},{3,27},{4,28},{5,29},{6,30},{7,31},{8,0},{9,1... | collective-permute-start | bytes 884744 | tf_op jit(solution)/shard_map/ppermute | solution.py:656
  39.8 3.3 %collective-permute-done.12.halo = bf16[112,768]{1,0:T(8,128)(2,1)S(1)} collective-permute-done((bf16[112,768]{1,0:T(8,128)(2,1)S(1)}, bf16[112,768]{1,0:T(8,128)(2,1)S(1)}, u32[]{:S(2)}, u32[]{:S(2)}) %collective-permute-start.12) | collective-permute-done | bytes 172064 | tf_op jit(solution)/shard_map/ppermute | solution.py:656
  44.6 9.4 %prep.1 = (bf16[1088,768]{1,0:T(8,128)(2,1)}, bf16[1088,768]{1,0:T(8,128)(2,1)}, bf16[1088,768]{1,0:T(8,128)(2,1)}, s32[1,512]{1,0:T(1,128)}, s32[1,48]{1,0:T(1,128)}) custom-call(s32[4]{0:T(128)} %pad_add_fusion.place, bf16[1040,768]{1,0:T(8,128)(2,1)} %copy-done, bf16[1040,768]{1,0:T(8,128)(2,1)} %copy-done.11, bf16[112,768]{1,0:T(8,128)(2,1)} %copy-done.22, ...), custom_call_target="tpu_custom_call" | custom-call | flops 1 | bytes 1 | tf_op jit(solution)/shard_map/prep/pallas_call | solution.py:146
  54.1 4.5 %collective-permute-done.9 = bf16[2,2,48,768]{3,2,1,0:T(8,128)(2,1)S(1)} collective-permute-done((bf16[2,2,48,768]{3,2,1,0:T(8,128)(2,1)S(1)}, bf16[2,2,48,768]{3,2,1,0:T(8,128)(2,1)S(1)}, u32[]{:S(2)}, u32[]{:S(2)}) %collective-permute-start.9) | collective-permute-done | bytes 294944 | tf_op jit(solution)/shard_map/ppermute | solution.py:656
  61.7 16.3 %attend.1 = (bf16[2,1088,576]{2,1,0:T(8,128)(2,1)}, bf16[4,2,3,256,256]{4,3,2,1,0:T(8,128)(2,1)}, bf16[2,1088,192]{2,1,0:T(8,128)(2,1)}, bf16[1088,768]{1,0:T(8,128)(2,1)}) custom-call(s32[4]{0:T(128)} %pad_add_fusion.place, bf16[1088,768]{1,0:T(8,128)(2,1)} %get-tuple-element.181.normed, bf16[2,4,48,768]{3,2,1,0:T(8,128)(2,1)} %copy-done.1, ...), custom_call_target="tpu_custom_call" | custom-call | flops 1 | bytes 1 | tf_op jit(solution)/shard_map/attend/pallas_call | solution.py:234
  85.3 19.5 %mlp.2 = (f32[1088,768]{1,0:T(8,128)}, bf16[1088,768]{1,0:T(8,128)(2,1)}, f32[1088,768]{1,0:T(8,128)}, f32[1088,768]{1,0:T(8,128)}, bf16[2,4,2,48,768]{4,3,2,1,0...) custom-call(bf16[2,4,2,48,768]{4,3,2,1,0:T(8,128)(2,1)} %copy-done.4, ...), custom_call_target="tpu_custom_call" | custom-call | flops 1 | bytes 1 | tf_op jit(solution)/shard_map/mlp/pallas_call | solution.py:355
  109.3 18.6 %mlp.3 = (bf16[1088,768]{1,0:T(8,128)(2,1)}, bf16[1088,768]{1,0:T(8,128)(2,1)}, bf16[2,4,2,48,768]{4,3,2,1,0:T(8,128)(2,1)}, bf16[2,4,2,48,768]{4,3,2,1,0:T(8,128)(2,1)}, f32[1,768]{1,0:T(1,128)}) custom-call(bf16[2,4,2,48,768]{4,3,2,1,0:T(8,128)(2,1)} %collective-permute-done.20.refs_0_, bf16[2,4,2,48,768]{4,3,2,1,0:T(8,128)(2,1)} %copy-done.14, ...), custom_call_target="tpu_custom_call" | custom-call | flops 1 | bytes 1 | tf_op jit(solution)/shard_map/mlp/pallas_call | solution.py:355
  133.0 23.1 %back.1 = (f32[1088,768]{1,0:T(8,128)}, bf16[1088,768]{1,0:T(8,128)(2,1)}, bf16[2,1088,576]{2,1,0:T(8,128)(2,1)}, bf16[1088,768]{1,0:T(8,128)(2,1)}, f32[8,768]{1,0:T(8,128)}) custom-call(s32[4]{0:T(128)} %pad_add_fusion.place, f32[1088,768]{1,0:T(8,128)} %get-tuple-element.164.middle, bf16[1088,768]{1,0:T(8,128)(2,1)} %get-tuple-element.169.one, ...), custom_call_target="tpu_custom_call" | custom-call | flops 1 | bytes 1 | tf_op jit(solution)/shard_map/back/pallas_call | solution.py:518
  158.9 3.9 %add_second.2 = (bf16[4,2,48,768]{3,2,1,0:T(8,128)(2,1)}, bf16[4,2,48,768]{3,2,1,0:T(8,128)(2,1)}) custom-call(bf16[2,4,2,48,768]{4,3,2,1,0:T(8,128)(2,1)} %get-tuple-element.171.a_zero, bf16[2,4,2,48,768]{4,3,2,1,0:T(8,128)(2,1)} %copy-done.5, bf16[2,4,2,48,768]{4,3,2,1,0:T(8,128)(2,1)} %get-tuple-element.178.b_zero, bf16[2,4,2,48,768]{4,3,2,1,0:T(8,128)(2,1)} %copy-done.6), custom_call_target="tpu_custom_call" | custom-call | flops 1 | bytes 1 | tf_op jit(solution)/shard_map/add_second/pallas_call | solution.py:391
  164.5 9.0 %weight_grads.1 = (bf16[2,4,48,768]{3,2,1,0:T(8,128)(2,1)}, bf16[2,4,48,768]{3,2,1,0:T(8,128)(2,1)}, bf16[2,4,48,768]{3,2,1,0:T(8,128)(2,1)}, bf16[2,4,48,768]{3,2,1,0:T(8,128)(2,1)}) custom-call(s32[4]{0:T(128)} %pad_add_fusion.place, bf16[1088,768]{1,0:T(8,128)(2,1)} %get-tuple-element.181.normed, bf16[1088,768]{1,0:T(8,128)(2,1)} %get-tuple-element.182.grad_proj, ...), custom_call_target="tpu_custom_call" | custom-call | flops 1 | bytes 1 | tf_op jit(solution)/shard_map/weight_grads/pallas_call | solution.py:577
  174.7 2.9 %collective-permute-done.29.b_last = bf16[4,2,48,768]{3,2,1,0:T(8,128)(2,1)S(1)} collective-permute-done((bf16[4,2,48,768]{3,2,1,0:T(8,128)(2,1)}, bf16[4,2,48,768]{3,2,1,0:T(8,128)(2,1)S(1)}, u32[]{:S(2)}, u32[]{:S(2)}) %collective-permute-start.29) | collective-permute-done | bytes 589856 | tf_op jit(solution)/shard_map/ppermute | solution.py:656
  180.0 3.2 %fold_first.2 = (bf16[2,2,48,768]{3,2,1,0:T(8,128)(2,1)}, bf16[2,2,48,768]{3,2,1,0:T(8,128)(2,1)}, bf16[2,2,48,768]{3,2,1,0:T(8,128)(2,1)}, bf16[2,2,48,768]{3,2,1,0:T(8,128)(2,1)}) custom-call(bf16[2,4,2,48,768]{4,3,2,1,0:T(8,128)(2,1)} %get-tuple-element.171.a_zero, bf16[2,4,2,48,768]{4,3,2,1,0:T(8,128)(2,1)} %copy-done.5, ...), custom_call_target="tpu_custom_call" | custom-call | flops 1 | bytes 1 | tf_op jit(solution)/shard_map/fold_first/pallas_call | solution.py:414
  183.2 9.0 %collective-permute-done.27.b_got = bf16[2,4,48,768]{3,2,1,0:T(8,128)(2,1)S(1)} collective-permute-done((bf16[2,4,48,768]{3,2,1,0:T(8,128)(2,1)}, bf16[2,4,48,768]{3,2,1,0:T(8,128)(2,1)S(1)}, u32[]{:S(2)}, u32[]{:S(2)}) %collective-permute-start.27) | collective-permute-done | bytes 589856 | tf_op jit(solution)/shard_map/ppermute | solution.py:656
  193.3 3.4 %add_second.3 = (bf16[4,48,768]{2,1,0:T(8,128)(2,1)}, bf16[4,48,768]{2,1,0:T(8,128)(2,1)}) custom-call(bf16[2,4,48,768]{3,2,1,0:T(8,128)(2,1)} %get-tuple-element.185.a_zero, bf16[2,4,48,768]{3,2,1,0:T(8,128)(2,1)} %copy-done.10, bf16[2,4,48,768]{3,2,1,0:T(8,128)(2,1)} %get-tuple-element.193.b_zero, bf16[2,4,48,768]{3,2,1,0:T(8,128)(2,1)} %copy-done.9), custom_call_target="tpu_custom_call" | custom-call | flops 1 | bytes 1 | tf_op jit(solution)/shard_map/add_second/pallas_call | solution.py:391
  201.2 4.3 %collective-permute-done.31.b_last = bf16[4,48,768]{2,1,0:T(8,128)(2,1)S(1)} collective-permute-done((bf16[4,48,768]{2,1,0:T(8,128)(2,1)}, bf16[4,48,768]{2,1,0:T(8,128)(2,1)S(1)}, u32[]{:S(2)}, u32[]{:S(2)}) %collective-permute-start.31) | collective-permute-done | bytes 294944 | tf_op jit(solution)/shard_map/ppermute | solution.py:656
  207.8 8.1 %last.1 = (f32[512,768]{1,0:T(8,128)}, bf16[48,768]{1,0:T(8,128)(2,1)}, f32[56,768]{1,0:T(8,128)}, f32[8,768]{1,0:T(8,128)}) custom-call(bf16[1088,768]{1,0:T(8,128)(2,1)} %get-tuple-element.153.refs_2_.x_in, f32[1088,768]{1,0:T(8,128)} %get-tuple-element.197.gm, bf16[1088,768]{1,0:T(8,128)(2,1)} %get-tuple-element.176.one, ...), custom_call_target="tpu_custom_call" | custom-call | flops 1 | bytes 1 | tf_op jit(solution)/shard_map/last/pallas_call | solution.py:622
  219.5 6.0 %finish.1 = (bf16[512,768]{1,0:T(8,128)(2,1)}, bf16[48,768]{1,0:T(8,128)(2,1)}) custom-call(f32[1088,768]{1,0:T(8,128)} %get-tuple-element.164.middle, bf16[1088,768]{1,0:T(8,128)(2,1)} %get-tuple-element.170.one, bf16[1088,768]{1,0:T(8,128)(2,1)} %collective-permute-done.23.two, s32[1,512]{1,0:T(1,128)} %get-tuple-element.199.dest_own, ...), custom_call_target="tpu_custom_call" | custom-call | flops 1 | bytes 1 | tf_op jit(solution)/shard_map/finish/pallas_call | solution.py:448
  228.7 2.9 %collective-permute-start.39 = (bf16[2,48,768]{2,1,0:T(8,128)(2,1)S(1)}, bf16[2,48,768]{2,1,0:T(8,128)(2,1)S(1)}, u32[]{:S(2)}, u32[]{:S(2)}) collective-permute-start(bf16[2,48,768]{2,1,0:T(8,128)(2,1)S(1)} %copy-done.31), channel_id=1, source_target_pairs={{0,24},{1,25},{2,26},{3,27},{4,28},{5,29},{6,30},{7,31},{8,0},{9,1... | collective-permute-start | bytes 442376 | tf_op jit(solution)/shard_map/ppermute | solution.py:656
  240.9 3.0 %collective-permute-done.36 = f32[62,768]{1,0:T(8,128)S(1)} collective-permute-done((f32[62,768]{1,0:T(8,128)S(1)}, f32[62,768]{1,0:T(8,128)S(1)}, u32[]{:S(2)}, u32[]{:S(2)}) %collective-permute-start.36) | collective-permute-done | bytes 190496 | tf_op jit(solution)/shard_map/ppermute | solution.py:656
  243.9 2.8 %collective-permute-start.37 = (f32[62,768]{1,0:T(8,128)S(1)}, f32[62,768]{1,0:T(8,128)S(1)}, u32[]{:S(2)}, u32[]{:S(2)}) collective-permute-start(f32[62,768]{1,0:T(8,128)S(1)} %add.129), channel_id=1, source_target_pairs={{0,8},{1,9},{2,10},{3,11},{4,12},{5,13},{6,14},{7,15},{8,0},{9,1},... | collective-permute-start | bytes 571400 | tf_op jit(solution)/shard_map/ppermute | solution.py:656
  248.3 3.9 %collective-permute-done.37 = f32[62,768]{1,0:T(8,128)S(1)} collective-permute-done((f32[62,768]{1,0:T(8,128)S(1)}, f32[62,768]{1,0:T(8,128)S(1)}, u32[]{:S(2)}, u32[]{:S(2)}) %collective-permute-start.37) | collective-permute-done | bytes 190496 | tf_op jit(solution)/shard_map/ppermute | solution.py:656
  255.7 5.3 %collective-permute-done.38 = f32[62,768]{1,0:T(8,128)S(1)} collective-permute-done((f32[62,768]{1,0:T(8,128)S(1)}, f32[62,768]{1,0:T(8,128)S(1)}, u32[]{:S(2)}, u32[]{:S(2)}) %collective-permute-start.38) | collective-permute-done | bytes 190496 | tf_op jit(solution)/shard_map/ppermute | solution.py:656
  (236 shorter events, 87.6 us)
Async XLA Ops:
  1.5 17.7 %collective-permute-start.5 = (bf16[2,48]{1,0:T(2,128)(2,1)S(1)}, bf16[2,48]{1,0:T(2,128)(2,1)S(1)}, u32[]{:S(2)}, u32[]{:S(2)}) collective-permute-start(bf16[2,48]{1,0:T(2,128)(2,1)S(1)} %reshape.191), channel_id=1, source_target_pairs={{0,24},{1,25},{2,26},{3,27},{4,28},{5,29},{6,30},{7,31},{8,0},{9,1... | collective-permute-start | bytes 584 | tf_op jit(solution)/shard_map/ppermute | solution.py:656
  9.7 17.0 %collective-permute-start.2 = (bf16[2,48,768]{2,1,0:T(8,128)(2,1)S(1)}, bf16[2,48,768]{2,1,0:T(8,128)(2,1)S(1)}, u32[]{:S(2)}, u32[]{:S(2)}) collective-permute-start(bf16[2,48,768]{2,1,0:T(8,128)(2,1)S(1)} %pad_maximum_fusion.10), channel_id=1, source_target_pairs={{0,24},{1,25},{2,26},{3,27},{4,28},{5,29},{6,30},{7,31},{8,0},{9,1... | collective-permute-start | bytes 442376 | tf_op jit(solution)/shard_map/ppermute | solution.py:656
  19.3 17.1 %collective-permute-start.11 = (bf16[1040,768]{1,0:T(8,128)(2,1)S(1)}, bf16[1040,768]{1,0:T(8,128)(2,1)S(1)}, u32[]{:S(2)}, u32[]{:S(2)}) collective-permute-start(bf16[1040,768]{1,0:T(8,128)(2,1)S(1)} %fusion.1.own), channel_id=1, source_target_pairs={{0,1},{1,0},{2,3},{3,2},{4,5},{5,4},{6,7},{7,6},{8,9},{9,8},{10,11... | collective-permute-start | bytes 4792328 | tf_op jit(solution)/shard_map/ppermute | solution.py:656
  31.3 22.7 %collective-permute-start.10 = (bf16[2,2,48,768]{3,2,1,0:T(8,128)(2,1)S(1)}, bf16[2,2,48,768]{3,2,1,0:T(8,128)(2,1)S(1)}, u32[]{:S(2)}, u32[]{:S(2)}) collective-permute-start(bf16[2,2,48,768]{3,2,1,0:T(8,128)(2,1)S(1)} %pad_maximum_fusion.6), channel_id=1, source_target_pairs={{0,24},{1,25},{2,26},{3,27},{4,28},{5,29},{6,30},{7,31},{8,0},{9,1... | collective-permute-start | bytes 884744 | tf_op jit(solution)/shard_map/ppermute | solution.py:656
  35.1 23.5 %collective-permute-start.9 = (bf16[2,2,48,768]{3,2,1,0:T(8,128)(2,1)S(1)}, bf16[2,2,48,768]{3,2,1,0:T(8,128)(2,1)S(1)}, u32[]{:S(2)}, u32[]{:S(2)}) collective-permute-start(bf16[2,2,48,768]{3,2,1,0:T(8,128)(2,1)S(1)} %pad_maximum_fusion.6), channel_id=1, source_target_pairs={{0,16},{1,17},{2,18},{3,19},{4,20},{5,21},{6,22},{7,23},{8,24},{9,... | collective-permute-start | bytes 884744 | tf_op jit(solution)/shard_map/ppermute | solution.py:656
  35.1 23.5 %collective-permute-start.8 = (bf16[2,2,48,768]{3,2,1,0:T(8,128)(2,1)S(1)}, bf16[2,2,48,768]{3,2,1,0:T(8,128)(2,1)S(1)}, u32[]{:S(2)}, u32[]{:S(2)}) collective-permute-start(bf16[2,2,48,768]{3,2,1,0:T(8,128)(2,1)S(1)} %pad_maximum_fusion.6), channel_id=1, source_target_pairs={{0,8},{1,9},{2,10},{3,11},{4,12},{5,13},{6,14},{7,15},{8,16},{9,17... | collective-permute-start | bytes 884744 | tf_op jit(solution)/shard_map/ppermute | solution.py:656
  38.3 21.8 %collective-permute-start.17 = (bf16[2,4,48,768]{3,2,1,0:T(8,128)(2,1)S(1)}, bf16[2,4,48,768]{3,2,1,0:T(8,128)(2,1)S(1)}, u32[]{:S(2)}, u32[]{:S(2)}) collective-permute-start(bf16[2,4,48,768]{3,2,1,0:T(8,128)(2,1)S(1)} %pad_maximum_fusion.4.refs_0_), channel_id=1, source_target_pairs={{0,4},{1,5},{2,6},{3,7},{4,0},{5,1},{6,2},{7,3},{8,12},{9,13},{10,... | collective-permute-start | bytes 1769480 | tf_op jit(solution)/shard_map/ppermute | solution.py:656
  43.1 17.0 %collective-permute-start.18 = (bf16[2,4,48,768]{3,2,1,0:T(8,128)(2,1)S(1)}, bf16[2,4,48,768]{3,2,1,0:T(8,128)(2,1)S(1)}, u32[]{:S(2)}, u32[]{:S(2)}) collective-permute-start(bf16[2,4,48,768]{3,2,1,0:T(8,128)(2,1)S(1)} %pad_maximum_fusion.5.refs_2_), channel_id=1, source_target_pairs={{0,2},{1,3},{2,0},{3,1},{4,6},{5,7},{6,4},{7,5},{8,10},{9,11},{10,... | collective-permute-start | bytes 1769480 | tf_op jit(solution)/shard_map/ppermute | solution.py:656
  58.8 19.3 %collective-permute-start.14 = (bf16[4,2,48,768]{3,2,1,0:T(8,128)(2,1)S(1)}, bf16[4,2,48,768]{3,2,1,0:T(8,128)(2,1)S(1)}, u32[]{:S(2)}, u32[]{:S(2)}) collective-permute-start(bf16[4,2,48,768]{3,2,1,0:T(8,128)(2,1)S(1)} %get-tuple-element.291), channel_id=1, source_target_pairs={{0,4},{1,5},{2,6},{3,7},{4,0},{5,1},{6,2},{7,3},{8,12},{9,13},{10,... | collective-permute-start | bytes 1769480 | tf_op jit(solution)/shard_map/ppermute | solution.py:656
  59.5 18.6 %collective-permute-start.13 = (bf16[4,2,48,768]{3,2,1,0:T(8,128)(2,1)S(1)}, bf16[4,2,48,768]{3,2,1,0:T(8,128)(2,1)S(1)}, u32[]{:S(2)}, u32[]{:S(2)}) collective-permute-start(bf16[4,2,48,768]{3,2,1,0:T(8,128)(2,1)S(1)} %get-tuple-element.293), channel_id=1, source_target_pairs={{0,2},{1,3},{2,0},{3,1},{4,6},{5,7},{6,4},{7,5},{8,10},{9,11},{10,... | collective-permute-start | bytes 1769480 | tf_op jit(solution)/shard_map/ppermute | solution.py:656
  78.3 28.4 %collective-permute-start.21 = (bf16[2,4,2,48,768]{4,3,2,1,0:T(8,128)(2,1)S(1)}, bf16[2,4,2,48,768]{4,3,2,1,0:T(8,128)(2,1)S(1)}, u32[]{:S(2)}, u32[]{:S(2)}) collective-permute-start(bf16[2,4,2,48,768]{4,3,2,1,0:T(8,128)(2,1)S(1)} %pad_maximum_fusion.1.refs_1_), channel_id=1, source_target_pairs={{0,2},{1,3},{2,0},{3,1},{4,6},{5,7},{6,4},{7,5},{8,10},{9,11},{10,... | collective-permute-start | bytes 3538952 | tf_op jit(solution)/shard_map/ppermute | solution.py:656
  81.1 28.2 %collective-permute-start.20 = (bf16[2,4,2,48,768]{4,3,2,1,0:T(8,128)(2,1)S(1)}, bf16[2,4,2,48,768]{4,3,2,1,0:T(8,128)(2,1)}, u32[]{:S(2)}, u32[]{:S(2)}) collective-permute-start(bf16[2,4,2,48,768]{4,3,2,1,0:T(8,128)(2,1)S(1)} %pad_maximum_fusion.refs_0_), channel_id=1, source_target_pairs={{0,4},{1,5},{2,6},{3,7},{4,0},{5,1},{6,2},{7,3},{8,12},{9,13},{10,... | collective-permute-start | bytes 3538952 | tf_op jit(solution)/shard_map/ppermute | solution.py:656
  128.0 28.6 %collective-permute-start.24 = (bf16[2,4,2,48,768]{4,3,2,1,0:T(8,128)(2,1)}, bf16[2,4,2,48,768]{4,3,2,1,0:T(8,128)(2,1)S(1)}, u32[]{:S(2)}, u32[]{:S(2)}) collective-permute-start(bf16[2,4,2,48,768]{4,3,2,1,0:T(8,128)(2,1)} %get-tuple-element.172), channel_id=1, source_target_pairs={{0,4},{1,5},{2,6},{3,7},{4,0},{5,1},{6,2},{7,3},{8,12},{9,13},{10,... | collective-permute-start | bytes 3538952 | tf_op jit(solution)/shard_map/ppermute | solution.py:656
  129.6 28.2 %collective-permute-start.25 = (bf16[2,4,2,48,768]{4,3,2,1,0:T(8,128)(2,1)}, bf16[2,4,2,48,768]{4,3,2,1,0:T(8,128)(2,1)S(1)}, u32[]{:S(2)}, u32[]{:S(2)}) collective-permute-start(bf16[2,4,2,48,768]{4,3,2,1,0:T(8,128)(2,1)} %get-tuple-element.173), channel_id=1, source_target_pairs={{0,2},{1,3},{2,0},{3,1},{4,6},{5,7},{6,4},{7,5},{8,10},{9,11},{10,... | collective-permute-start | bytes 3538952 | tf_op jit(solution)/shard_map/ppermute | solution.py:656
  156.1 49.9 %collective-permute-start.32 = (bf16[1088,768]{1,0:T(8,128)(2,1)}, bf16[1088,768]{1,0:T(8,128)(2,1)}, u32[]{:S(2)}, u32[]{:S(2)}) collective-permute-start(bf16[1088,768]{1,0:T(8,128)(2,1)} %get-tuple-element.176.one), channel_id=1, source_target_pairs={{0,1},{1,0},{2,3},{3,2},{4,5},{5,4},{6,7},{7,6},{8,9},{9,8},{10,11... | collective-permute-start | bytes 5013512 | tf_op jit(solution)/shard_map/ppermute | solution.py:656
  163.4 56.1 %collective-permute-start.23 = (bf16[1088,768]{1,0:T(8,128)(2,1)S(1)}, bf16[1088,768]{1,0:T(8,128)(2,1)}, u32[]{:S(2)}, u32[]{:S(2)}) collective-permute-start(bf16[1088,768]{1,0:T(8,128)(2,1)S(1)} %copy-done.13), channel_id=1, source_target_pairs={{0,1},{1,0},{2,3},{3,2},{4,5},{5,4},{6,7},{7,6},{8,9},{9,8},{10,11... | collective-permute-start | bytes 5013512 | tf_op jit(solution)/shard_map/ppermute | solution.py:656
  163.5 16.5 %collective-permute-start.28 = (bf16[4,2,48,768]{3,2,1,0:T(8,128)(2,1)}, bf16[4,2,48,768]{3,2,1,0:T(8,128)(2,1)}, u32[]{:S(2)}, u32[]{:S(2)}) collective-permute-start(bf16[4,2,48,768]{3,2,1,0:T(8,128)(2,1)} %get-tuple-element.180), channel_id=1, source_target_pairs={{0,2},{1,3},{2,0},{3,1},{4,6},{5,7},{6,4},{7,5},{8,10},{9,11},{10,... | collective-permute-start | bytes 1769480 | tf_op jit(solution)/shard_map/ppermute | solution.py:656
  173.5 18.7 %collective-permute-start.27 = (bf16[2,4,48,768]{3,2,1,0:T(8,128)(2,1)}, bf16[2,4,48,768]{3,2,1,0:T(8,128)(2,1)S(1)}, u32[]{:S(2)}, u32[]{:S(2)}) collective-permute-start(bf16[2,4,48,768]{3,2,1,0:T(8,128)(2,1)} %get-tuple-element.187), channel_id=1, source_target_pairs={{0,2},{1,3},{2,0},{3,1},{4,6},{5,7},{6,4},{7,5},{8,10},{9,11},{10,... | collective-permute-start | bytes 1769480 | tf_op jit(solution)/shard_map/ppermute | solution.py:656
  198.7 27.9 %collective-permute-start.42 = (bf16[2,2,48,768]{3,2,1,0:T(8,128)(2,1)}, bf16[2,2,48,768]{3,2,1,0:T(8,128)(2,1)S(1)}, u32[]{:S(2)}, u32[]{:S(2)}) collective-permute-start(bf16[2,2,48,768]{3,2,1,0:T(8,128)(2,1)} %get-tuple-element.220), channel_id=1, source_target_pairs={{0,24},{1,25},{2,26},{3,27},{4,28},{5,29},{6,30},{7,31},{8,0},{9,1... | collective-permute-start | bytes 884744 | tf_op jit(solution)/shard_map/ppermute | solution.py:656
  198.7 28.2 %collective-permute-start.43 = (bf16[2,2,48,768]{3,2,1,0:T(8,128)(2,1)}, bf16[2,2,48,768]{3,2,1,0:T(8,128)(2,1)S(1)}, u32[]{:S(2)}, u32[]{:S(2)}) collective-permute-start(bf16[2,2,48,768]{3,2,1,0:T(8,128)(2,1)} %get-tuple-element.221), channel_id=1, source_target_pairs={{0,16},{1,17},{2,18},{3,19},{4,20},{5,21},{6,22},{7,23},{8,24},{9,... | collective-permute-start | bytes 884744 | tf_op jit(solution)/shard_map/ppermute | solution.py:656
  205.5 21.4 %collective-permute-start.44 = (bf16[2,2,48,768]{3,2,1,0:T(8,128)(2,1)}, bf16[2,2,48,768]{3,2,1,0:T(8,128)(2,1)S(1)}, u32[]{:S(2)}, u32[]{:S(2)}) collective-permute-start(bf16[2,2,48,768]{3,2,1,0:T(8,128)(2,1)} %get-tuple-element.222), channel_id=1, source_target_pairs={{0,8},{1,9},{2,10},{3,11},{4,12},{5,13},{6,14},{7,15},{8,16},{9,17... | collective-permute-start | bytes 884744 | tf_op jit(solution)/shard_map/ppermute | solution.py:656
  216.0 16.4 %collective-permute-start.34 = (bf16[48,768]{1,0:T(8,128)(2,1)}, bf16[48,768]{1,0:T(8,128)(2,1)S(1)}, u32[]{:S(2)}, u32[]{:S(2)}) collective-permute-start(bf16[48,768]{1,0:T(8,128)(2,1)} %get-tuple-element.201), channel_id=1, source_target_pairs={{0,2},{1,3},{2,0},{3,1},{4,6},{5,7},{6,4},{7,5},{8,10},{9,11},{10,... | collective-permute-start | bytes 221192 | tf_op jit(solution)/shard_map/ppermute | solution.py:656
  228.7 19.6 %collective-permute-start.39 = (bf16[2,48,768]{2,1,0:T(8,128)(2,1)S(1)}, bf16[2,48,768]{2,1,0:T(8,128)(2,1)S(1)}, u32[]{:S(2)}, u32[]{:S(2)}) collective-permute-start(bf16[2,48,768]{2,1,0:T(8,128)(2,1)S(1)} %copy-done.31), channel_id=1, source_target_pairs={{0,24},{1,25},{2,26},{3,27},{4,28},{5,29},{6,30},{7,31},{8,0},{9,1... | collective-permute-start | bytes 442376 | tf_op jit(solution)/shard_map/ppermute | solution.py:656
  231.6 16.7 %collective-permute-start.40 = (bf16[2,48,768]{2,1,0:T(8,128)(2,1)S(1)}, bf16[2,48,768]{2,1,0:T(8,128)(2,1)S(1)}, u32[]{:S(2)}, u32[]{:S(2)}) collective-permute-start(bf16[2,48,768]{2,1,0:T(8,128)(2,1)S(1)} %copy-done.30), channel_id=1, source_target_pairs={{0,16},{1,17},{2,18},{3,19},{4,20},{5,21},{6,22},{7,23},{8,24},{9,... | collective-permute-start | bytes 442376 | tf_op jit(solution)/shard_map/ppermute | solution.py:656
  (53 other events, 405.1 us)

commit v3 on v2

--- a/solution.py
+++ b/solution.py
@@ -14,6 +14,7 @@
 PROMPTS = 50
 SLOT = 272
 CORE = 256
+TAIL = 16
 HALO = 48
 EPSILON = 1e-06
 AXES = ("rows", "heads")
@@ -38,7 +39,11 @@
     return pltpu.CompilerParams(vmem_limit_bytes=VMEM_LIMIT, **more)
 
 
-COST = pl.CostEstimate(flops=1, bytes_accessed=1, transcendentals=0)
+SCALE = 0.15
+
+
+def cost(time):
+    return pl.CostEstimate(flops=int(time * SCALE * 1.15e9), bytes_accessed=1, transcendentals=0)
 
 
 SMEM = pl.BlockSpec(memory_space=pltpu.SMEM)
@@ -157,9 +162,13 @@
         ],
         scratch_shapes=[pltpu.VMEM((1, count), jnp.int32)],
         compiler_params=params(),
-        cost_estimate=COST,
+        cost_estimate=cost(8),
         name="prep",
     )(place, own, other, halo, prom, norms)
+
+
+def reverse_bits(index, size):
+    return sum(((index >> i) & 1) * (size >> (i + 1)) for i in range(size.bit_length() - 1))
 
 
 def weight_pieces(place, refs):
@@ -173,7 +182,7 @@
         col = place[1] if dx == 0 else 1 - place[1]
         for dy in range(2):
             for k in range(deep):
-                row = lax.rem(place[0] + deep - k, deep)
+                row = place[0] ^ reverse_bits(k, deep)
                 for part in range(2):
                     ref = ((a_zero, a_one)[dx].at[dy, k], (b_zero, b_one)[dy].at[dx, k])[part]
                     first = ((row * 2 + col) * 2 + part) * half
@@ -184,11 +193,14 @@
     return 2 if len(held) == 1 else 8 * held[0].shape[1]
 
 
-def load_weight(place, held, weight, sem):
-    copies = [
+def weight_copies(place, held, weight, sem):
+    return [
         pltpu.make_async_copy(ref, weight.at[group, pl.ds(first, size)], sem.at[i])
         for i, (ref, group, first, size) in enumerate(weight_pieces(place, held))
     ]
+
+
+def load_weight(copies):
     for copy in copies:
         copy.start()
     for copy in copies:
@@ -198,29 +210,40 @@
 def attend_kernel(held_count, place, normed, *refs):
     held = refs[:held_count]
     qkv_out, prob_out, att_out, part_out, weight, sem = refs[held_count:]
+    copies = weight_copies(place, held, weight, sem)
 
     @pl.when(pl.program_id(0) == 0)
     def _():
-        load_weight(place, held, weight, sem)
+        load_weight(copies)
 
     third = weight.shape[2] // 4
-    rows = lax.broadcasted_iota(jnp.int32, (CORE, CORE), 0)
-    cols = lax.broadcasted_iota(jnp.int32, (CORE, CORE), 1)
-    allowed = ((rows < IMG) & (cols < IMG)) | (rows == cols)
+    live = lax.broadcasted_iota(jnp.int32, (TAIL, 1), 0) < IMG - (CORE - TAIL)
+    groups, heads = weight.shape[0], third // HEAD
+    pairs = [(group, head) for group in range(groups) for head in range(heads)]
+    for group in range(groups):
+        qkv_out[group] = dot(normed[...], weight[group, :, : 3 * third]).astype(BF16)
+
+    def part_of(which, group, head):
+        at = which * third + head * HEAD
+        return qkv_out[group, :CORE, at : at + HEAD]
+
+    scores = [dot(part_of(1, *pair), part_of(0, *pair) * 0.125, NT) for pair in pairs]
+    for (group, head), score in zip(pairs, scores):
+        score = jnp.concatenate(
+            [score[: CORE - TAIL], jnp.where(live, score[CORE - TAIL :], -1e30)]
+        )
+        exp_scores = jnp.exp(score - jnp.max(score, axis=0, keepdims=True))
+        shrink = 1.0 / jnp.sum(exp_scores, axis=0, keepdims=True)
+        prob_out[0, group, head] = (exp_scores * shrink).astype(BF16)
+    mixed = [dot(part_of(2, *pair), prob_out[(0, *pair)], TN) for pair in pairs]
     total = None
-    for group in range(weight.shape[0]):
-        qkv_out[group] = dot(normed[...], weight[group, :, : 3 * third]).astype(BF16)
-        for head in range(third // HEAD):
-            at = head * HEAD
-            queries = qkv_out[group, :CORE, at : at + HEAD]
-            keys = qkv_out[group, :CORE, third + at : third + at + HEAD]
-            values = qkv_out[group, :, 2 * third + at : 2 * third + at + HEAD]
-            scores = jnp.where(allowed, dot(queries, keys, NT) * 0.125, -1e30)
-            exp_scores = jnp.exp(scores - jnp.max(scores, axis=-1, keepdims=True))
-            probs = (exp_scores / jnp.sum(exp_scores, axis=-1, keepdims=True)).astype(BF16)
-            prob_out[0, group, head] = probs
-            att_out[group, :CORE, at : at + HEAD] = dot(probs, values[:CORE]).astype(BF16)
-            att_out[group, CORE:, at : at + HEAD] = values[CORE:]
+    for group in range(groups):
+        mix = jnp.concatenate(mixed[group * heads : (group + 1) * heads]).T.astype(BF16)
+        att_out[group, : CORE - TAIL] = mix[: CORE - TAIL]
+        att_out[group, CORE - TAIL : CORE] = jnp.where(
+            live, mix[CORE - TAIL :], qkv_out[group, CORE - TAIL : CORE, 2 * third :]
+        )
+        att_out[group, CORE:] = qkv_out[group, CORE:, 2 * third :]
         part = dot(att_out[group], weight[group, :, 3 * third :], NT)
         total = part if total is None else total + part
     part_out[...] = total.astype(BF16)
@@ -252,129 +275,130 @@
             pltpu.SemaphoreType.DMA((piece_count(held),)),
         ],
         compiler_params=params(),
-        cost_estimate=COST,
+        cost_estimate=cost(13),
         name="attend",
     )(place, normed, *held)
 
 
-def mlp_kernel(more, *refs):
+def mlp_kernel(more, count, *refs):
+    parts, refs = refs[:count], refs[count:]
     if more:
-        (a_in, b_in, normed, cot, bias, o_acc, g_acc, *refs) = refs
+        (normed, cot, bias, o_acc, g_acc, *refs) = refs
     else:
-        (a_in, b_in, x_in, one, two, norms, cot, bias, middle_out, normed, *refs) = refs
-    (o_out, g_out, a_out, b_out, bias_out, weight, act, grad, result, in_sem, out_sem) = refs
+        (x_in, one, two, norms, cot, bias, middle_out, normed, *refs) = refs
+    (o_out, g_out), grads, refs = refs[:2], refs[2 : 2 + count], refs[2 + count :]
+    (bias_out, weight, act, grad, result, in_sem, out_sem) = refs
     step = pl.program_id(0)
-    lead, count, _, span, _ = a_in.shape
-    hidden = weight.shape[1]
-
-    def pieces(first, second):
-        for source, ref in enumerate((first, second)):
-            for i in range(lead):
-                for j in range(count):
-                    for kind in range(2):
-                        place = ((source * lead + i) * count + j) * span
-                        index = ((source * lead + i) * count + j) * 2 + kind
-                        yield ref.at[i, j, kind], kind, place, index
+    _, pieces, span, wide = weight.shape
+    hidden = pieces * span
+    cut = 384
+    spots = []
+    for ref in parts:
+        spots.append(sum(size for _, size in spots))
+        spots[-1] = (spots[-1], ref.shape[0])
+    loads = [
+        pltpu.make_async_copy(
+            parts[i].at[:, kind], weight.at[kind, pl.ds(first, size)], in_sem.at[2 * i + kind]
+        )
+        for i, (first, size) in enumerate(spots)
+        for kind in range(2)
+    ]
+    stores = [
+        pltpu.make_async_copy(
+            result.at[kind, pl.ds(first, size)], grads[i].at[:, kind], out_sem.at[2 * i + kind]
+        )
+        for i, (first, size) in enumerate(spots)
+        for kind in range(2)
+    ]
 
     @pl.when(step == 0)
     def _():
-        copies = [
-            pltpu.make_async_copy(ref, weight.at[kind, pl.ds(place, span)], in_sem.at[index])
-            for ref, kind, place, index in pieces(a_in, b_in)
-        ]
-        for copy in copies:
+        for copy in loads:
             copy.start()
         bias_out[...] = jnp.zeros_like(bias_out)
-        for copy in copies:
+        for copy in loads:
             copy.wait()
 
     rows = pl.ds(pl.multiple_of(step * SLOT, 16), SLOT)
     if not more:
-        middle = x_in[...].astype(F32) + one[...].astype(F32) + two[...].astype(F32)
+        middle = x_in[...].astype(F32) + (one[...].astype(F32) + two[...].astype(F32))
         middle_out[...] = middle
         hat, _ = stats(middle)
         normed[rows] = (hat * norms[2:3] + norms[3:4]).astype(BF16)
     tile_n = normed[rows]
     tile_c = cot[rows]
-    cut = 256
-    o_sum = o_acc[...] if more else None
-    g_sum = g_acc[...] if more else None
     for at in range(0, hidden, cut):
-        up = weight[0, at : at + cut]
-        down = weight[1, at : at + cut]
+        up = weight[0, at // span : (at + cut) // span].reshape(cut, wide)
+        down = weight[1, at // span : (at + cut) // span].reshape(cut, wide)
         pre = dot(tile_n, up, NT) + bias[:, at : at + cut]
         cdf = 0.5 * (1.0 + lax.erf(pre * 0.7071067811865476))
         pdf = jnp.exp(-0.5 * pre * pre) * 0.3989422804014327
-        low = (pre * cdf).astype(BF16)
+        act[rows, at : at + cut] = (pre * cdf).astype(BF16)
         grad_low = (dot(tile_c, down, NT) * (cdf + pre * pdf)).astype(BF16)
-        act[rows, at : at + cut] = low
         grad[rows, at : at + cut] = grad_low
         bias_out[:, at : at + cut] += jnp.sum(grad_low.astype(F32), axis=0, keepdims=True)
-        o_part = dot(low, down)
-        g_part = dot(grad_low, up)
-        o_sum = o_part if o_sum is None else o_sum + o_part
-        g_sum = g_part if g_sum is None else g_sum + g_part
+    o_sum = dot(act[rows], weight[1].reshape(hidden, wide))
+    g_sum = dot(grad[rows], weight[0].reshape(hidden, wide))
+    if more:
+        o_sum = o_sum + o_acc[...].astype(F32)
+        g_sum = g_sum + g_acc[...].astype(F32)
     o_out[...] = o_sum.astype(o_out.dtype)
     g_out[...] = g_sum.astype(g_out.dtype)
 
     @pl.when(step == pl.num_programs(0) - 1)
     def _():
-        def tile(i, _):
-            at = pl.ds(pl.multiple_of(i * cut, cut), cut)
-            result[0, at] = dot(grad[:, at], normed[...], TN).astype(BF16)
-            result[1, at] = dot(act[:, at], cot[...], TN).astype(BF16)
-            return 0
-
-        lax.fori_loop(0, hidden // cut, tile, 0)
-        copies = [
-            pltpu.make_async_copy(result.at[kind, pl.ds(place, span)], ref, out_sem.at[index])
-            for ref, kind, place, index in pieces(a_out, b_out)
-        ]
-        for copy in copies:
-            copy.start()
-        for copy in copies:
+        sent = 0
+        for at in range(0, hidden, cut):
+            own = pl.ds(at // span, cut // span)
+            shape = (cut // span, span, wide)
+            result[0, own] = dot(grad[:, at : at + cut], normed[...], TN).astype(BF16).reshape(shape)
+            result[1, own] = dot(act[:, at : at + cut], cot[...], TN).astype(BF16).reshape(shape)
+            done = sum((first + size) * span <= at + cut for first, size in spots)
+            for copy in stores[2 * sent : 2 * done]:
+                copy.start()
+            sent = done
+        for copy in stores:
             copy.wait()
 
 
-def mlp(a_in, b_in, cot, bias, slots, start=None, sums=None):
+def mlp(parts, cot, bias, slots, start=None, sums=None):
     rows, wide = cot.shape
     hidden = bias.shape[1]
+    span = parts[0].shape[2]
     more = sums is not None
     tile = pl.BlockSpec((SLOT, wide), lambda t: (t, 0))
     wide_f32, wide_bf16 = (jax.ShapeDtypeStruct((rows, wide), kind) for kind in (F32, BF16))
-    kept = wide_bf16 if more else wide_f32
-    count = 4 * a_in.shape[0] * a_in.shape[1]
     full = whole(cot.shape)
+    count = len(parts)
     if more:
-        operands = (a_in, b_in, start, cot, bias, *sums)
-        specs = [ANY, ANY, full, full, whole(bias.shape), tile, tile]
+        operands = (*parts, start, cot, bias, *sums)
+        specs = [ANY] * count + [full, full, whole(bias.shape), tile, tile]
     else:
         x_in, one, two, norms = start
-        operands = (a_in, b_in, x_in, one, two, norms, cot, bias)
-        specs = [ANY, ANY, tile, tile, tile, whole(norms.shape), full, whole(bias.shape)]
+        operands = (*parts, x_in, one, two, norms, cot, bias)
+        specs = [ANY] * count + [tile, tile, tile, whole(norms.shape), full, whole(bias.shape)]
     return pl.pallas_call(
-        functools.partial(mlp_kernel, more),
+        functools.partial(mlp_kernel, more, count),
         grid=(slots,),
         in_specs=specs,
-        out_specs=([] if more else [tile, full]) + [tile, tile, ANY, ANY, whole(bias.shape)],
+        out_specs=([] if more else [tile, full])
+        + [tile, tile]
+        + [ANY] * count
+        + [whole(bias.shape)],
         out_shape=([] if more else [wide_f32, wide_bf16])
-        + [
-            kept,
-            kept,
-            jax.ShapeDtypeStruct(a_in.shape, BF16),
-            jax.ShapeDtypeStruct(b_in.shape, BF16),
-            jax.ShapeDtypeStruct(bias.shape, F32),
-        ],
+        + [wide_bf16, wide_bf16]
+        + [jax.ShapeDtypeStruct(v.shape, BF16) for v in parts]
+        + [jax.ShapeDtypeStruct(bias.shape, F32)],
         scratch_shapes=[
-            pltpu.VMEM((2, hidden, wide), BF16),
+            pltpu.VMEM((2, hidden // span, span, wide), BF16),
             pltpu.VMEM((rows, hidden), BF16),
             pltpu.VMEM((rows, hidden), BF16),
-            pltpu.VMEM((2, hidden, wide), BF16),
-            pltpu.SemaphoreType.DMA((count,)),
-            pltpu.SemaphoreType.DMA((count,)),
+            pltpu.VMEM((2, hidden // span, span, wide), BF16),
+            pltpu.SemaphoreType.DMA((2 * count,)),
+            pltpu.SemaphoreType.DMA((2 * count,)),
         ],
         compiler_params=params(),
-        cost_estimate=COST,
+        cost_estimate=cost(17),
         name="mlp",
     )(*operands)
 
@@ -395,50 +419,76 @@
         out_specs=[out] * 2,
         out_shape=[jax.ShapeDtypeStruct(shape, BF16)] * 2,
         compiler_params=params(),
-        cost_estimate=COST,
+        cost_estimate=cost(3.4),
         name="add_second",
     )(a_zero, a_got, b_zero, b_got)
 
 
-def fold_kernel(a_zero, a_got, a_last, b_zero, b_got, b_last, *outs):
+def split_kernel(count, *refs):
+    total = refs[0][...].astype(F32)
+    for ref in refs[1:count]:
+        total = total + ref[...].astype(F32)
+    low = total.astype(BF16)
+    half = low.shape[0] // 2
+    refs[count][...] = low[:half]
+    refs[count + 1][...] = low[half:]
+
+
+def sum_split(values):
+    shape = values[0].shape
+    half = (shape[0] // 2,) + shape[1:]
+    return pl.pallas_call(
+        functools.partial(split_kernel, len(values)),
+        grid=(1,),
+        in_specs=[whole(shape)] * len(values),
+        out_specs=[whole(half)] * 2,
+        out_shape=[jax.ShapeDtypeStruct(half, BF16)] * 2,
+        compiler_params=params(),
+        cost_estimate=cost(2),
+        name="sum_split",
+    )(*values)
+
+
+def fold_kernel(a_zero, a_got, a_last, b_zero, b_got, b_last, keep, send):
+    half = keep.shape[0]
     for part, (zero, got, last_got) in enumerate(((a_zero, a_got, a_last), (b_zero, b_got, b_last))):
-        for k, out in enumerate(outs):
-            total = zero[0, k].astype(F32) + got[0, k].astype(F32) + last_got[k].astype(F32)
-            out[part] = total.astype(BF16)
+        total = zero[0].astype(F32) + got[0].astype(F32) + last_got[...].astype(F32)
+        total = total.astype(BF16)
+        keep[:, part] = total[:half]
+        send[:, part] = total[half:]
 
 
 def fold_first(a_zero, a_got, a_last, b_zero, b_got, b_last):
     shape = a_last.shape
     first = whole((1,) + shape)
-    out = (2,) + shape[1:]
+    out = (shape[0] // 2, 2) + shape[1:]
     return pl.pallas_call(
         fold_kernel,
         grid=(1,),
         in_specs=[first, first, whole(shape)] * 2,
-        out_specs=[whole(out)] * shape[0],
-        out_shape=[jax.ShapeDtypeStruct(out, BF16)] * shape[0],
+        out_specs=[whole(out)] * 2,
+        out_shape=[jax.ShapeDtypeStruct(out, BF16)] * 2,
         compiler_params=params(),
-        cost_estimate=COST,
+        cost_estimate=cost(3),
         name="fold_first",
     )(a_zero, a_got, a_last, b_zero, b_got, b_last)
 
 
-def finish_kernel(middle, one, two, dest_own, dest_halo, own_out, halo_out, total, total_halo):
+def finish_kernel(middle, one, two, dest_own, dest_halo, own_out, halo_out, values):
     step = pl.program_id(0)
-    value = middle[...] + one[...].astype(F32) + two[...].astype(F32)
-    spread_rows(step, value.astype(BF16), dest_own, dest_halo, total, total_halo)
-
-    @pl.when(step == pl.num_programs(0) - 1)
+    value = middle[...] + (one[...].astype(F32) + two[...].astype(F32))
+    values[pl.ds(pl.multiple_of(step * SLOT, 16), SLOT)] = value.astype(BF16)
+    spread_rows(values, dest_own, dest_halo, own_out, halo_out)
+
+
+def spread_rows(values, dest_own, dest_halo, own_out, halo_out):
+    @pl.when(pl.program_id(0) == pl.num_programs(0) - 1)
     def _():
-        own_out[...] = total[...].astype(own_out.dtype)
-        halo_out[...] = total_halo[...].astype(halo_out.dtype)
-
-
-def spread_rows(step, value, dest_own, dest_halo, total, total_halo):
-    for dest, sum_ref in ((dest_own, total), (dest_halo, total_halo)):
-        at = step * SLOT + lax.broadcasted_iota(jnp.int32, (SLOT, dest.shape[1]), 0)
-        part = dot((at == dest[...]).astype(BF16), value, TN)
-        sum_ref[...] = jnp.where(step == 0, part, sum_ref[...] + part)
+        for dest, out in ((dest_own, own_out), (dest_halo, halo_out)):
+            shape = (dest.shape[1], values.shape[0])
+            at = lax.broadcasted_iota(jnp.int32, shape, 1)
+            pick = (at == dest[...].reshape(dest.shape[1], 1)).astype(BF16)
+            out[...] = dot(pick, values[...]).astype(out.dtype)
 
 
 def finish(middle, one, two, dest_own, dest_halo, slots):
@@ -454,23 +504,24 @@
             jax.ShapeDtypeStruct((count, wide), BF16),
             jax.ShapeDtypeStruct((HALO, wide), BF16),
         ],
-        scratch_shapes=[pltpu.VMEM((count, wide), F32), pltpu.VMEM((HALO, wide), F32)],
+        scratch_shapes=[pltpu.VMEM((rows, wide), BF16)],
         compiler_params=params(),
-        cost_estimate=COST,
+        cost_estimate=cost(5),
         name="finish",
     )(middle, one, two, dest_own, dest_halo)
 
 
 def back_kernel(held_count, place, middle, one, two, cot, norms, qkv, prob, *refs):
     held = refs[:held_count]
-    gm_out, gp_out, dq_out, part_out, sums_out, weight, sem = refs[held_count:]
+    gm_out, gp_out, dq_out, part_out, sums_out, weight, scored, sem = refs[held_count:]
     step = pl.program_id(0)
     third = weight.shape[2] // 4
+    copies = weight_copies(place, held, weight, sem)
 
     @pl.when(step == 0)
     def _():
+        load_weight(copies)
         sums_out[...] = jnp.zeros_like(sums_out)
-        load_weight(place, held, weight, sem)
 
     grad = one[...].astype(F32) + two[...].astype(F32)
     hat, inverse = stats(middle[...])
@@ -480,31 +531,44 @@
     gm_out[...] = grad_middle
     grad_proj = grad_middle.astype(BF16)
     gp_out[...] = grad_proj
+    live = lax.broadcasted_iota(jnp.int32, (TAIL, 1), 0) < IMG - (CORE - TAIL)
+    groups, heads = weight.shape[0], third // HEAD
+    pairs = [(group, head) for group in range(groups) for head in range(heads)]
+
+    def part_of(which, group, head):
+        at = which * third + head * HEAD
+        return qkv[group, :CORE, at : at + HEAD]
+
+    grad_atts, grad_cores = [], []
+    for group in range(groups):
+        grad_att = dot(grad_proj, weight[group, :, 3 * third :]).astype(BF16)
+        tail = grad_att[CORE - TAIL : CORE]
+        tail = jnp.where(live, tail, jnp.zeros_like(tail))
+        grad_atts.append(grad_att)
+        grad_cores.append(jnp.concatenate([grad_att[: CORE - TAIL], tail]))
+    grad_heads = [grad_cores[group][:, head * HEAD : (head + 1) * HEAD] for group, head in pairs]
+    grad_probs = [dot(part_of(2, *pair), grad, NT) for pair, grad in zip(pairs, grad_heads)]
+    grads_v = [dot(prob[(0, *pair)], grad) for pair, grad in zip(pairs, grad_heads)]
+    for (group, head), grad_prob in zip(pairs, grad_probs):
+        probs = prob[0, group, head].astype(F32)
+        center = jnp.sum(probs * grad_prob, axis=0, keepdims=True)
+        scored[group * heads + head] = (probs * (grad_prob - center)).astype(BF16)
+    grads_q, grads_k = [], []
+    for group, head in pairs:
+        at = group * heads + head
+        grads_q.append(dot(part_of(1, group, head) * 0.125, scored[at], TN))
+        grads_k.append(dot(scored[at], part_of(0, group, head) * 0.125))
     total = None
-    for group in range(weight.shape[0]):
-        grad_att = dot(grad_proj, weight[group, :, 3 * third :]).astype(BF16)
-        for head in range(third // HEAD):
-            at = head * HEAD
-            queries = qkv[group, :CORE, at : at + HEAD]
-            keys = qkv[group, :CORE, third + at : third + at + HEAD]
-            values = qkv[group, :CORE, 2 * third + at : 2 * third + at + HEAD]
-            grad_head = grad_att[:, at : at + HEAD]
-            grad_core = grad_head[:CORE]
-            probs = prob[0, group, head]
-            probs_wide = probs.astype(F32)
-            grad_probs = dot(grad_core, values, NT)
-            center = jnp.sum(probs_wide * grad_probs, axis=-1, keepdims=True)
-            grad_scores = (probs_wide * (grad_probs - center)).astype(BF16)
-            grad_q = (dot(grad_scores, keys) * 0.125).astype(BF16)
-            grad_k = (dot(grad_scores, queries, TN) * 0.125).astype(BF16)
-            grad_v = dot(probs, grad_core, TN).astype(BF16)
-            blank = jnp.zeros((SLOT - CORE, HEAD), BF16)
-            dq_out[group, :CORE, at : at + HEAD] = grad_q
-            dq_out[group, CORE:, at : at + HEAD] = blank
-            dq_out[group, :CORE, third + at : third + at + HEAD] = grad_k
-            dq_out[group, CORE:, third + at : third + at + HEAD] = blank
-            dq_out[group, :CORE, 2 * third + at : 2 * third + at + HEAD] = grad_v
-            dq_out[group, CORE:, 2 * third + at : 2 * third + at + HEAD] = grad_head[CORE:]
+    for group in range(groups):
+        own = slice(group * heads, (group + 1) * heads)
+        grad_q = jnp.concatenate(grads_q[own]).T.astype(BF16)
+        grad_k = jnp.concatenate(grads_k[own], axis=1).astype(BF16)
+        grad_v = jnp.concatenate(grads_v[own], axis=1).astype(BF16)
+        tail = grad_atts[group][CORE - TAIL : CORE]
+        dq_out[group, :CORE, : 3 * third] = jnp.concatenate([grad_q, grad_k, grad_v], axis=1)
+        dq_out[group, CORE - TAIL : CORE, 2 * third :] = jnp.where(live, grad_v[CORE - TAIL :], tail)
+        dq_out[group, CORE:, : 2 * third] = jnp.zeros((SLOT - CORE, 2 * third), BF16)
+        dq_out[group, CORE:, 2 * third :] = grad_atts[group][CORE:]
         part = dot(dq_out[group], weight[group, :, : 3 * third], NT)
         total = part if total is None else total + part
     part_out[...] = total.astype(BF16)
@@ -539,10 +603,11 @@
         ],
         scratch_shapes=[
             pltpu.VMEM((groups, wide, 4 * third), BF16),
+            pltpu.VMEM((groups * (third // HEAD), CORE, CORE), BF16),
             pltpu.SemaphoreType.DMA((piece_count(held),)),
         ],
         compiler_params=params(),
-        cost_estimate=COST,
+        cost_estimate=cost(19),
         name="back",
     )(place, middle, one, two, cot, norms, qkv, prob, *held)
 
@@ -585,13 +650,13 @@
             pltpu.SemaphoreType.DMA((piece_count(held),)),
         ],
         compiler_params=params(),
-        cost_estimate=COST,
+        cost_estimate=cost(9),
         name="weight_grads",
     )(place, normed, grad_proj, grad_qkv, att)
 
 
 def last_kernel(
-    x_in, gm, one, two, norms, dest_own, dest_halo, own_out, halo_out, prompt_out, sums_out, halo_sum
+    x_in, gm, one, two, norms, dest_own, dest_halo, own_out, halo_out, prompt_out, sums_out, values
 ):
     step = pl.program_id(0)
 
@@ -608,11 +673,8 @@
     prompt_out[...] += grad_in[: prompt_out.shape[0]]
     at = lax.broadcasted_iota(jnp.int32, (SLOT, 1), 0)
     value = jnp.where((at >= 1) & (at <= PROMPTS), 0.0, grad_in).astype(BF16)
-    spread_rows(step, value, dest_own, dest_halo, own_out, halo_sum)
-
-    @pl.when(step == pl.num_programs(0) - 1)
-    def _():
-        halo_out[...] = halo_sum[...].astype(BF16)
+    values[pl.ds(pl.multiple_of(step * SLOT, 16), SLOT)] = value
+    spread_rows(values, dest_own, dest_halo, own_out, halo_out)
 
 
 def last(x_in, gm, one, two, norms, dest_own, dest_halo, slots):
@@ -630,9 +692,9 @@
             jax.ShapeDtypeStruct((56, wide), F32),
             jax.ShapeDtypeStruct((8, wide), F32),
         ],
-        scratch_shapes=[pltpu.VMEM((HALO, wide), F32)],
+        scratch_shapes=[pltpu.VMEM((rows, wide), BF16)],
         compiler_params=params(),
-        cost_estimate=COST,
+        cost_estimate=cost(7),
         name="last",
     )(x_in, gm, one, two, norms, dest_own, dest_halo)
 
@@ -664,19 +726,19 @@
     def by_core(self, value):
         return self.send(value, lambda z, x, y, c: (z, x, y, 1 - c))
 
-    def by_z(self, value, shift):
-        return self.send(value, lambda z, x, y, c: ((z + shift) % self.deep, x, y, c))
-
-    def gather_z(self, value):
-        return [value] + [self.by_z(value, k) for k in range(1, self.deep)]
-
-    def scatter_z(self, values, earlier):
-        got = [self.by_z(values[k], self.deep - k) for k in range(1, self.deep)]
-        got = tie(*got, earlier)[:-1]
-        total = values[0].astype(F32)
-        for item in got:
-            total = total + item.astype(F32)
-        return total
+    def by_z(self, value, bit):
+        return self.send(value, lambda z, x, y, c: (z ^ bit, x, y, c))
+
+    def gather_z(self, value, axis, *between):
+        first = None
+        bit = self.deep // 2
+        while bit:
+            got = self.by_z(value, bit)
+            if first is None:
+                got = first = after(got, *between)
+            value = jnp.concatenate([value, got], axis=axis)
+            bit //= 2
+        return value, first
 
     def spread(self, first, second):
         a_next, b_next = tie(self.by_y(first), self.by_x(second))
@@ -687,17 +749,40 @@
     def spread_more(self, a_zero, b_zero):
         return self.by_x(a_zero), self.by_y(b_zero)
 
+    def fold_z(self, keep, got):
+        bit, first = 2, got
+        while bit < self.deep:
+            keep, send = sum_split([keep, got])
+            got = self.by_z(send, bit)
+            first = send if bit == 2 else first
+            bit *= 2
+        return keep, got, first
+
     def to_absolute(self, blocks, z_axis, x_axis):
-        size = self.deep
-        turned = jnp.take(blocks, jnp.asarray([-m % size for m in range(size)]), axis=z_axis)
-        turned = jnp.roll(turned, self.z, axis=z_axis)
-        return jnp.where(self.x == 0, turned, jnp.flip(turned, axis=x_axis))
+        return self.turn(jnp.where(self.x == 0, blocks, jnp.flip(blocks, axis=x_axis)), z_axis, False)
 
     def to_relative(self, blocks, z_axis, x_axis):
-        size = self.deep
-        turned = jnp.where(self.x == 0, blocks, jnp.flip(blocks, axis=x_axis))
-        turned = jnp.roll(turned, -self.z, axis=z_axis)
-        return jnp.take(turned, jnp.asarray([-m % size for m in range(size)]), axis=z_axis)
+        return self.turn(jnp.where(self.x == 0, blocks, jnp.flip(blocks, axis=x_axis)), z_axis, True)
+
+    def turn(self, blocks, z_axis, back):
+        shape = blocks.shape
+        bits = self.deep.bit_length() - 1
+        blocks = blocks.reshape(shape[:z_axis] + (2,) * bits + shape[z_axis + 1 :])
+        order = list(range(blocks.ndim))
+        order[z_axis : z_axis + bits] = order[z_axis : z_axis + bits][::-1]
+        if back:
+            blocks = blocks.transpose(order)
+        for i in range(bits):
+            flipped = jnp.flip(blocks, axis=z_axis + i)
+            blocks = jnp.where((self.z >> i) & 1 == 0, blocks, flipped)
+        if not back:
+            blocks = blocks.transpose(order)
+        return blocks.reshape(shape)
+
+
+def exchange(value, send):
+    low = value.astype(BF16)
+    return low.astype(F32) + send(low).astype(F32)
 
 
 def tie(*values):
@@ -742,13 +827,19 @@
     third = qkv_weight.shape[2]
     shard = jnp.concatenate(
         [qkv_weight.reshape(depth, 3 * third), out_weight.swapaxes(0, 1)], axis=1
-    ).reshape(2, depth // 2, 4 * third)
+    ).reshape(2, 1, depth // 2, 4 * third)
+
     hidden = up_weight.shape[1]
     span = hidden // 2
-    bias = jnp.stack(grid.gather_z(up_bias.reshape(2, span)))
+    halves = jnp.stack(
+        [up_weight.swapaxes(0, 1).reshape(2, span, wide), down_weight.reshape(2, span, wide)],
+        axis=1,
+    )
+    bias, first = grid.gather_z(up_bias.reshape(1, hidden), 0)
+    shard = after(shard, first)
+    got, first = grid.gather_z(shard, 1, bias)
     bias = jnp.stack([bias, grid.by_x(bias)])
     bias = jnp.stack([bias, grid.by_y(bias)])
-    *got, bias = tie(*grid.gather_z(shard), bias)
 
     code = ((segment % IMGS_ROW) * 2 + live_token).astype(BF16)
     marks = jnp.pad(code[None], ((0, 15), (0, wide - count)))
@@ -771,23 +862,17 @@
     edge = jnp.concatenate(edge_parts)
     halo = grid.by_y(edge)
 
-    a_zero, b_zero = grid.spread(jnp.stack([g[0] for g in got]), jnp.stack([g[1] for g in got]))
-    a_zero, b_zero, _ = tie(a_zero, b_zero, edge)
+    got, bias, halo = tie(got, bias, halo)
+    a_zero, b_zero = grid.spread(got[0], got[1])
     a_one, b_one = grid.spread_more(a_zero, b_zero)
     x_in, normed, cot, dest_own, dest_halo = prep(place, own, other, halo, prompts, norms, slots)
 
-    shard = jnp.stack(
-        [up_weight.swapaxes(0, 1).reshape(2, span, wide), down_weight.reshape(2, span, wide)],
-        axis=1,
-    )
-    shard = after(shard, got[0])
-    held = tie(*grid.gather_z(shard), normed)[:deep]
-    mlp_a = jnp.stack([h[0] for h in held])
-    mlp_b = jnp.stack([h[1] for h in held])
+    held, _ = grid.gather_z(after(halves, first)[:, None], 1, normed)
+    mlp_a, mlp_b = held[0], held[1]
     mlp_a0, mlp_b0 = grid.spread(mlp_a, mlp_b)
     mlp_a1, mlp_b1 = grid.spread_more(mlp_a0, mlp_b0)
-    bias_a = jnp.stack([bias[0, 0, :, 0], bias[1, 0, :, 0], bias[0, 0, :, 1], bias[0, 1, :, 1]])
-    bias_b = jnp.stack([bias[0, 1, :, 0], bias[1, 1, :, 0], bias[1, 0, :, 1], bias[1, 1, :, 1]])
+    bias_a = jnp.stack([bias[:, 0, :, :span], bias[0, :, :, span:]])
+    bias_b = jnp.stack([bias[:, 1, :, :span], bias[1, :, :, span:]])
 
     weights = [a_zero, a_one, b_zero, b_one]
     if (depth // 2) % 16:
@@ -805,31 +890,38 @@
     fine = span % 16 == 0
 
     def enter(value):
+        value = value.reshape(-1, 2, span, wide)
         if fine:
             return value
-        return value.swapaxes(1, 2).reshape(2, 1, 2, deep * span, wide)
+        return value.swapaxes(0, 1).reshape(2, -1, 48, wide).swapaxes(0, 1)
 
     def leave(value):
         if fine:
             return value
-        return value.reshape(2, 2, deep, span, wide).swapaxes(1, 2)
+        return value.swapaxes(0, 1).reshape(2, -1, span, wide).swapaxes(0, 1)
 
     start = (x_in, part, grid.by_core(part), norms)
-    middle, normed_two, o_sum, g_sum, grad_a0, grad_b0, grad_bias_a = mlp(
-        enter(mlp_a0), enter(mlp_b0), cot, row_of(bias_a), slots, start
+    middle, normed_two, o_sum, g_sum, *grads, grad_bias_a = mlp(
+        [enter(mlp_a0), enter(mlp_b0)], cot, row_of(bias_a), slots, start
     )
-    o_part, g_part, grad_a1, grad_b1, grad_bias_b = mlp(
-        enter(mlp_a1), enter(mlp_b1), cot, row_of(bias_b), slots, normed_two, (o_sum, g_sum)
+    grad_a0, grad_b0 = [leave(v).reshape(2, deep, 2, span, wide) for v in grads]
+    o_part, g_part, *grads, grad_bias_b = mlp(
+        [enter(mlp_a1), enter(mlp_b1)],
+        cot,
+        row_of(bias_b),
+        slots,
+        normed_two,
+        (o_sum, g_sum),
     )
-    grad_a0, grad_b0 = leave(grad_a0), leave(grad_b0)
-    a_got, b_got = grid.by_x(leave(grad_a1)), grid.by_y(leave(grad_b1))
+    grad_a1, grad_b1 = [leave(v).reshape(2, deep, 2, span, wide) for v in grads]
+    a_got, b_got = grid.by_x(grad_a1), grid.by_y(grad_b1)
     g_other = grid.by_core(g_part)
-    o_other = grid.by_core(after(o_part, g_other))
 
     grad_middle, grad_proj, grad_qkv, g_one, sums_two = back(
         place, middle, g_part, g_other, cot, norms, weights, qkv, prob, slots
     )
     g_one_other = grid.by_core(g_one)
+    o_other = grid.by_core(after(o_part, g_one))
     a_got, b_got, _ = tie(a_got, b_got, g_one)
     a_send, b_send = add_second(grad_a0, a_got, grad_b0, b_got)
     a_last, b_last = grid.by_y(a_send), grid.by_x(b_send)
@@ -848,26 +940,47 @@
         ]
     att_a0, att_a1, att_b0, att_b1 = weight_blocks
     att_a_got, att_b_got = grid.by_x(att_a1), grid.by_y(att_b1)
-    a_last, b_last, _ = tie(a_last, b_last, att_a1)
-    pieces = fold_first(grad_a0, a_got, a_last, grad_b0, b_got, b_last)
-
-    att_a_got, att_b_got, _ = tie(att_a_got, att_b_got, pieces[0])
+    a_last, b_last, o_other, g_one_other, _ = tie(a_last, b_last, o_other, g_one_other, att_a1)
+    grad_keep, grad_send = fold_first(grad_a0, a_got, a_last, grad_b0, b_got, b_last)
+    grad_got = grid.by_z(grad_send, 1)
+
+    tok_own, tok_halo, prompt_sum, sums_one = last(
+        x_in, grad_middle, g_one, after(g_one_other, grad_send), norms, dest_own, dest_halo, slots
+    )
+    tok_edge = grid.by_y(tok_halo)
+
+    g_a = grad_bias_a.reshape(2, 2, deep, span)
+    g_b = grad_bias_b.reshape(2, 2, deep, span)
+    bias_blocks = jnp.stack(
+        [jnp.stack([g_a[0], g_b[0]], axis=1), jnp.stack([g_a[1], g_b[1]], axis=0)], axis=3
+    )
+    bias_blocks = grid.to_absolute(bias_blocks, 2, 1)
+    bias_blocks = jnp.where(grid.y == 0, bias_blocks, jnp.flip(bias_blocks, axis=0))
+    small = jnp.concatenate(
+        [prompt_sum, sums_one[:2], sums_two[:2], bias_blocks.reshape(-1, wide)]
+    )
+    small = exchange(small, grid.by_x)
+    att_a_got, att_b_got, _ = tie(att_a_got, att_b_got, tok_halo)
     a_send, b_send = add_second(att_a0, att_a_got, att_b0, att_b_got)
     att_a_last, att_b_last = grid.by_y(a_send), grid.by_x(b_send)
-    tok_own, tok_halo, prompt_sum, sums_one = last(
-        x_in, grad_middle, g_one, after(g_one_other, a_send), norms, dest_own, dest_halo, slots
-    )
-    tok_edge = grid.by_y(tok_halo)
-    att_a_last, att_b_last, _ = tie(att_a_last, att_b_last, tok_halo)
-    att_pieces = fold_first(att_a0, att_a_got, att_a_last, att_b0, att_b_got, att_b_last)
+    grad_got, small, _ = tie(grad_got, small, a_send)
+    grad_keep, grad_got, grad_send = grid.fold_z(grad_keep, grad_got)
+    small = exchange(small, grid.by_y)
     out_own, out_halo = finish(
-        middle, o_part, after(o_other, att_pieces[0]), dest_own, dest_halo, slots
+        middle, o_part, after(o_other, grad_send), dest_own, dest_halo, slots
     )
     out_edge = grid.by_y(out_halo)
-    grad_shard = grid.scatter_z(pieces, out_halo)
+    att_a_last, att_b_last, small, _ = tie(att_a_last, att_b_last, small, out_halo)
+    att_keep, att_send = fold_first(att_a0, att_a_got, att_a_last, att_b0, att_b_got, att_b_last)
+    att_got = grid.by_z(att_send, 1)
+    small = exchange(small, lambda v: grid.by_z(v, 1))
+    att_got, small = tie(att_got, small)
+    att_keep, att_got, _ = grid.fold_z(att_keep, att_got)
+    grad_got = after(grad_got, att_keep)
+    grad_shard = (grad_keep.astype(F32) + grad_got.astype(F32))[0]
     grad_up = grad_shard[:, 0].reshape(hidden, wide).swapaxes(0, 1)
     grad_down = grad_shard[:, 1].reshape(hidden, wide)
-    att_shard = grid.scatter_z(att_pieces, out_halo)
+    att_shard = att_keep.astype(F32) + att_got.astype(F32)
     att_shard = att_shard.reshape(depth, 4 * third)
     grad_qkv_weight = att_shard[:, : 3 * third].reshape(depth, 3, third)
     grad_out_weight = att_shard[:, 3 * third :].swapaxes(0, 1)
@@ -879,26 +992,9 @@
         value = value.at[count - HALO :].add(ends)
         return value.at[:HALO].add(begins)
 
-    g_a = grad_bias_a.reshape(4, deep, span)
-    g_b = grad_bias_b.reshape(4, deep, span)
-    bias_blocks = jnp.stack(
-        [
-            jnp.stack([jnp.stack([g_a[0], g_a[2]], 1), jnp.stack([g_b[0], g_a[3]], 1)]),
-            jnp.stack([jnp.stack([g_a[1], g_b[2]], 1), jnp.stack([g_b[1], g_b[3]], 1)]),
-        ]
-    )
-    bias_blocks = grid.to_absolute(bias_blocks, 2, 1)
-    bias_blocks = jnp.where(grid.y == 0, bias_blocks, jnp.flip(bias_blocks, axis=0))
-    small = jnp.concatenate(
-        [prompt_sum, sums_one[:2], sums_two[:2], bias_blocks.reshape(-1, wide)]
-    )
-    small = small + grid.by_x(small)
-    small = small + grid.by_y(small)
-    stride = 1
+    stride = 2
     while stride < deep:
-        small = small + grid.send(
-            small, lambda z, x, y, c, stride=stride: (z ^ stride, x, y, c)
-        )
+        small = exchange(small, lambda v, stride=stride: grid.by_z(v, stride))
         stride *= 2
     bias_all = small[60:].reshape(2, 2, deep, hidden)
     grad_bias = lax.dynamic_slice(

time: 264 us -> 242 us (0.917)
  starting transfers between devices: 55.5 us -> 41.6 us
  Pallas kernels: 123 us -> 115 us
  local copies, waits for them, and re-layouts: 21.9 us -> 16.3 us
  waiting for transfers between devices: 49.4 us -> 53 us
    ppermute x45 -> x40, starting transfers between devices: 55.5 us -> 41.6 us  [send(): return lax.ppermute(value, AXES, pairs)]
    pallas_call x1, Pallas kernels: 23.1 us -> 18.9 us  [back(): pl.pallas_call(functools.partial(back_kernel, len(held)), grid=(slots,),...]
    ppermute x45 -> x40, waiting for transfers between devices: 49.4 us -> 53 us  [send(): return lax.ppermute(value, AXES, pairs)]
    pallas_call x1, Pallas kernels: 16.3 us -> 12.8 us  [attend(): pl.pallas_call(functools.partial(attend_kernel, len(held)), grid=(slots,)...]
    another operation x4, local copies, waits for them, and re-layouts: 2.74 us -> 0.02 us  [local(): norms = jnp.stack([attn_gain, attn_shift, mlp_gain, mlp_shift]).astype(F32)]
    pallas_call x2 -> x4, Pallas kernels: 38.1 us -> 38 us  [the longest x2 34.1 us: mlp(): pl.pallas_call(functools.partial(mlp_kernel, more, count), grid=(slots,),...]
    unnamed x72 -> x68, local copies, waits for them, and re-layouts: 8.66 us -> 8.64 us
  transfers between devices with their start and end apart: 45 -> 40, of which waited for: 18 -> 18; matrix products, arithmetic and copies ran while one was open for 10% -> 9% of each run, Pallas kernels for 40% -> 41%
where the time goes in v3:
time: 242 us; the launch traced here: 241 us
  Pallas kernels  115 us (48%)
  waiting for transfers between devices  53 us (22%)
  starting transfers between devices  41.6 us (17%)
  local copies, waits for them, and re-layouts  16.3 us (7%)
  other arithmetic  13.8 us (6%)
    ppermute x40, waiting for transfers between devices, send(): return lax.ppermute(value, AXES, pairs)  53 us
    ppermute x40, starting transfers between devices, send(): return lax.ppermute(value, AXES, pairs)  41.6 us
    pallas_call x2, Pallas kernels, mlp(): pl.pallas_call(functools.partial(mlp_kernel, more, count), grid=(slots,),...  34.1 us
    pallas_call x1, Pallas kernels, back(): pl.pallas_call(functools.partial(back_kernel, len(held)), grid=(slots,),...  18.9 us
    pallas_call x1, Pallas kernels, attend(): pl.pallas_call(functools.partial(attend_kernel, len(held)), grid=(slots,)...  12.8 us
    pallas_call x1, Pallas kernels, prep(): pl.pallas_call(prep_kernel, grid=(slots,), in_specs=[SMEM] + [whole(v.sha...  9.45 us
    pallas_call x1, Pallas kernels, weight_grads(): pl.pallas_call(functools.partial(weight_kernel, len(held)), grid=(wide //...  8.95 us
    unnamed x68, local copies, waits for them, and re-layouts  8.64 us
  transfers between devices with their start and end apart: 40, of which 18 were waited for; matrix products, arithmetic and copies ran while one was open for 9% of the time, Pallas kernels for 41%

profile of v3, /device:TPU:0, one launch (start us, length us, event | category | flops | bytes accessed | tf_op | source)
XLA Modules:
  0.0 241.1 jit_solution(5621250688309744686)
XLA Ops:
  0.6 4.1 %collective-permute-start = (bf16[1,96]{1,0:T(2,128)(2,1)}, bf16[1,96]{1,0:T(2,128)(2,1)S(1)}, u32[]{:S(2)}, u32[]{:S(2)}) collective-permute-start(bf16[1,96]{1,0:T(2,128)(2,1)} %bitcast.96), channel_id=1, source_target_pairs={{0,16},{1,17},{2,18},{3,19},{4,20},{5,21},{6,22},{7,23},{8,24},{9,... | collective-permute-start | bytes 584 | tf_op jit(solution)/shard_map/ppermute | solution.py:718
  19.9 2.5 %collective-permute-done.1 = bf16[2,1,48,768]{3,2,1,0:T(8,128)(2,1)S(1)} collective-permute-done((bf16[2,1,48,768]{3,2,1,0:T(8,128)(2,1)S(1)}, bf16[2,1,48,768]{3,2,1,0:T(8,128)(2,1)S(1)}, u32[]{:S(2)}, u32[]{:S(2)}) %collective-permute-start.1) | collective-permute-done | bytes 147488 | tf_op jit(solution)/shard_map/ppermute | solution.py:718
  26.9 5.8 %collective-permute-done.5 = bf16[2,2,48,768]{3,2,1,0:T(8,128)(2,1)S(1)} collective-permute-done((bf16[2,2,48,768]{3,2,1,0:T(8,128)(2,1)S(1)}, bf16[2,2,48,768]{3,2,1,0:T(8,128)(2,1)S(1)}, u32[]{:S(2)}, u32[]{:S(2)}) %collective-permute-start.5) | collective-permute-done | bytes 294944 | tf_op jit(solution)/shard_map/ppermute | solution.py:718
  32.9 2.6 %collective-permute-start.12 = (bf16[4,48,768]{2,1,0:T(8,128)(2,1)S(1)}, bf16[4,48,768]{2,1,0:T(8,128)(2,1)S(1)}, u32[]{:S(2)}, u32[]{:S(2)}) collective-permute-start(bf16[4,48,768]{2,1,0:T(8,128)(2,1)S(1)} %get-tuple-element.249), channel_id=1, source_target_pairs={{0,2},{1,3},{2,0},{3,1},{4,6},{5,7},{6,4},{7,5},{8,10},{9,11},{10,... | collective-permute-start | bytes 884744 | tf_op jit(solution)/shard_map/ppermute | solution.py:718
  36.9 9.4 %prep.1 = (bf16[1088,768]{1,0:T(8,128)(2,1)}, bf16[1088,768]{1,0:T(8,128)(2,1)}, bf16[1088,768]{1,0:T(8,128)(2,1)}, s32[1,512]{1,0:T(1,128)}, s32[1,48]{1,0:T(1,128)}) custom-call(s32[4]{0:T(128)} %pad_add_fusion.place, bf16[1040,768]{1,0:T(8,128)(2,1)} %copy-done.6, bf16[1040,768]{1,0:T(8,128)(2,1)} %collective-permute-done.4.other, ...), custom_call_target="tpu_custom_call" | custom-call | flops 1380000000 | bytes 1 | tf_op jit(solution)/shard_map/prep/pallas_call | solution.py:151
  47.4 12.9 %collective-permute-done.9 = bf16[2,2,2,48,768]{4,3,2,1,0:T(8,128)(2,1)S(1)} collective-permute-done((bf16[2,2,2,48,768]{4,3,2,1,0:T(8,128)(2,1)S(1)}, bf16[2,2,2,48,768]{4,3,2,1,0:T(8,128)(2,1)S(1)}, u32[]{:S(2)}, u32[]{:S(2)}) %collective-permute-start.9) | collective-permute-done | bytes 589856 | tf_op jit(solution)/shard_map/ppermute | solution.py:718
  63.5 12.8 %attend.1 = (bf16[2,1088,576]{2,1,0:T(8,128)(2,1)}, bf16[4,2,3,256,256]{4,3,2,1,0:T(8,128)(2,1)}, bf16[2,1088,192]{2,1,0:T(8,128)(2,1)}, bf16[1088,768]{1,0:T(8,128)(2,1)}) custom-call(s32[4]{0:T(128)} %pad_add_fusion.place, bf16[1088,768]{1,0:T(8,128)(2,1)} %get-tuple-element.174.normed, bf16[2,4,48,768]{3,2,1,0:T(8,128)(2,1)} %copy-done.3, ...), custom_call_target="tpu_custom_call" | custom-call | flops 2242500096 | bytes 1 | tf_op jit(solution)/shard_map/attend/pallas_call | solution.py:257
  81.3 17.8 %mlp.2 = (f32[1088,768]{1,0:T(8,128)}, bf16[1088,768]{1,0:T(8,128)(2,1)}, bf16[1088,768]{1,0:T(8,128)(2,1)}, bf16[1088,768]{1,0:T(8,128)(2,1)}, bf16[8,2,48,768]...) custom-call(bf16[8,2,48,768]{3,2,1,0:T(8,128)(2,1)} %bitcast.78, ...), custom_call_target="tpu_custom_call" | custom-call | flops 2932499968 | bytes 1 | tf_op jit(solution)/shard_map/mlp/pallas_call | solution.py:380
  99.1 5.9 %collective-permute-done.18 = bf16[2,4,2,48,768]{4,3,2,1,0:T(8,128)(2,1)S(1)} collective-permute-done((bf16[2,4,2,48,768]{4,3,2,1,0:T(8,128)(2,1)S(1)}, bf16[2,4,2,48,768]{4,3,2,1,0:T(8,128)(2,1)S(1)}, u32[]{:S(2)}, u32[]{:S(2)}) %collective-permute-start.18) | collective-permute-done | bytes 1179680 | tf_op jit(solution)/shard_map/ppermute | solution.py:718
  106.5 16.3 %mlp.3 = (bf16[1088,768]{1,0:T(8,128)(2,1)}, bf16[1088,768]{1,0:T(8,128)(2,1)}, bf16[8,2,48,768]{3,2,1,0:T(8,128)(2,1)}, bf16[8,2,48,768]{3,2,1,0:T(8,128)(2,1)}, f32[1,768]{1,0:T(1,128)}) custom-call(bf16[8,2,48,768]{3,2,1,0:T(8,128)(2,1)} %bitcast.29.refs_0_, bf16[8,2,48,768]{3,2,1,0:T(8,128)(2,1)} %bitcast.104, ...), custom_call_target="tpu_custom_call" | custom-call | flops 2932499968 | bytes 1 | tf_op jit(solution)/shard_map/mlp/pallas_call | solution.py:380
  127.9 18.9 %back.1 = (f32[1088,768]{1,0:T(8,128)}, bf16[1088,768]{1,0:T(8,128)(2,1)}, bf16[2,1088,576]{2,1,0:T(8,128)(2,1)}, bf16[1088,768]{1,0:T(8,128)(2,1)}, f32[8,768]{1,0:T(8,128)}) custom-call(s32[4]{0:T(128)} %pad_add_fusion.place, f32[1088,768]{1,0:T(8,128)} %get-tuple-element.156.middle, bf16[1088,768]{1,0:T(8,128)(2,1)} %get-tuple-element.164.one, ...), custom_call_target="tpu_custom_call" | custom-call | flops 3277499904 | bytes 1 | tf_op jit(solution)/shard_map/back/pallas_call | solution.py:582
  147.8 3.7 %collective-permute-done.20.b_got = bf16[2,4,2,48,768]{4,3,2,1,0:T(8,128)(2,1)S(1)} collective-permute-done((bf16[2,4,2,48,768]{4,3,2,1,0:T(8,128)(2,1)}, bf16[2,4,2,48,768]{4,3,2,1,0:T(8,128)(2,1)S(1)}, u32[]{:S(2)}, u32[]{:S(2)}) %collective-permute-start.20) | collective-permute-done | bytes 1179680 | tf_op jit(solution)/shard_map/ppermute | solution.py:718
  153.0 3.7 %add_second.2 = (bf16[4,2,48,768]{3,2,1,0:T(8,128)(2,1)}, bf16[4,2,48,768]{3,2,1,0:T(8,128)(2,1)}) custom-call(bf16[2,4,2,48,768]{4,3,2,1,0:T(8,128)(2,1)} %bitcast.68, bf16[2,4,2,48,768]{4,3,2,1,0:T(8,128)(2,1)} %copy-done.1, bf16[2,4,2,48,768]{4,3,2,1,0:T(8,128)(2,1)} %bitcast.70, bf16[2,4,2,48,768]{4,3,2,1,0:T(8,128)(2,1)} %copy-done), custom_call_target="tpu_custom_call" | custom-call | flops 586499968 | bytes 1 | tf_op jit(solution)/shard_map/add_second/pallas_call | solution.py:415
  159.6 9.0 %weight_grads.1 = (bf16[2,4,48,768]{3,2,1,0:T(8,128)(2,1)}, bf16[2,4,48,768]{3,2,1,0:T(8,128)(2,1)}, bf16[2,4,48,768]{3,2,1,0:T(8,128)(2,1)}, bf16[2,4,48,768]{3,2,1,0:T(8,128)(2,1)}) custom-call(s32[4]{0:T(128)} %pad_add_fusion.place, bf16[1088,768]{1,0:T(8,128)(2,1)} %get-tuple-element.174.normed, bf16[1088,768]{1,0:T(8,128)(2,1)} %get-tuple-element.175.grad_proj, ...), custom_call_target="tpu_custom_call" | custom-call | flops 1552499968 | bytes 1 | tf_op jit(solution)/shard_map/weight_grads/pallas_call | solution.py:642
  169.4 2.3 collective-permute-done.23.b_last
  175.7 3.3 %fold_first.2 = (bf16[2,2,2,48,768]{4,3,2,1,0:T(8,128)(2,1)}, bf16[2,2,2,48,768]{4,3,2,1,0:T(8,128)(2,1)}) custom-call(bf16[2,4,2,48,768]{4,3,2,1,0:T(8,128)(2,1)} %bitcast.69, bf16[2,4,2,48,768]{4,3,2,1,0:T(8,128)(2,1)} %copy-done.1, bf16[4,2,48,768]{3,2,1,0:T(8,128)(2,1)} %copy-done.13, bf16[2,4,2,48,768]{4,3,2,1,0:T(8,128)(2,1)} %bitcast.71, ...), custom_call_target="tpu_custom_call" | custom-call | flops 517500000 | bytes 1 | tf_op jit(solution)/shard_map/fold_first/pallas_call | solution.py:465
  179.3 8.1 %last.1 = (f32[512,768]{1,0:T(8,128)}, bf16[48,768]{1,0:T(8,128)(2,1)}, f32[56,768]{1,0:T(8,128)}, f32[8,768]{1,0:T(8,128)}) custom-call(bf16[1088,768]{1,0:T(8,128)(2,1)} %get-tuple-element.149.refs_2_.x_in, f32[1088,768]{1,0:T(8,128)} %get-tuple-element.184.gm, bf16[1088,768]{1,0:T(8,128)(2,1)} %get-tuple-element.167.one, ...), custom_call_target="tpu_custom_call" | custom-call | flops 1207500032 | bytes 1 | tf_op jit(solution)/shard_map/last/pallas_call | solution.py:684
  191.4 3.4 %add_second.3 = (bf16[4,48,768]{2,1,0:T(8,128)(2,1)}, bf16[4,48,768]{2,1,0:T(8,128)(2,1)}) custom-call(bf16[2,4,48,768]{3,2,1,0:T(8,128)(2,1)} %get-tuple-element.194.a_zero, bf16[2,4,48,768]{3,2,1,0:T(8,128)(2,1)} %copy-done.5, bf16[2,4,48,768]{3,2,1,0:T(8,128)(2,1)} %get-tuple-element.198.b_zero, bf16[2,4,48,768]{3,2,1,0:T(8,128)(2,1)} %copy-done.4), custom_call_target="tpu_custom_call" | custom-call | flops 586499968 | bytes 1 | tf_op jit(solution)/shard_map/add_second/pallas_call | solution.py:415
  199.1 2.1 sum_split.2
  201.3 6.1 %finish.1 = (bf16[512,768]{1,0:T(8,128)(2,1)}, bf16[48,768]{1,0:T(8,128)(2,1)}) custom-call(f32[1088,768]{1,0:T(8,128)} %get-tuple-element.156.middle, bf16[1088,768]{1,0:T(8,128)(2,1)} %get-tuple-element.173.one, bf16[1088,768]{1,0:T(8,128)(2,1)} %collective-permute-done.24.two, s32[1,512]{1,0:T(1,128)} %get-tuple-element.187.dest_own, ...), custom_call_target="tpu_custom_call" | custom-call | flops 862499968 | bytes 1 | tf_op jit(solution)/shard_map/finish/pallas_call | solution.py:498
  216.7 2.4 fold_first.3
  223.2 3.1 %collective-permute-done.35.refs_1_ = bf16[2,2,48,768]{3,2,1,0:T(8,128)(2,1)S(1)} collective-permute-done((bf16[2,2,48,768]{3,2,1,0:T(8,128)(2,1)}, bf16[2,2,48,768]{3,2,1,0:T(8,128)(2,1)S(1)}, u32[]{:S(2)}, u32[]{:S(2)}) %collective-permute-start.35) | collective-permute-done | bytes 294944 | tf_op jit(solution)/shard_map/ppermute | solution.py:718
  226.3 2.6 %collective-permute-start.37 = (bf16[62,768]{1,0:T(8,128)(2,1)S(1)}, bf16[62,768]{1,0:T(8,128)(2,1)S(1)}, u32[]{:S(2)}, u32[]{:S(2)}) collective-permute-start(bf16[62,768]{1,0:T(8,128)(2,1)S(1)} %convert_add_fusion.2), channel_id=1, source_target_pairs={{0,16},{1,17},{2,18},{3,19},{4,20},{5,21},{6,22},{7,23},{8,24},{9,... | collective-permute-start | bytes 285704 | tf_op jit(solution)/shard_map/ppermute | solution.py:718
  235.3 3.9 %collective-permute-done.38 = bf16[1,2,48,768]{3,2,1,0:T(8,128)(2,1)S(1)} collective-permute-done((bf16[1,2,48,768]{3,2,1,0:T(8,128)(2,1)}, bf16[1,2,48,768]{3,2,1,0:T(8,128)(2,1)S(1)}, u32[]{:S(2)}, u32[]{:S(2)}) %collective-permute-start.38) | collective-permute-done | bytes 147488 | tf_op jit(solution)/shard_map/ppermute | solution.py:718
  (212 shorter events, 77.0 us)
Async XLA Ops:
  9.3 13.2 %collective-permute-start.4 = (bf16[1040,768]{1,0:T(8,128)(2,1)S(1)}, bf16[1040,768]{1,0:T(8,128)(2,1)}, u32[]{:S(2)}, u32[]{:S(2)}) collective-permute-start(bf16[1040,768]{1,0:T(8,128)(2,1)S(1)} %fusion.1.own), channel_id=1, source_target_pairs={{0,1},{1,0},{2,3},{3,2},{4,5},{5,4},{6,7},{7,6},{8,9},{9,8},{10,11... | collective-permute-start | bytes 4792328 | tf_op jit(solution)/shard_map/ppermute | solution.py:718
  22.4 10.2 %collective-permute-start.5 = (bf16[2,2,48,768]{3,2,1,0:T(8,128)(2,1)S(1)}, bf16[2,2,48,768]{3,2,1,0:T(8,128)(2,1)S(1)}, u32[]{:S(2)}, u32[]{:S(2)}) collective-permute-start(bf16[2,2,48,768]{3,2,1,0:T(8,128)(2,1)S(1)} %pad_maximum_fusion.8), channel_id=1, source_target_pairs={{0,8},{1,9},{2,10},{3,11},{4,12},{5,13},{6,14},{7,15},{8,0},{9,1},... | collective-permute-start | bytes 884744 | tf_op jit(solution)/shard_map/ppermute | solution.py:718
  25.9 20.5 %collective-permute-start.3 = (bf16[2,1,2,48,768]{4,3,2,1,0:T(8,128)(2,1)S(1)}, bf16[2,1,2,48,768]{4,3,2,1,0:T(8,128)(2,1)S(1)}, u32[]{:S(2)}, u32[]{:S(2)}) collective-permute-start(bf16[2,1,2,48,768]{4,3,2,1,0:T(8,128)(2,1)S(1)} %bitcast.72), channel_id=1, source_target_pairs={{0,16},{1,17},{2,18},{3,19},{4,20},{5,21},{6,22},{7,23},{8,24},{9,... | collective-permute-start | bytes 884744 | tf_op jit(solution)/shard_map/ppermute | solution.py:718
  32.9 13.7 %collective-permute-start.12 = (bf16[4,48,768]{2,1,0:T(8,128)(2,1)S(1)}, bf16[4,48,768]{2,1,0:T(8,128)(2,1)S(1)}, u32[]{:S(2)}, u32[]{:S(2)}) collective-permute-start(bf16[4,48,768]{2,1,0:T(8,128)(2,1)S(1)} %get-tuple-element.249), channel_id=1, source_target_pairs={{0,2},{1,3},{2,0},{3,1},{4,6},{5,7},{6,4},{7,5},{8,10},{9,11},{10,... | collective-permute-start | bytes 884744 | tf_op jit(solution)/shard_map/ppermute | solution.py:718
  35.5 11.1 %collective-permute-start.13 = (bf16[4,48,768]{2,1,0:T(8,128)(2,1)S(1)}, bf16[4,48,768]{2,1,0:T(8,128)(2,1)S(1)}, u32[]{:S(2)}, u32[]{:S(2)}) collective-permute-start(bf16[4,48,768]{2,1,0:T(8,128)(2,1)S(1)} %get-tuple-element.250), channel_id=1, source_target_pairs={{0,4},{1,5},{2,6},{3,7},{4,0},{5,1},{6,2},{7,3},{8,12},{9,13},{10,... | collective-permute-start | bytes 884744 | tf_op jit(solution)/shard_map/ppermute | solution.py:718
  46.5 13.9 %collective-permute-start.9 = (bf16[2,2,2,48,768]{4,3,2,1,0:T(8,128)(2,1)S(1)}, bf16[2,2,2,48,768]{4,3,2,1,0:T(8,128)(2,1)S(1)}, u32[]{:S(2)}, u32[]{:S(2)}) collective-permute-start(bf16[2,2,2,48,768]{4,3,2,1,0:T(8,128)(2,1)S(1)} %pad_maximum_fusion.4), channel_id=1, source_target_pairs={{0,8},{1,9},{2,10},{3,11},{4,12},{5,13},{6,14},{7,15},{8,0},{9,1},... | collective-permute-start | bytes 1769480 | tf_op jit(solution)/shard_map/ppermute | solution.py:718
  46.6 15.2 %collective-permute-start.15 = (bf16[2,4,48,768]{3,2,1,0:T(8,128)(2,1)S(1)}, bf16[2,4,48,768]{3,2,1,0:T(8,128)(2,1)S(1)}, u32[]{:S(2)}, u32[]{:S(2)}) collective-permute-start(bf16[2,4,48,768]{3,2,1,0:T(8,128)(2,1)S(1)} %pad_maximum_fusion.6.refs_2_), channel_id=1, source_target_pairs={{0,2},{1,3},{2,0},{3,1},{4,6},{5,7},{6,4},{7,5},{8,10},{9,11},{10,... | collective-permute-start | bytes 1769480 | tf_op jit(solution)/shard_map/ppermute | solution.py:718
  46.8 15.0 %collective-permute-start.14 = (bf16[2,4,48,768]{3,2,1,0:T(8,128)(2,1)S(1)}, bf16[2,4,48,768]{3,2,1,0:T(8,128)(2,1)S(1)}, u32[]{:S(2)}, u32[]{:S(2)}) collective-permute-start(bf16[2,4,48,768]{3,2,1,0:T(8,128)(2,1)S(1)} %pad_maximum_fusion.5.refs_0_), channel_id=1, source_target_pairs={{0,4},{1,5},{2,6},{3,7},{4,0},{5,1},{6,2},{7,3},{8,12},{9,13},{10,... | collective-permute-start | bytes 1769480 | tf_op jit(solution)/shard_map/ppermute | solution.py:718
  60.7 15.7 %collective-permute-start.10 = (bf16[4,2,48,768]{3,2,1,0:T(8,128)(2,1)S(1)}, bf16[4,2,48,768]{3,2,1,0:T(8,128)(2,1)S(1)}, u32[]{:S(2)}, u32[]{:S(2)}) collective-permute-start(bf16[4,2,48,768]{3,2,1,0:T(8,128)(2,1)S(1)} %get-tuple-element.243), channel_id=1, source_target_pairs={{0,2},{1,3},{2,0},{3,1},{4,6},{5,7},{6,4},{7,5},{8,10},{9,11},{10,... | collective-permute-start | bytes 1769480 | tf_op jit(solution)/shard_map/ppermute | solution.py:718
  61.2 15.3 %collective-permute-start.11 = (bf16[4,2,48,768]{3,2,1,0:T(8,128)(2,1)S(1)}, bf16[4,2,48,768]{3,2,1,0:T(8,128)(2,1)S(1)}, u32[]{:S(2)}, u32[]{:S(2)}) collective-permute-start(bf16[4,2,48,768]{3,2,1,0:T(8,128)(2,1)S(1)} %get-tuple-element.244), channel_id=1, source_target_pairs={{0,4},{1,5},{2,6},{3,7},{4,0},{5,1},{6,2},{7,3},{8,12},{9,13},{10,... | collective-permute-start | bytes 1769480 | tf_op jit(solution)/shard_map/ppermute | solution.py:718
  76.6 28.4 %collective-permute-start.18 = (bf16[2,4,2,48,768]{4,3,2,1,0:T(8,128)(2,1)S(1)}, bf16[2,4,2,48,768]{4,3,2,1,0:T(8,128)(2,1)S(1)}, u32[]{:S(2)}, u32[]{:S(2)}) collective-permute-start(bf16[2,4,2,48,768]{4,3,2,1,0:T(8,128)(2,1)S(1)} %pad_maximum_fusion.2), channel_id=1, source_target_pairs={{0,2},{1,3},{2,0},{3,1},{4,6},{5,7},{6,4},{7,5},{8,10},{9,11},{10,... | collective-permute-start | bytes 3538952 | tf_op jit(solution)/shard_map/ppermute | solution.py:718
  78.3 28.2 %collective-permute-start.17 = (bf16[2,4,2,48,768]{4,3,2,1,0:T(8,128)(2,1)S(1)}, bf16[2,4,2,48,768]{4,3,2,1,0:T(8,128)(2,1)}, u32[]{:S(2)}, u32[]{:S(2)}) collective-permute-start(bf16[2,4,2,48,768]{4,3,2,1,0:T(8,128)(2,1)S(1)} %pad_maximum_fusion.1), channel_id=1, source_target_pairs={{0,4},{1,5},{2,6},{3,7},{4,0},{5,1},{6,2},{7,3},{8,12},{9,13},{10,... | collective-permute-start | bytes 3538952 | tf_op jit(solution)/shard_map/ppermute | solution.py:718
  122.9 28.6 %collective-permute-start.20 = (bf16[2,4,2,48,768]{4,3,2,1,0:T(8,128)(2,1)}, bf16[2,4,2,48,768]{4,3,2,1,0:T(8,128)(2,1)S(1)}, u32[]{:S(2)}, u32[]{:S(2)}) collective-permute-start(bf16[2,4,2,48,768]{4,3,2,1,0:T(8,128)(2,1)} %bitcast.103), channel_id=1, source_target_pairs={{0,2},{1,3},{2,0},{3,1},{4,6},{5,7},{6,4},{7,5},{8,10},{9,11},{10,... | collective-permute-start | bytes 3538952 | tf_op jit(solution)/shard_map/ppermute | solution.py:718
  123.8 28.2 %collective-permute-start.19 = (bf16[2,4,2,48,768]{4,3,2,1,0:T(8,128)(2,1)}, bf16[2,4,2,48,768]{4,3,2,1,0:T(8,128)(2,1)S(1)}, u32[]{:S(2)}, u32[]{:S(2)}) collective-permute-start(bf16[2,4,2,48,768]{4,3,2,1,0:T(8,128)(2,1)} %bitcast.102), channel_id=1, source_target_pairs={{0,4},{1,5},{2,6},{3,7},{4,0},{5,1},{6,2},{7,3},{8,12},{9,13},{10,... | collective-permute-start | bytes 3538952 | tf_op jit(solution)/shard_map/ppermute | solution.py:718
  146.8 28.1 %collective-permute-start.24 = (bf16[1088,768]{1,0:T(8,128)(2,1)}, bf16[1088,768]{1,0:T(8,128)(2,1)}, u32[]{:S(2)}, u32[]{:S(2)}) collective-permute-start(bf16[1088,768]{1,0:T(8,128)(2,1)} %get-tuple-element.173.one), channel_id=1, source_target_pairs={{0,1},{1,0},{2,3},{3,2},{4,5},{5,4},{6,7},{7,6},{8,9},{9,8},{10,11... | collective-permute-start | bytes 5013512 | tf_op jit(solution)/shard_map/ppermute | solution.py:718
  147.0 27.9 %collective-permute-start.25 = (bf16[1088,768]{1,0:T(8,128)(2,1)}, bf16[1088,768]{1,0:T(8,128)(2,1)}, u32[]{:S(2)}, u32[]{:S(2)}) collective-permute-start(bf16[1088,768]{1,0:T(8,128)(2,1)} %get-tuple-element.167.one), channel_id=1, source_target_pairs={{0,1},{1,0},{2,3},{3,2},{4,5},{5,4},{6,7},{7,6},{8,9},{9,8},{10,11... | collective-permute-start | bytes 5013512 | tf_op jit(solution)/shard_map/ppermute | solution.py:718
  156.8 15.0 %collective-permute-start.23 = (bf16[4,2,48,768]{3,2,1,0:T(8,128)(2,1)}, bf16[4,2,48,768]{3,2,1,0:T(8,128)(2,1)S(1)}, u32[]{:S(2)}, u32[]{:S(2)}) collective-permute-start(bf16[4,2,48,768]{3,2,1,0:T(8,128)(2,1)} %get-tuple-element.172), channel_id=1, source_target_pairs={{0,4},{1,5},{2,6},{3,7},{4,0},{5,1},{6,2},{7,3},{8,12},{9,13},{10,... | collective-permute-start | bytes 1769480 | tf_op jit(solution)/shard_map/ppermute | solution.py:718
  158.3 16.5 %collective-permute-start.22 = (bf16[4,2,48,768]{3,2,1,0:T(8,128)(2,1)}, bf16[4,2,48,768]{3,2,1,0:T(8,128)(2,1)S(1)}, u32[]{:S(2)}, u32[]{:S(2)}) collective-permute-start(bf16[4,2,48,768]{3,2,1,0:T(8,128)(2,1)} %get-tuple-element.171), channel_id=1, source_target_pairs={{0,2},{1,3},{2,0},{3,1},{4,6},{5,7},{6,4},{7,5},{8,10},{9,11},{10,... | collective-permute-start | bytes 1769480 | tf_op jit(solution)/shard_map/ppermute | solution.py:718
  168.6 21.8 %collective-permute-start.29 = (bf16[2,4,48,768]{3,2,1,0:T(8,128)(2,1)}, bf16[2,4,48,768]{3,2,1,0:T(8,128)(2,1)S(1)}, u32[]{:S(2)}, u32[]{:S(2)}) collective-permute-start(bf16[2,4,48,768]{3,2,1,0:T(8,128)(2,1)} %get-tuple-element.195), channel_id=1, source_target_pairs={{0,2},{1,3},{2,0},{3,1},{4,6},{5,7},{6,4},{7,5},{8,10},{9,11},{10,... | collective-permute-start | bytes 1769480 | tf_op jit(solution)/shard_map/ppermute | solution.py:718
  171.8 18.6 %collective-permute-start.28 = (bf16[2,4,48,768]{3,2,1,0:T(8,128)(2,1)}, bf16[2,4,48,768]{3,2,1,0:T(8,128)(2,1)S(1)}, u32[]{:S(2)}, u32[]{:S(2)}) collective-permute-start(bf16[2,4,48,768]{3,2,1,0:T(8,128)(2,1)} %get-tuple-element.178), channel_id=1, source_target_pairs={{0,4},{1,5},{2,6},{3,7},{4,0},{5,1},{6,2},{7,3},{8,12},{9,13},{10,... | collective-permute-start | bytes 1769480 | tf_op jit(solution)/shard_map/ppermute | solution.py:718
  179.0 19.3 %collective-permute-start.26 = (bf16[2,2,2,48,768]{4,3,2,1,0:T(8,128)(2,1)}, bf16[2,2,2,48,768]{4,3,2,1,0:T(8,128)(2,1)S(1)}, u32[]{:S(2)}, u32[]{:S(2)}) collective-permute-start(bf16[2,2,2,48,768]{4,3,2,1,0:T(8,128)(2,1)} %get-tuple-element.183), channel_id=1, source_target_pairs={{0,8},{1,9},{2,10},{3,11},{4,12},{5,13},{6,14},{7,15},{8,0},{9,1},... | collective-permute-start | bytes 1769480 | tf_op jit(solution)/shard_map/ppermute | solution.py:718
  194.8 20.3 %collective-permute-start.33 = (bf16[4,48,768]{2,1,0:T(8,128)(2,1)}, bf16[4,48,768]{2,1,0:T(8,128)(2,1)S(1)}, u32[]{:S(2)}, u32[]{:S(2)}) collective-permute-start(bf16[4,48,768]{2,1,0:T(8,128)(2,1)} %get-tuple-element.207), channel_id=1, source_target_pairs={{0,4},{1,5},{2,6},{3,7},{4,0},{5,1},{6,2},{7,3},{8,12},{9,13},{10,... | collective-permute-start | bytes 884744 | tf_op jit(solution)/shard_map/ppermute | solution.py:718
  195.9 19.2 %collective-permute-start.32 = (bf16[4,48,768]{2,1,0:T(8,128)(2,1)}, bf16[4,48,768]{2,1,0:T(8,128)(2,1)S(1)}, u32[]{:S(2)}, u32[]{:S(2)}) collective-permute-start(bf16[4,48,768]{2,1,0:T(8,128)(2,1)} %get-tuple-element.200), channel_id=1, source_target_pairs={{0,2},{1,3},{2,0},{3,1},{4,6},{5,7},{6,4},{7,5},{8,10},{9,11},{10,... | collective-permute-start | bytes 884744 | tf_op jit(solution)/shard_map/ppermute | solution.py:718
  210.2 21.3 %collective-permute-start.39 = (bf16[1,2,2,48,768]{4,3,2,1,0:T(8,128)(2,1)S(1)}, bf16[1,2,2,48,768]{4,3,2,1,0:T(8,128)(2,1)S(1)}, u32[]{:S(2)}, u32[]{:S(2)}) collective-permute-start(bf16[1,2,2,48,768]{4,3,2,1,0:T(8,128)(2,1)S(1)} %copy-done.29), channel_id=1, source_target_pairs={{0,16},{1,17},{2,18},{3,19},{4,20},{5,21},{6,22},{7,23},{8,24},{9,... | collective-permute-start | bytes 884744 | tf_op jit(solution)/shard_map/ppermute | solution.py:718
  (48 other events, 274.7 us)

commit v4 on v3

--- a/solution.py
+++ b/solution.py
@@ -322,7 +322,7 @@
     rows = pl.ds(pl.multiple_of(step * SLOT, 16), SLOT)
     if not more:
         middle = x_in[...].astype(F32) + (one[...].astype(F32) + two[...].astype(F32))
-        middle_out[...] = middle
+        middle_out[...] = middle.astype(BF16)
         hat, _ = stats(middle)
         normed[rows] = (hat * norms[2:3] + norms[3:4]).astype(BF16)
     tile_n = normed[rows]
@@ -367,7 +367,7 @@
     span = parts[0].shape[2]
     more = sums is not None
     tile = pl.BlockSpec((SLOT, wide), lambda t: (t, 0))
-    wide_f32, wide_bf16 = (jax.ShapeDtypeStruct((rows, wide), kind) for kind in (F32, BF16))
+    wide_bf16 = jax.ShapeDtypeStruct((rows, wide), BF16)
     full = whole(cot.shape)
     count = len(parts)
     if more:
@@ -385,7 +385,7 @@
         + [tile, tile]
         + [ANY] * count
         + [whole(bias.shape)],
-        out_shape=([] if more else [wide_f32, wide_bf16])
+        out_shape=([] if more else [wide_bf16, wide_bf16])
         + [wide_bf16, wide_bf16]
         + [jax.ShapeDtypeStruct(v.shape, BF16) for v in parts]
         + [jax.ShapeDtypeStruct(bias.shape, F32)],
@@ -408,7 +408,7 @@
         out[...] = (zero[0].astype(F32) + got[0].astype(F32)).astype(BF16)
 
 
-def add_second(a_zero, a_got, b_zero, b_got):
+def add_second(a_zero, a_got, b_zero, b_got, time):
     shape = a_zero.shape[1:]
     block = pl.BlockSpec((1, 1) + shape[1:], lambda k: (1, k) + (0,) * (len(shape) - 1))
     out = pl.BlockSpec((1,) + shape[1:], lambda k: (k,) + (0,) * (len(shape) - 1))
@@ -419,7 +419,7 @@
         out_specs=[out] * 2,
         out_shape=[jax.ShapeDtypeStruct(shape, BF16)] * 2,
         compiler_params=params(),
-        cost_estimate=cost(3.4),
+        cost_estimate=cost(time),
         name="add_second",
     )(a_zero, a_got, b_zero, b_got)
 
@@ -476,7 +476,7 @@
 
 def finish_kernel(middle, one, two, dest_own, dest_halo, own_out, halo_out, values):
     step = pl.program_id(0)
-    value = middle[...] + (one[...].astype(F32) + two[...].astype(F32))
+    value = middle[...].astype(F32) + (one[...].astype(F32) + two[...].astype(F32))
     values[pl.ds(pl.multiple_of(step * SLOT, 16), SLOT)] = value.astype(BF16)
     spread_rows(values, dest_own, dest_halo, own_out, halo_out)
 
@@ -513,7 +513,7 @@
 
 def back_kernel(held_count, place, middle, one, two, cot, norms, qkv, prob, *refs):
     held = refs[:held_count]
-    gm_out, gp_out, dq_out, part_out, sums_out, weight, scored, sem = refs[held_count:]
+    gp_out, dq_out, part_out, sums_out, weight, scored, sem = refs[held_count:]
     step = pl.program_id(0)
     third = weight.shape[2] // 4
     copies = weight_copies(place, held, weight, sem)
@@ -524,11 +524,10 @@
         sums_out[...] = jnp.zeros_like(sums_out)
 
     grad = one[...].astype(F32) + two[...].astype(F32)
-    hat, inverse = stats(middle[...])
+    hat, inverse = stats(middle[...].astype(F32))
     sums_out[0:1] += jnp.sum(grad * hat, axis=0, keepdims=True)
     sums_out[1:2] += jnp.sum(grad, axis=0, keepdims=True)
     grad_middle = cot[...].astype(F32) + norm_back(grad, hat, inverse, norms[2:3])
-    gm_out[...] = grad_middle
     grad_proj = grad_middle.astype(BF16)
     gp_out[...] = grad_proj
     live = lax.broadcasted_iota(jnp.int32, (TAIL, 1), 0) < IMG - (CORE - TAIL)
@@ -593,9 +592,8 @@
             pl.BlockSpec((1,) + prob.shape[1:], lambda t: (t, 0, 0, 0, 0)),
         ]
         + [ANY] * len(held),
-        out_specs=[tile, tile, tile_q, tile, whole((8, wide))],
+        out_specs=[tile, tile_q, tile, whole((8, wide))],
         out_shape=[
-            jax.ShapeDtypeStruct((rows, wide), F32),
             jax.ShapeDtypeStruct((rows, wide), BF16),
             jax.ShapeDtypeStruct(qkv.shape, BF16),
             jax.ShapeDtypeStruct((rows, wide), BF16),
@@ -669,7 +667,7 @@
     hat, inverse = stats(x_in[...].astype(F32))
     sums_out[0:1] += jnp.sum(grad * hat, axis=0, keepdims=True)
     sums_out[1:2] += jnp.sum(grad, axis=0, keepdims=True)
-    grad_in = gm[...] + norm_back(grad, hat, inverse, norms[0:1])
+    grad_in = gm[...].astype(F32) + norm_back(grad, hat, inverse, norms[0:1])
     prompt_out[...] += grad_in[: prompt_out.shape[0]]
     at = lax.broadcasted_iota(jnp.int32, (SLOT, 1), 0)
     value = jnp.where((at >= 1) & (at <= PROMPTS), 0.0, grad_in).astype(BF16)
@@ -917,17 +915,15 @@
     a_got, b_got = grid.by_x(grad_a1), grid.by_y(grad_b1)
     g_other = grid.by_core(g_part)
 
-    grad_middle, grad_proj, grad_qkv, g_one, sums_two = back(
+    grad_proj, grad_qkv, g_one, sums_two = back(
         place, middle, g_part, g_other, cot, norms, weights, qkv, prob, slots
     )
     g_one_other = grid.by_core(g_one)
     o_other = grid.by_core(after(o_part, g_one))
-    a_got, b_got, _ = tie(a_got, b_got, g_one)
-    a_send, b_send = add_second(grad_a0, a_got, grad_b0, b_got)
+    weight_blocks = weight_grads(place, normed, grad_proj, grad_qkv, att, weights)
+    a_got, b_got, _ = tie(a_got, b_got, weight_blocks[0])
+    a_send, b_send = add_second(grad_a0, a_got, grad_b0, b_got, 40)
     a_last, b_last = grid.by_y(a_send), grid.by_x(b_send)
-    weight_blocks = weight_grads(
-        place, after(normed, a_send), grad_proj, grad_qkv, att, weights
-    )
     if len(weight_blocks) == 1:
         blocks = weight_blocks[0].reshape(2, deep, 2, depth, 4 * third).swapaxes(1, 2)
         blocks = grid.to_relative(blocks, 2, 1)
@@ -939,15 +935,10 @@
             blocks[1, :, :, 1],
         ]
     att_a0, att_a1, att_b0, att_b1 = weight_blocks
-    att_a_got, att_b_got = grid.by_x(att_a1), grid.by_y(att_b1)
-    a_last, b_last, o_other, g_one_other, _ = tie(a_last, b_last, o_other, g_one_other, att_a1)
-    grad_keep, grad_send = fold_first(grad_a0, a_got, a_last, grad_b0, b_got, b_last)
-    grad_got = grid.by_z(grad_send, 1)
-
+    att_a_got, att_b_got = grid.by_x(after(att_a1, a_send)), grid.by_y(after(att_b1, b_send))
     tok_own, tok_halo, prompt_sum, sums_one = last(
-        x_in, grad_middle, g_one, after(g_one_other, grad_send), norms, dest_own, dest_halo, slots
+        x_in, grad_proj, g_one, after(g_one_other, a_send), norms, dest_own, dest_halo, slots
     )
-    tok_edge = grid.by_y(tok_halo)
 
     g_a = grad_bias_a.reshape(2, 2, deep, span)
     g_b = grad_bias_b.reshape(2, 2, deep, span)
@@ -959,24 +950,32 @@
     small = jnp.concatenate(
         [prompt_sum, sums_one[:2], sums_two[:2], bias_blocks.reshape(-1, wide)]
     )
+    out_own, out_halo = finish(
+        middle, o_part, after(o_other, tok_halo), dest_own, dest_halo, slots
+    )
+    edges = grid.by_y(jnp.concatenate([out_halo, tok_halo]))
+    small = exchange(small, lambda v: grid.by_z(v, 1))
+    a_last, b_last, _ = tie(a_last, b_last, out_halo)
+    grad_keep, grad_send = fold_first(grad_a0, a_got, a_last, grad_b0, b_got, b_last)
+    grad_got = grid.by_z(grad_send, 1)
+    att_a_got, att_b_got, small, _ = tie(att_a_got, att_b_got, small, grad_send)
+    stride = 2
+    while stride < deep:
+        small = exchange(small, lambda v, stride=stride: grid.by_z(v, stride))
+        stride *= 2
+    a_send, b_send = add_second(att_a0, att_a_got, att_b0, att_b_got, 4)
+    att_a_last, att_b_last = grid.by_y(a_send), grid.by_x(b_send)
+    grad_got, _ = tie(grad_got, a_send)
+    grad_keep, grad_got, grad_send = grid.fold_z(grad_keep, grad_got)
+    att_a_last, att_b_last, small, edges, _ = tie(
+        att_a_last, att_b_last, small, edges, grad_send
+    )
     small = exchange(small, grid.by_x)
-    att_a_got, att_b_got, _ = tie(att_a_got, att_b_got, tok_halo)
-    a_send, b_send = add_second(att_a0, att_a_got, att_b0, att_b_got)
-    att_a_last, att_b_last = grid.by_y(a_send), grid.by_x(b_send)
-    grad_got, small, _ = tie(grad_got, small, a_send)
-    grad_keep, grad_got, grad_send = grid.fold_z(grad_keep, grad_got)
-    small = exchange(small, grid.by_y)
-    out_own, out_halo = finish(
-        middle, o_part, after(o_other, grad_send), dest_own, dest_halo, slots
-    )
-    out_edge = grid.by_y(out_halo)
-    att_a_last, att_b_last, small, _ = tie(att_a_last, att_b_last, small, out_halo)
     att_keep, att_send = fold_first(att_a0, att_a_got, att_a_last, att_b0, att_b_got, att_b_last)
     att_got = grid.by_z(att_send, 1)
-    small = exchange(small, lambda v: grid.by_z(v, 1))
-    att_got, small = tie(att_got, small)
+    att_got, small, grad_got = tie(att_got, small, grad_got)
+    small = exchange(small, grid.by_y)
     att_keep, att_got, _ = grid.fold_z(att_keep, att_got)
-    grad_got = after(grad_got, att_keep)
     grad_shard = (grad_keep.astype(F32) + grad_got.astype(F32))[0]
     grad_up = grad_shard[:, 0].reshape(hidden, wide).swapaxes(0, 1)
     grad_down = grad_shard[:, 1].reshape(hidden, wide)
@@ -992,17 +991,13 @@
         value = value.at[count - HALO :].add(ends)
         return value.at[:HALO].add(begins)
 
-    stride = 2
-    while stride < deep:
-        small = exchange(small, lambda v, stride=stride: grid.by_z(v, stride))
-        stride *= 2
     bias_all = small[60:].reshape(2, 2, deep, hidden)
     grad_bias = lax.dynamic_slice(
         bias_all, (grid.y, grid.x, grid.z, jnp.int32(0)), (1, 1, 1, hidden)
     ).reshape(hidden)
     return (
-        merge(out_own, out_edge),
-        merge(tok_own, tok_edge),
+        merge(out_own, edges[:HALO]),
+        merge(tok_own, edges[HALO:]),
         small[1 : 1 + PROMPTS],
         small[56],
         small[57],

time: 242 us -> 239 us (0.988)
  starting transfers between devices: 41.6 us -> 38.1 us
    ppermute x40 -> x39, starting transfers between devices: 41.6 us -> 38.1 us  [send(): return lax.ppermute(value, AXES, pairs)]
    unnamed x68 -> x60, local copies, waits for them, and re-layouts: 8.64 us -> 6.62 us
    ppermute x40 -> x39, waiting for transfers between devices: 53 us -> 54.6 us  [send(): return lax.ppermute(value, AXES, pairs)]
  transfers between devices with their start and end apart: 40 -> 39, of which waited for: 18 -> 14; matrix products, arithmetic and copies ran while one was open for 9% -> 10% of each run, Pallas kernels for 41% -> 41%
where the time goes in v4:
time: 239 us; the launch traced here: 238 us
  Pallas kernels  115 us (48%)
  waiting for transfers between devices  54.6 us (23%)
  starting transfers between devices  38.1 us (16%)
  local copies, waits for them, and re-layouts  15 us (6%)
  other arithmetic  13.8 us (6%)
    ppermute x39, waiting for transfers between devices, send(): return lax.ppermute(value, AXES, pairs)  54.6 us
    ppermute x39, starting transfers between devices, send(): return lax.ppermute(value, AXES, pairs)  38.1 us
    pallas_call x2, Pallas kernels, mlp(): pl.pallas_call(functools.partial(mlp_kernel, more, count), grid=(slots,),...  34.1 us
    pallas_call x1, Pallas kernels, back(): pl.pallas_call(functools.partial(back_kernel, len(held)), grid=(slots,),...  18.8 us
    pallas_call x1, Pallas kernels, attend(): pl.pallas_call(functools.partial(attend_kernel, len(held)), grid=(slots,)...  12.9 us
    pallas_call x1, Pallas kernels, prep(): pl.pallas_call(prep_kernel, grid=(slots,), in_specs=[SMEM] + [whole(v.sha...  9.44 us
    pallas_call x1, Pallas kernels, weight_grads(): pl.pallas_call(functools.partial(weight_kernel, len(held)), grid=(wide //...  9.03 us
    pallas_call x1, Pallas kernels, last(): pl.pallas_call(last_kernel, grid=(slots,), in_specs=[tile] * 4 + [whole(n...  7.83 us
  transfers between devices with their start and end apart: 39, of which 14 were waited for; matrix products, arithmetic and copies ran while one was open for 10% of the time, Pallas kernels for 41%

profile of v4, /device:TPU:0, one launch (start us, length us, event | category | flops | bytes accessed | tf_op | source)
XLA Modules:
  0.0 237.5 jit_solution(17332576199964692001)
XLA Ops:
  0.6 4.1 %collective-permute-start = (bf16[1,96]{1,0:T(2,128)(2,1)}, bf16[1,96]{1,0:T(2,128)(2,1)S(1)}, u32[]{:S(2)}, u32[]{:S(2)}) collective-permute-start(bf16[1,96]{1,0:T(2,128)(2,1)} %bitcast.96), channel_id=1, source_target_pairs={{0,16},{1,17},{2,18},{3,19},{4,20},{5,21},{6,22},{7,23},{8,24},{9,... | collective-permute-start | bytes 584 | tf_op jit(solution)/shard_map/ppermute | solution.py:716
  19.7 2.6 %collective-permute-done.1 = bf16[2,1,48,768]{3,2,1,0:T(8,128)(2,1)S(1)} collective-permute-done((bf16[2,1,48,768]{3,2,1,0:T(8,128)(2,1)S(1)}, bf16[2,1,48,768]{3,2,1,0:T(8,128)(2,1)S(1)}, u32[]{:S(2)}, u32[]{:S(2)}) %collective-permute-start.1) | collective-permute-done | bytes 147488 | tf_op jit(solution)/shard_map/ppermute | solution.py:716
  26.8 5.8 %collective-permute-done.5 = bf16[2,2,48,768]{3,2,1,0:T(8,128)(2,1)S(1)} collective-permute-done((bf16[2,2,48,768]{3,2,1,0:T(8,128)(2,1)S(1)}, bf16[2,2,48,768]{3,2,1,0:T(8,128)(2,1)S(1)}, u32[]{:S(2)}, u32[]{:S(2)}) %collective-permute-start.5) | collective-permute-done | bytes 294944 | tf_op jit(solution)/shard_map/ppermute | solution.py:716
  32.7 2.6 %collective-permute-start.12 = (bf16[4,48,768]{2,1,0:T(8,128)(2,1)S(1)}, bf16[4,48,768]{2,1,0:T(8,128)(2,1)S(1)}, u32[]{:S(2)}, u32[]{:S(2)}) collective-permute-start(bf16[4,48,768]{2,1,0:T(8,128)(2,1)S(1)} %get-tuple-element.247), channel_id=1, source_target_pairs={{0,2},{1,3},{2,0},{3,1},{4,6},{5,7},{6,4},{7,5},{8,10},{9,11},{10,... | collective-permute-start | bytes 884744 | tf_op jit(solution)/shard_map/ppermute | solution.py:716
  36.8 9.4 %prep.1 = (bf16[1088,768]{1,0:T(8,128)(2,1)}, bf16[1088,768]{1,0:T(8,128)(2,1)}, bf16[1088,768]{1,0:T(8,128)(2,1)}, s32[1,512]{1,0:T(1,128)}, s32[1,48]{1,0:T(1,128)}) custom-call(s32[4]{0:T(128)} %pad_add_fusion.place, bf16[1040,768]{1,0:T(8,128)(2,1)} %copy-done.2, bf16[1040,768]{1,0:T(8,128)(2,1)} %collective-permute-done.4.other, ...), custom_call_target="tpu_custom_call" | custom-call | flops 1380000000 | bytes 1 | tf_op jit(solution)/shard_map/prep/pallas_call | solution.py:151
  47.3 12.9 %collective-permute-done.9 = bf16[2,2,2,48,768]{4,3,2,1,0:T(8,128)(2,1)S(1)} collective-permute-done((bf16[2,2,2,48,768]{4,3,2,1,0:T(8,128)(2,1)S(1)}, bf16[2,2,2,48,768]{4,3,2,1,0:T(8,128)(2,1)S(1)}, u32[]{:S(2)}, u32[]{:S(2)}) %collective-permute-start.9) | collective-permute-done | bytes 589856 | tf_op jit(solution)/shard_map/ppermute | solution.py:716
  63.4 12.9 %attend.1 = (bf16[2,1088,576]{2,1,0:T(8,128)(2,1)}, bf16[4,2,3,256,256]{4,3,2,1,0:T(8,128)(2,1)}, bf16[2,1088,192]{2,1,0:T(8,128)(2,1)}, bf16[1088,768]{1,0:T(8,128)(2,1)}) custom-call(s32[4]{0:T(128)} %pad_add_fusion.place, bf16[1088,768]{1,0:T(8,128)(2,1)} %get-tuple-element.144.normed, bf16[2,4,48,768]{3,2,1,0:T(8,128)(2,1)} %copy-done.1, ...), custom_call_target="tpu_custom_call" | custom-call | flops 2242500096 | bytes 1 | tf_op jit(solution)/shard_map/attend/pallas_call | solution.py:257
  81.3 17.8 %mlp.2 = (bf16[1088,768]{1,0:T(8,128)(2,1)}, bf16[1088,768]{1,0:T(8,128)(2,1)}, bf16[1088,768]{1,0:T(8,128)(2,1)}, bf16[1088,768]{1,0:T(8,128)(2,1)}, bf16[8,2,4...) custom-call(bf16[8,2,48,768]{3,2,1,0:T(8,128)(2,1)} %bitcast.74, ...), custom_call_target="tpu_custom_call" | custom-call | flops 2932499968 | bytes 1 | tf_op jit(solution)/shard_map/mlp/pallas_call | solution.py:380
  99.1 5.9 %collective-permute-done.18 = bf16[2,4,2,48,768]{4,3,2,1,0:T(8,128)(2,1)S(1)} collective-permute-done((bf16[2,4,2,48,768]{4,3,2,1,0:T(8,128)(2,1)S(1)}, bf16[2,4,2,48,768]{4,3,2,1,0:T(8,128)(2,1)S(1)}, u32[]{:S(2)}, u32[]{:S(2)}) %collective-permute-start.18) | collective-permute-done | bytes 1179680 | tf_op jit(solution)/shard_map/ppermute | solution.py:716
  106.5 16.3 %mlp.3 = (bf16[1088,768]{1,0:T(8,128)(2,1)}, bf16[1088,768]{1,0:T(8,128)(2,1)}, bf16[8,2,48,768]{3,2,1,0:T(8,128)(2,1)}, bf16[8,2,48,768]{3,2,1,0:T(8,128)(2,1)}, f32[1,768]{1,0:T(1,128)}) custom-call(bf16[8,2,48,768]{3,2,1,0:T(8,128)(2,1)} %bitcast.29.refs_0_, bf16[8,2,48,768]{3,2,1,0:T(8,128)(2,1)} %bitcast.104, ...), custom_call_target="tpu_custom_call" | custom-call | flops 2932499968 | bytes 1 | tf_op jit(solution)/shard_map/mlp/pallas_call | solution.py:380
  127.9 18.8 %back.1 = (bf16[1088,768]{1,0:T(8,128)(2,1)}, bf16[2,1088,576]{2,1,0:T(8,128)(2,1)}, bf16[1088,768]{1,0:T(8,128)(2,1)}, f32[8,768]{1,0:T(8,128)}) custom-call(s32[4]{0:T(128)} %pad_add_fusion.place, bf16[1088,768]{1,0:T(8,128)(2,1)} %get-tuple-element.155.middle, bf16[1088,768]{1,0:T(8,128)(2,1)} %get-tuple-element.160.one, bf16[1088,768]{1,0:T(8,128)(2,1)} %copy-done.3, ...), custom_call_target="tpu_custom_call" | custom-call | flops 3277499904 | bytes 1 | tf_op jit(solution)/shard_map/back/pallas_call | solution.py:581
  147.4 9.0 %weight_grads.1 = (bf16[2,4,48,768]{3,2,1,0:T(8,128)(2,1)}, bf16[2,4,48,768]{3,2,1,0:T(8,128)(2,1)}, bf16[2,4,48,768]{3,2,1,0:T(8,128)(2,1)}, bf16[2,4,48,768]{3,2,1,0:T(8,128)(2,1)}) custom-call(s32[4]{0:T(128)} %pad_add_fusion.place, bf16[1088,768]{1,0:T(8,128)(2,1)} %get-tuple-element.144.normed, bf16[1088,768]{1,0:T(8,128)(2,1)} %get-tuple-element.165.grad_proj.gm, ...), custom_call_target="tpu_custom_call" | custom-call | flops 1552499968 | bytes 1 | tf_op jit(solution)/shard_map/weight_grads/pallas_call | solution.py:640
  156.5 3.7 %add_second.2 = (bf16[4,2,48,768]{3,2,1,0:T(8,128)(2,1)}, bf16[4,2,48,768]{3,2,1,0:T(8,128)(2,1)}) custom-call(bf16[2,4,2,48,768]{4,3,2,1,0:T(8,128)(2,1)} %bitcast.76, bf16[2,4,2,48,768]{4,3,2,1,0:T(8,128)(2,1)} %collective-permute-done.22.a_got, bf16[2,4,2,48,768]{4,3,2,1,0:T(8,128)(2,1)} %bitcast.78, bf16[2,4,2,48,768]{4,3,2,1,0:T(8,128)(2,1)} %collective-permute-done.23.b_got), custom_call_target="tpu_custom_call" | custom-call | flops 6899999744 | bytes 1 | tf_op jit(solution)/shard_map/add_second/pallas_call | solution.py:415
  165.2 7.8 %last.1 = (f32[512,768]{1,0:T(8,128)}, bf16[48,768]{1,0:T(8,128)(2,1)}, f32[56,768]{1,0:T(8,128)}, f32[8,768]{1,0:T(8,128)}) custom-call(bf16[1088,768]{1,0:T(8,128)(2,1)} %get-tuple-element.148.refs_2_.x_in, bf16[1088,768]{1,0:T(8,128)(2,1)} %get-tuple-element.165.grad_proj.gm, bf16[1088,768]{1,0:T(8,128)(2,1)} %get-tuple-element.163.one, ...), custom_call_target="tpu_custom_call" | custom-call | flops 1207500032 | bytes 1 | tf_op jit(solution)/shard_map/last/pallas_call | solution.py:682
  175.4 5.7 %finish.1 = (bf16[512,768]{1,0:T(8,128)(2,1)}, bf16[48,768]{1,0:T(8,128)(2,1)}) custom-call(bf16[1088,768]{1,0:T(8,128)(2,1)} %get-tuple-element.155.middle, bf16[1088,768]{1,0:T(8,128)(2,1)} %get-tuple-element.164.one, bf16[1088,768]{1,0:T(8,128)(2,1)} %copy-done.5, s32[1,512]{1,0:T(1,128)} %get-tuple-element.177.dest_own, s32[1,48]{1,0:T(1,128)} %get-tuple-element.178.dest_halo), custom_call_target="tpu_custom_call" | custom-call | flops 862499968 | bytes 1 | tf_op jit(solution)/shard_map/finish/pallas_call | solution.py:498
  181.1 3.3 %fold_first.2 = (bf16[2,2,2,48,768]{4,3,2,1,0:T(8,128)(2,1)}, bf16[2,2,2,48,768]{4,3,2,1,0:T(8,128)(2,1)}) custom-call(bf16[2,4,2,48,768]{4,3,2,1,0:T(8,128)(2,1)} %bitcast.77, bf16[2,4,2,48,768]{4,3,2,1,0:T(8,128)(2,1)} %collective-permute-done.22.a_got, bf16[4,2,48,768]{3,2,1,0:T(8,128)(2,1)} %collective-permute-done.27.a_last, ...), custom_call_target="tpu_custom_call" | custom-call | flops 517500000 | bytes 1 | tf_op jit(solution)/shard_map/fold_first/pallas_call | solution.py:465
  185.9 2.6 %collective-permute-done.24.a_got = bf16[2,4,48,768]{3,2,1,0:T(8,128)(2,1)} collective-permute-done((bf16[2,4,48,768]{3,2,1,0:T(8,128)(2,1)}, bf16[2,4,48,768]{3,2,1,0:T(8,128)(2,1)}, u32[]{:S(2)}, u32[]{:S(2)}) %collective-permute-start.24) | collective-permute-done | bytes 589856 | tf_op jit(solution)/shard_map/ppermute | solution.py:716
  189.8 3.4 %add_second.3 = (bf16[4,48,768]{2,1,0:T(8,128)(2,1)}, bf16[4,48,768]{2,1,0:T(8,128)(2,1)}) custom-call(bf16[2,4,48,768]{3,2,1,0:T(8,128)(2,1)} %get-tuple-element.171.a_zero, bf16[2,4,48,768]{3,2,1,0:T(8,128)(2,1)} %collective-permute-done.24.a_got, bf16[2,4,48,768]{3,2,1,0:T(8,128)(2,1)} %get-tuple-element.197.b_zero, ...), custom_call_target="tpu_custom_call" | custom-call | flops 690000000 | bytes 1 | tf_op jit(solution)/shard_map/add_second/pallas_call | solution.py:415
  195.8 3.9 %collective-permute-done.31 = bf16[62,768]{1,0:T(8,128)(2,1)S(1)} collective-permute-done((bf16[62,768]{1,0:T(8,128)(2,1)S(1)}, bf16[62,768]{1,0:T(8,128)(2,1)S(1)}, u32[]{:S(2)}, u32[]{:S(2)}) %collective-permute-start.31) | collective-permute-done | bytes 95264 | tf_op jit(solution)/shard_map/ppermute | solution.py:716
  201.6 2.1 sum_split.2
  203.8 2.3 collective-permute-start.36
  210.9 2.4 %fold_first.3 = (bf16[2,2,48,768]{3,2,1,0:T(8,128)(2,1)}, bf16[2,2,48,768]{3,2,1,0:T(8,128)(2,1)}) custom-call(bf16[2,4,48,768]{3,2,1,0:T(8,128)(2,1)} %get-tuple-element.171.a_zero, bf16[2,4,48,768]{3,2,1,0:T(8,128)(2,1)} %collective-permute-done.24.a_got, bf16[4,48,768]{2,1,0:T(8,128)(2,1)} %copy-done.11, ...), custom_call_target="tpu_custom_call" | custom-call | flops 517500000 | bytes 1 | tf_op jit(solution)/shard_map/fold_first/pallas_call | solution.py:465
  216.5 7.4 %collective-permute-done.34.refs_1_ = bf16[2,2,48,768]{3,2,1,0:T(8,128)(2,1)S(1)} collective-permute-done((bf16[2,2,48,768]{3,2,1,0:T(8,128)(2,1)}, bf16[2,2,48,768]{3,2,1,0:T(8,128)(2,1)S(1)}, u32[]{:S(2)}, u32[]{:S(2)}) %collective-permute-start.34) | collective-permute-done | bytes 294944 | tf_op jit(solution)/shard_map/ppermute | solution.py:716
  230.6 5.0 %collective-permute-done.38 = bf16[1,2,48,768]{3,2,1,0:T(8,128)(2,1)S(1)} collective-permute-done((bf16[1,2,48,768]{3,2,1,0:T(8,128)(2,1)}, bf16[1,2,48,768]{3,2,1,0:T(8,128)(2,1)S(1)}, u32[]{:S(2)}, u32[]{:S(2)}) %collective-permute-start.38) | collective-permute-done | bytes 147488 | tf_op jit(solution)/shard_map/ppermute | solution.py:716
  (203 shorter events, 68.2 us)
Async XLA Ops:
  9.3 13.1 %collective-permute-start.4 = (bf16[1040,768]{1,0:T(8,128)(2,1)S(1)}, bf16[1040,768]{1,0:T(8,128)(2,1)}, u32[]{:S(2)}, u32[]{:S(2)}) collective-permute-start(bf16[1040,768]{1,0:T(8,128)(2,1)S(1)} %fusion.1.own), channel_id=1, source_target_pairs={{0,1},{1,0},{2,3},{3,2},{4,5},{5,4},{6,7},{7,6},{8,9},{9,8},{10,11... | collective-permute-start | bytes 4792328 | tf_op jit(solution)/shard_map/ppermute | solution.py:716
  25.8 20.5 %collective-permute-start.3 = (bf16[2,1,2,48,768]{4,3,2,1,0:T(8,128)(2,1)S(1)}, bf16[2,1,2,48,768]{4,3,2,1,0:T(8,128)(2,1)S(1)}, u32[]{:S(2)}, u32[]{:S(2)}) collective-permute-start(bf16[2,1,2,48,768]{4,3,2,1,0:T(8,128)(2,1)S(1)} %bitcast.68), channel_id=1, source_target_pairs={{0,16},{1,17},{2,18},{3,19},{4,20},{5,21},{6,22},{7,23},{8,24},{9,... | collective-permute-start | bytes 884744 | tf_op jit(solution)/shard_map/ppermute | solution.py:716
  32.7 13.7 %collective-permute-start.12 = (bf16[4,48,768]{2,1,0:T(8,128)(2,1)S(1)}, bf16[4,48,768]{2,1,0:T(8,128)(2,1)S(1)}, u32[]{:S(2)}, u32[]{:S(2)}) collective-permute-start(bf16[4,48,768]{2,1,0:T(8,128)(2,1)S(1)} %get-tuple-element.247), channel_id=1, source_target_pairs={{0,2},{1,3},{2,0},{3,1},{4,6},{5,7},{6,4},{7,5},{8,10},{9,11},{10,... | collective-permute-start | bytes 884744 | tf_op jit(solution)/shard_map/ppermute | solution.py:716
  46.3 13.9 %collective-permute-start.9 = (bf16[2,2,2,48,768]{4,3,2,1,0:T(8,128)(2,1)S(1)}, bf16[2,2,2,48,768]{4,3,2,1,0:T(8,128)(2,1)S(1)}, u32[]{:S(2)}, u32[]{:S(2)}) collective-permute-start(bf16[2,2,2,48,768]{4,3,2,1,0:T(8,128)(2,1)S(1)} %pad_maximum_fusion.4), channel_id=1, source_target_pairs={{0,8},{1,9},{2,10},{3,11},{4,12},{5,13},{6,14},{7,15},{8,0},{9,1},... | collective-permute-start | bytes 1769480 | tf_op jit(solution)/shard_map/ppermute | solution.py:716
  46.5 15.2 %collective-permute-start.15 = (bf16[2,4,48,768]{3,2,1,0:T(8,128)(2,1)S(1)}, bf16[2,4,48,768]{3,2,1,0:T(8,128)(2,1)S(1)}, u32[]{:S(2)}, u32[]{:S(2)}) collective-permute-start(bf16[2,4,48,768]{3,2,1,0:T(8,128)(2,1)S(1)} %pad_maximum_fusion.6.refs_2_), channel_id=1, source_target_pairs={{0,2},{1,3},{2,0},{3,1},{4,6},{5,7},{6,4},{7,5},{8,10},{9,11},{10,... | collective-permute-start | bytes 1769480 | tf_op jit(solution)/shard_map/ppermute | solution.py:716
  46.7 15.0 %collective-permute-start.14 = (bf16[2,4,48,768]{3,2,1,0:T(8,128)(2,1)S(1)}, bf16[2,4,48,768]{3,2,1,0:T(8,128)(2,1)S(1)}, u32[]{:S(2)}, u32[]{:S(2)}) collective-permute-start(bf16[2,4,48,768]{3,2,1,0:T(8,128)(2,1)S(1)} %pad_maximum_fusion.5.refs_0_), channel_id=1, source_target_pairs={{0,4},{1,5},{2,6},{3,7},{4,0},{5,1},{6,2},{7,3},{8,12},{9,13},{10,... | collective-permute-start | bytes 1769480 | tf_op jit(solution)/shard_map/ppermute | solution.py:716
  60.6 15.8 %collective-permute-start.10 = (bf16[4,2,48,768]{3,2,1,0:T(8,128)(2,1)S(1)}, bf16[4,2,48,768]{3,2,1,0:T(8,128)(2,1)S(1)}, u32[]{:S(2)}, u32[]{:S(2)}) collective-permute-start(bf16[4,2,48,768]{3,2,1,0:T(8,128)(2,1)S(1)} %get-tuple-element.241), channel_id=1, source_target_pairs={{0,2},{1,3},{2,0},{3,1},{4,6},{5,7},{6,4},{7,5},{8,10},{9,11},{10,... | collective-permute-start | bytes 1769480 | tf_op jit(solution)/shard_map/ppermute | solution.py:716
  61.1 15.4 %collective-permute-start.11 = (bf16[4,2,48,768]{3,2,1,0:T(8,128)(2,1)S(1)}, bf16[4,2,48,768]{3,2,1,0:T(8,128)(2,1)S(1)}, u32[]{:S(2)}, u32[]{:S(2)}) collective-permute-start(bf16[4,2,48,768]{3,2,1,0:T(8,128)(2,1)S(1)} %get-tuple-element.242), channel_id=1, source_target_pairs={{0,4},{1,5},{2,6},{3,7},{4,0},{5,1},{6,2},{7,3},{8,12},{9,13},{10,... | collective-permute-start | bytes 1769480 | tf_op jit(solution)/shard_map/ppermute | solution.py:716
  76.6 28.4 %collective-permute-start.18 = (bf16[2,4,2,48,768]{4,3,2,1,0:T(8,128)(2,1)S(1)}, bf16[2,4,2,48,768]{4,3,2,1,0:T(8,128)(2,1)S(1)}, u32[]{:S(2)}, u32[]{:S(2)}) collective-permute-start(bf16[2,4,2,48,768]{4,3,2,1,0:T(8,128)(2,1)S(1)} %pad_maximum_fusion.2), channel_id=1, source_target_pairs={{0,2},{1,3},{2,0},{3,1},{4,6},{5,7},{6,4},{7,5},{8,10},{9,11},{10,... | collective-permute-start | bytes 3538952 | tf_op jit(solution)/shard_map/ppermute | solution.py:716
  78.3 28.2 %collective-permute-start.17 = (bf16[2,4,2,48,768]{4,3,2,1,0:T(8,128)(2,1)S(1)}, bf16[2,4,2,48,768]{4,3,2,1,0:T(8,128)(2,1)}, u32[]{:S(2)}, u32[]{:S(2)}) collective-permute-start(bf16[2,4,2,48,768]{4,3,2,1,0:T(8,128)(2,1)S(1)} %pad_maximum_fusion.1), channel_id=1, source_target_pairs={{0,4},{1,5},{2,6},{3,7},{4,0},{5,1},{6,2},{7,3},{8,12},{9,13},{10,... | collective-permute-start | bytes 3538952 | tf_op jit(solution)/shard_map/ppermute | solution.py:716
  123.0 33.5 %collective-permute-start.23 = (bf16[2,4,2,48,768]{4,3,2,1,0:T(8,128)(2,1)}, bf16[2,4,2,48,768]{4,3,2,1,0:T(8,128)(2,1)}, u32[]{:S(2)}, u32[]{:S(2)}) collective-permute-start(bf16[2,4,2,48,768]{4,3,2,1,0:T(8,128)(2,1)} %bitcast.103), channel_id=1, source_target_pairs={{0,2},{1,3},{2,0},{3,1},{4,6},{5,7},{6,4},{7,5},{8,10},{9,11},{10,... | collective-permute-start | bytes 3538952 | tf_op jit(solution)/shard_map/ppermute | solution.py:716
  124.1 32.4 %collective-permute-start.22 = (bf16[2,4,2,48,768]{4,3,2,1,0:T(8,128)(2,1)}, bf16[2,4,2,48,768]{4,3,2,1,0:T(8,128)(2,1)}, u32[]{:S(2)}, u32[]{:S(2)}) collective-permute-start(bf16[2,4,2,48,768]{4,3,2,1,0:T(8,128)(2,1)} %bitcast.102), channel_id=1, source_target_pairs={{0,4},{1,5},{2,6},{3,7},{4,0},{5,1},{6,2},{7,3},{8,12},{9,13},{10,... | collective-permute-start | bytes 3538952 | tf_op jit(solution)/shard_map/ppermute | solution.py:716
  146.7 16.6 %collective-permute-start.21 = (bf16[1088,768]{1,0:T(8,128)(2,1)}, bf16[1088,768]{1,0:T(8,128)(2,1)}, u32[]{:S(2)}, u32[]{:S(2)}) collective-permute-start(bf16[1088,768]{1,0:T(8,128)(2,1)} %get-tuple-element.163.one), channel_id=1, source_target_pairs={{0,1},{1,0},{2,3},{3,2},{4,5},{5,4},{6,7},{7,6},{8,9},{9,8},{10,11... | collective-permute-start | bytes 5013512 | tf_op jit(solution)/shard_map/ppermute | solution.py:716
  146.9 27.0 %collective-permute-start.20 = (bf16[1088,768]{1,0:T(8,128)(2,1)S(1)}, bf16[1088,768]{1,0:T(8,128)(2,1)S(1)}, u32[]{:S(2)}, u32[]{:S(2)}) collective-permute-start(bf16[1088,768]{1,0:T(8,128)(2,1)S(1)} %copy-done.4), channel_id=1, source_target_pairs={{0,1},{1,0},{2,3},{3,2},{4,5},{5,4},{6,7},{7,6},{8,9},{9,8},{10,11... | collective-permute-start | bytes 5013512 | tf_op jit(solution)/shard_map/ppermute | solution.py:716
  160.2 20.9 %collective-permute-start.28 = (bf16[4,2,48,768]{3,2,1,0:T(8,128)(2,1)}, bf16[4,2,48,768]{3,2,1,0:T(8,128)(2,1)}, u32[]{:S(2)}, u32[]{:S(2)}) collective-permute-start(bf16[4,2,48,768]{3,2,1,0:T(8,128)(2,1)} %get-tuple-element.185), channel_id=1, source_target_pairs={{0,4},{1,5},{2,6},{3,7},{4,0},{5,1},{6,2},{7,3},{8,12},{9,13},{10,... | collective-permute-start | bytes 1769480 | tf_op jit(solution)/shard_map/ppermute | solution.py:716
  161.7 19.4 %collective-permute-start.27 = (bf16[4,2,48,768]{3,2,1,0:T(8,128)(2,1)}, bf16[4,2,48,768]{3,2,1,0:T(8,128)(2,1)}, u32[]{:S(2)}, u32[]{:S(2)}) collective-permute-start(bf16[4,2,48,768]{3,2,1,0:T(8,128)(2,1)} %get-tuple-element.175), channel_id=1, source_target_pairs={{0,2},{1,3},{2,0},{3,1},{4,6},{5,7},{6,4},{7,5},{8,10},{9,11},{10,... | collective-permute-start | bytes 1769480 | tf_op jit(solution)/shard_map/ppermute | solution.py:716
  162.7 25.8 %collective-permute-start.24 = (bf16[2,4,48,768]{3,2,1,0:T(8,128)(2,1)}, bf16[2,4,48,768]{3,2,1,0:T(8,128)(2,1)}, u32[]{:S(2)}, u32[]{:S(2)}) collective-permute-start(bf16[2,4,48,768]{3,2,1,0:T(8,128)(2,1)} %get-tuple-element.183), channel_id=1, source_target_pairs={{0,4},{1,5},{2,6},{3,7},{4,0},{5,1},{6,2},{7,3},{8,12},{9,13},{10,... | collective-permute-start | bytes 1769480 | tf_op jit(solution)/shard_map/ppermute | solution.py:716
  163.4 26.4 %collective-permute-start.25 = (bf16[2,4,48,768]{3,2,1,0:T(8,128)(2,1)}, bf16[2,4,48,768]{3,2,1,0:T(8,128)(2,1)}, u32[]{:S(2)}, u32[]{:S(2)}) collective-permute-start(bf16[2,4,48,768]{3,2,1,0:T(8,128)(2,1)} %get-tuple-element.186), channel_id=1, source_target_pairs={{0,2},{1,3},{2,0},{3,1},{4,6},{5,7},{6,4},{7,5},{8,10},{9,11},{10,... | collective-permute-start | bytes 1769480 | tf_op jit(solution)/shard_map/ppermute | solution.py:716
  174.8 11.1 %collective-permute-start.26 = (bf16[62,768]{1,0:T(8,128)(2,1)S(1)}, bf16[62,768]{1,0:T(8,128)(2,1)S(1)}, u32[]{:S(2)}, u32[]{:S(2)}) collective-permute-start(bf16[62,768]{1,0:T(8,128)(2,1)S(1)} %pad_maximum_fusion.11), channel_id=1, source_target_pairs={{0,8},{1,9},{2,10},{3,11},{4,12},{5,13},{6,14},{7,15},{8,0},{9,1},... | collective-permute-start | bytes 285704 | tf_op jit(solution)/shard_map/ppermute | solution.py:716
  184.4 16.4 %collective-permute-start.33 = (bf16[2,2,2,48,768]{4,3,2,1,0:T(8,128)(2,1)}, bf16[2,2,2,48,768]{4,3,2,1,0:T(8,128)(2,1)S(1)}, u32[]{:S(2)}, u32[]{:S(2)}) collective-permute-start(bf16[2,2,2,48,768]{4,3,2,1,0:T(8,128)(2,1)} %get-tuple-element.195), channel_id=1, source_target_pairs={{0,8},{1,9},{2,10},{3,11},{4,12},{5,13},{6,14},{7,15},{8,0},{9,1},... | collective-permute-start | bytes 1769480 | tf_op jit(solution)/shard_map/ppermute | solution.py:716
  193.1 12.9 %collective-permute-start.30 = (bf16[4,48,768]{2,1,0:T(8,128)(2,1)}, bf16[4,48,768]{2,1,0:T(8,128)(2,1)S(1)}, u32[]{:S(2)}, u32[]{:S(2)}) collective-permute-start(bf16[4,48,768]{2,1,0:T(8,128)(2,1)} %get-tuple-element.200), channel_id=1, source_target_pairs={{0,4},{1,5},{2,6},{3,7},{4,0},{5,1},{6,2},{7,3},{8,12},{9,13},{10,... | collective-permute-start | bytes 884744 | tf_op jit(solution)/shard_map/ppermute | solution.py:716
  193.7 12.4 %collective-permute-start.29 = (bf16[4,48,768]{2,1,0:T(8,128)(2,1)}, bf16[4,48,768]{2,1,0:T(8,128)(2,1)S(1)}, u32[]{:S(2)}, u32[]{:S(2)}) collective-permute-start(bf16[4,48,768]{2,1,0:T(8,128)(2,1)} %get-tuple-element.199), channel_id=1, source_target_pairs={{0,2},{1,3},{2,0},{3,1},{4,6},{5,7},{6,4},{7,5},{8,10},{9,11},{10,... | collective-permute-start | bytes 884744 | tf_op jit(solution)/shard_map/ppermute | solution.py:716
  194.7 11.4 %collective-permute-start.32 = (bf16[96,768]{1,0:T(8,128)(2,1)S(1)}, bf16[96,768]{1,0:T(8,128)(2,1)S(1)}, u32[]{:S(2)}, u32[]{:S(2)}) collective-permute-start(bf16[96,768]{1,0:T(8,128)(2,1)S(1)} %pad_maximum_fusion.10), channel_id=1, source_target_pairs={{0,2},{1,3},{2,0},{3,1},{4,6},{5,7},{6,4},{7,5},{8,10},{9,11},{10,... | collective-permute-start | bytes 442376 | tf_op jit(solution)/shard_map/ppermute | solution.py:716
  203.8 20.2 %collective-permute-start.36 = (bf16[1,2,2,48,768]{4,3,2,1,0:T(8,128)(2,1)}, bf16[1,2,2,48,768]{4,3,2,1,0:T(8,128)(2,1)S(1)}, u32[]{:S(2)}, u32[]{:S(2)}) collective-permute-start(bf16[1,2,2,48,768]{4,3,2,1,0:T(8,128)(2,1)} %get-tuple-element.204), channel_id=1, source_target_pairs={{0,16},{1,17},{2,18},{3,19},{4,20},{5,21},{6,22},{7,23},{8,24},{9,... | collective-permute-start | bytes 884744 | tf_op jit(solution)/shard_map/ppermute | solution.py:716
  (43 other events, 292.3 us)

commit v5 on v4

--- a/solution.py
+++ b/solution.py
@@ -410,11 +410,12 @@
 
 def add_second(a_zero, a_got, b_zero, b_got, time):
     shape = a_zero.shape[1:]
-    block = pl.BlockSpec((1, 1) + shape[1:], lambda k: (1, k) + (0,) * (len(shape) - 1))
-    out = pl.BlockSpec((1,) + shape[1:], lambda k: (k,) + (0,) * (len(shape) - 1))
+    size = shape[0] // 2
+    block = pl.BlockSpec((1, size) + shape[1:], lambda k: (1, k) + (0,) * (len(shape) - 1))
+    out = pl.BlockSpec((size,) + shape[1:], lambda k: (k,) + (0,) * (len(shape) - 1))
     return pl.pallas_call(
         add_kernel,
-        grid=(shape[0],),
+        grid=(2,),
         in_specs=[block] * 4,
         out_specs=[out] * 2,
         out_shape=[jax.ShapeDtypeStruct(shape, BF16)] * 2,
@@ -967,12 +968,11 @@
     att_a_last, att_b_last = grid.by_y(a_send), grid.by_x(b_send)
     grad_got, _ = tie(grad_got, a_send)
     grad_keep, grad_got, grad_send = grid.fold_z(grad_keep, grad_got)
-    att_a_last, att_b_last, small, edges, _ = tie(
-        att_a_last, att_b_last, small, edges, grad_send
-    )
-    small = exchange(small, grid.by_x)
+    att_a_last, att_b_last, _ = tie(att_a_last, att_b_last, grad_send)
     att_keep, att_send = fold_first(att_a0, att_a_got, att_a_last, att_b0, att_b_got, att_b_last)
     att_got = grid.by_z(att_send, 1)
+    small, edges, _ = tie(small, edges, att_send)
+    small = exchange(small, grid.by_x)
     att_got, small, grad_got = tie(att_got, small, grad_got)
     small = exchange(small, grid.by_y)
     att_keep, att_got, _ = grid.fold_z(att_keep, att_got)

time: 239 us -> 234 us (0.979)
  waiting for transfers between devices: 54.6 us -> 51.3 us
  Pallas kernels: 115 us -> 112 us
    ppermute x39, waiting for transfers between devices: 54.6 us -> 51.3 us  [send(): return lax.ppermute(value, AXES, pairs)]
    pallas_call x2, Pallas kernels: 7.11 us -> 4.59 us  [add_second(): pl.pallas_call(add_kernel, grid=(2,), in_specs=[block] * 4, out_specs=[ou...]
where the time goes in v5:
time: 234 us; the launch traced here: 233 us
  Pallas kernels  112 us (48%)
  waiting for transfers between devices  51.3 us (22%)
  starting transfers between devices  38 us (16%)
  local copies, waits for them, and re-layouts  16.4 us (7%)
  other arithmetic  13.6 us (6%)
    ppermute x39, waiting for transfers between devices, send(): return lax.ppermute(value, AXES, pairs)  51.3 us
    ppermute x39, starting transfers between devices, send(): return lax.ppermute(value, AXES, pairs)  38 us
    pallas_call x2, Pallas kernels, mlp(): pl.pallas_call(functools.partial(mlp_kernel, more, count), grid=(slots,),...  34.1 us
    pallas_call x1, Pallas kernels, back(): pl.pallas_call(functools.partial(back_kernel, len(held)), grid=(slots,),...  18.8 us
    pallas_call x1, Pallas kernels, attend(): pl.pallas_call(functools.partial(attend_kernel, len(held)), grid=(slots,)...  12.9 us
    pallas_call x1, Pallas kernels, prep(): pl.pallas_call(prep_kernel, grid=(slots,), in_specs=[SMEM] + [whole(v.sha...  9.44 us
    pallas_call x1, Pallas kernels, weight_grads(): pl.pallas_call(functools.partial(weight_kernel, len(held)), grid=(wide //...  9.03 us
    unnamed x60, local copies, waits for them, and re-layouts  8.03 us
  transfers between devices with their start and end apart: 39, of which 14 were waited for; matrix products, arithmetic and copies ran while one was open for 10% of the time, Pallas kernels for 41%

profile of v5, /device:TPU:0, one launch (start us, length us, event | category | flops | bytes accessed | tf_op | source)
XLA Modules:
  0.0 232.9 jit_solution(1732314278758623986)
XLA Ops:
  0.6 4.1 %collective-permute-start = (bf16[1,96]{1,0:T(2,128)(2,1)}, bf16[1,96]{1,0:T(2,128)(2,1)S(1)}, u32[]{:S(2)}, u32[]{:S(2)}) collective-permute-start(bf16[1,96]{1,0:T(2,128)(2,1)} %bitcast.96), channel_id=1, source_target_pairs={{0,16},{1,17},{2,18},{3,19},{4,20},{5,21},{6,22},{7,23},{8,24},{9,... | collective-permute-start | bytes 584 | tf_op jit(solution)/shard_map/ppermute | solution.py:717
  19.7 2.6 %collective-permute-done.1 = bf16[2,1,48,768]{3,2,1,0:T(8,128)(2,1)S(1)} collective-permute-done((bf16[2,1,48,768]{3,2,1,0:T(8,128)(2,1)S(1)}, bf16[2,1,48,768]{3,2,1,0:T(8,128)(2,1)S(1)}, u32[]{:S(2)}, u32[]{:S(2)}) %collective-permute-start.1) | collective-permute-done | bytes 147488 | tf_op jit(solution)/shard_map/ppermute | solution.py:717
  26.8 5.8 %collective-permute-done.5 = bf16[2,2,48,768]{3,2,1,0:T(8,128)(2,1)S(1)} collective-permute-done((bf16[2,2,48,768]{3,2,1,0:T(8,128)(2,1)S(1)}, bf16[2,2,48,768]{3,2,1,0:T(8,128)(2,1)S(1)}, u32[]{:S(2)}, u32[]{:S(2)}) %collective-permute-start.5) | collective-permute-done | bytes 294944 | tf_op jit(solution)/shard_map/ppermute | solution.py:717
  32.7 2.6 %collective-permute-start.12 = (bf16[4,48,768]{2,1,0:T(8,128)(2,1)S(1)}, bf16[4,48,768]{2,1,0:T(8,128)(2,1)S(1)}, u32[]{:S(2)}, u32[]{:S(2)}) collective-permute-start(bf16[4,48,768]{2,1,0:T(8,128)(2,1)S(1)} %get-tuple-element.247), channel_id=1, source_target_pairs={{0,2},{1,3},{2,0},{3,1},{4,6},{5,7},{6,4},{7,5},{8,10},{9,11},{10,... | collective-permute-start | bytes 884744 | tf_op jit(solution)/shard_map/ppermute | solution.py:717
  36.8 9.4 %prep.1 = (bf16[1088,768]{1,0:T(8,128)(2,1)}, bf16[1088,768]{1,0:T(8,128)(2,1)}, bf16[1088,768]{1,0:T(8,128)(2,1)}, s32[1,512]{1,0:T(1,128)}, s32[1,48]{1,0:T(1,128)}) custom-call(s32[4]{0:T(128)} %pad_add_fusion.place, bf16[1040,768]{1,0:T(8,128)(2,1)} %copy-done.2, bf16[1040,768]{1,0:T(8,128)(2,1)} %collective-permute-done.4.other, ...), custom_call_target="tpu_custom_call" | custom-call | flops 1380000000 | bytes 1 | tf_op jit(solution)/shard_map/prep/pallas_call | solution.py:151
  47.3 12.9 %collective-permute-done.9 = bf16[2,2,2,48,768]{4,3,2,1,0:T(8,128)(2,1)S(1)} collective-permute-done((bf16[2,2,2,48,768]{4,3,2,1,0:T(8,128)(2,1)S(1)}, bf16[2,2,2,48,768]{4,3,2,1,0:T(8,128)(2,1)S(1)}, u32[]{:S(2)}, u32[]{:S(2)}) %collective-permute-start.9) | collective-permute-done | bytes 589856 | tf_op jit(solution)/shard_map/ppermute | solution.py:717
  63.4 12.9 %attend.1 = (bf16[2,1088,576]{2,1,0:T(8,128)(2,1)}, bf16[4,2,3,256,256]{4,3,2,1,0:T(8,128)(2,1)}, bf16[2,1088,192]{2,1,0:T(8,128)(2,1)}, bf16[1088,768]{1,0:T(8,128)(2,1)}) custom-call(s32[4]{0:T(128)} %pad_add_fusion.place, bf16[1088,768]{1,0:T(8,128)(2,1)} %get-tuple-element.144.normed, bf16[2,4,48,768]{3,2,1,0:T(8,128)(2,1)} %copy-done.1, ...), custom_call_target="tpu_custom_call" | custom-call | flops 2242500096 | bytes 1 | tf_op jit(solution)/shard_map/attend/pallas_call | solution.py:257
  81.3 17.8 %mlp.2 = (bf16[1088,768]{1,0:T(8,128)(2,1)}, bf16[1088,768]{1,0:T(8,128)(2,1)}, bf16[1088,768]{1,0:T(8,128)(2,1)}, bf16[1088,768]{1,0:T(8,128)(2,1)}, bf16[8,2,4...) custom-call(bf16[8,2,48,768]{3,2,1,0:T(8,128)(2,1)} %bitcast.74, ...), custom_call_target="tpu_custom_call" | custom-call | flops 2932499968 | bytes 1 | tf_op jit(solution)/shard_map/mlp/pallas_call | solution.py:380
  99.1 5.9 %collective-permute-done.18 = bf16[2,4,2,48,768]{4,3,2,1,0:T(8,128)(2,1)S(1)} collective-permute-done((bf16[2,4,2,48,768]{4,3,2,1,0:T(8,128)(2,1)S(1)}, bf16[2,4,2,48,768]{4,3,2,1,0:T(8,128)(2,1)S(1)}, u32[]{:S(2)}, u32[]{:S(2)}) %collective-permute-start.18) | collective-permute-done | bytes 1179680 | tf_op jit(solution)/shard_map/ppermute | solution.py:717
  106.5 16.3 %mlp.3 = (bf16[1088,768]{1,0:T(8,128)(2,1)}, bf16[1088,768]{1,0:T(8,128)(2,1)}, bf16[8,2,48,768]{3,2,1,0:T(8,128)(2,1)}, bf16[8,2,48,768]{3,2,1,0:T(8,128)(2,1)}, f32[1,768]{1,0:T(1,128)}) custom-call(bf16[8,2,48,768]{3,2,1,0:T(8,128)(2,1)} %bitcast.29.refs_0_, bf16[8,2,48,768]{3,2,1,0:T(8,128)(2,1)} %bitcast.104, ...), custom_call_target="tpu_custom_call" | custom-call | flops 2932499968 | bytes 1 | tf_op jit(solution)/shard_map/mlp/pallas_call | solution.py:380
  127.9 18.8 %back.1 = (bf16[1088,768]{1,0:T(8,128)(2,1)}, bf16[2,1088,576]{2,1,0:T(8,128)(2,1)}, bf16[1088,768]{1,0:T(8,128)(2,1)}, f32[8,768]{1,0:T(8,128)}) custom-call(s32[4]{0:T(128)} %pad_add_fusion.place, bf16[1088,768]{1,0:T(8,128)(2,1)} %get-tuple-element.155.middle, bf16[1088,768]{1,0:T(8,128)(2,1)} %get-tuple-element.160.one, bf16[1088,768]{1,0:T(8,128)(2,1)} %copy-done.3, ...), custom_call_target="tpu_custom_call" | custom-call | flops 3277499904 | bytes 1 | tf_op jit(solution)/shard_map/back/pallas_call | solution.py:582
  147.4 9.0 %weight_grads.1 = (bf16[2,4,48,768]{3,2,1,0:T(8,128)(2,1)}, bf16[2,4,48,768]{3,2,1,0:T(8,128)(2,1)}, bf16[2,4,48,768]{3,2,1,0:T(8,128)(2,1)}, bf16[2,4,48,768]{3,2,1,0:T(8,128)(2,1)}) custom-call(s32[4]{0:T(128)} %pad_add_fusion.place, bf16[1088,768]{1,0:T(8,128)(2,1)} %get-tuple-element.144.normed, bf16[1088,768]{1,0:T(8,128)(2,1)} %get-tuple-element.165.grad_proj.gm, ...), custom_call_target="tpu_custom_call" | custom-call | flops 1552499968 | bytes 1 | tf_op jit(solution)/shard_map/weight_grads/pallas_call | solution.py:641
  156.5 2.5 %add_second.2 = (bf16[4,2,48,768]{3,2,1,0:T(8,128)(2,1)}, bf16[4,2,48,768]{3,2,1,0:T(8,128)(2,1)}) custom-call(bf16[2,4,2,48,768]{4,3,2,1,0:T(8,128)(2,1)} %bitcast.76, bf16[2,4,2,48,768]{4,3,2,1,0:T(8,128)(2,1)} %collective-permute-done.22.a_got, bf16[2,4,2,48,768]{4,3,2,1,0:T(8,128)(2,1)} %bitcast.78, bf16[2,4,2,48,768]{4,3,2,1,0:T(8,128)(2,1)} %collective-permute-done.23.b_got), custom_call_target="tpu_custom_call" | custom-call | flops 6899999744 | bytes 1 | tf_op jit(solution)/shard_map/add_second/pallas_call | solution.py:416
  164.0 7.8 %last.1 = (f32[512,768]{1,0:T(8,128)}, bf16[48,768]{1,0:T(8,128)(2,1)}, f32[56,768]{1,0:T(8,128)}, f32[8,768]{1,0:T(8,128)}) custom-call(bf16[1088,768]{1,0:T(8,128)(2,1)} %get-tuple-element.148.refs_2_.x_in, bf16[1088,768]{1,0:T(8,128)(2,1)} %get-tuple-element.165.grad_proj.gm, bf16[1088,768]{1,0:T(8,128)(2,1)} %get-tuple-element.163.one, ...), custom_call_target="tpu_custom_call" | custom-call | flops 1207500032 | bytes 1 | tf_op jit(solution)/shard_map/last/pallas_call | solution.py:683
  174.2 5.7 %finish.1 = (bf16[512,768]{1,0:T(8,128)(2,1)}, bf16[48,768]{1,0:T(8,128)(2,1)}) custom-call(bf16[1088,768]{1,0:T(8,128)(2,1)} %get-tuple-element.155.middle, bf16[1088,768]{1,0:T(8,128)(2,1)} %get-tuple-element.164.one, bf16[1088,768]{1,0:T(8,128)(2,1)} %copy-done.5, s32[1,512]{1,0:T(1,128)} %get-tuple-element.177.dest_own, s32[1,48]{1,0:T(1,128)} %get-tuple-element.178.dest_halo), custom_call_target="tpu_custom_call" | custom-call | flops 862499968 | bytes 1 | tf_op jit(solution)/shard_map/finish/pallas_call | solution.py:499
  179.9 3.3 %fold_first.2 = (bf16[2,2,2,48,768]{4,3,2,1,0:T(8,128)(2,1)}, bf16[2,2,2,48,768]{4,3,2,1,0:T(8,128)(2,1)}) custom-call(bf16[2,4,2,48,768]{4,3,2,1,0:T(8,128)(2,1)} %bitcast.77, bf16[2,4,2,48,768]{4,3,2,1,0:T(8,128)(2,1)} %collective-permute-done.22.a_got, bf16[4,2,48,768]{3,2,1,0:T(8,128)(2,1)} %collective-permute-done.27.a_last, ...), custom_call_target="tpu_custom_call" | custom-call | flops 517500000 | bytes 1 | tf_op jit(solution)/shard_map/fold_first/pallas_call | solution.py:466
  184.7 2.6 %collective-permute-done.24.a_got = bf16[2,4,48,768]{3,2,1,0:T(8,128)(2,1)} collective-permute-done((bf16[2,4,48,768]{3,2,1,0:T(8,128)(2,1)}, bf16[2,4,48,768]{3,2,1,0:T(8,128)(2,1)}, u32[]{:S(2)}, u32[]{:S(2)}) %collective-permute-start.24) | collective-permute-done | bytes 589856 | tf_op jit(solution)/shard_map/ppermute | solution.py:717
  188.5 2.1 add_second.3
  193.3 5.2 %collective-permute-done.29 = bf16[62,768]{1,0:T(8,128)(2,1)S(1)} collective-permute-done((bf16[62,768]{1,0:T(8,128)(2,1)S(1)}, bf16[62,768]{1,0:T(8,128)(2,1)S(1)}, u32[]{:S(2)}, u32[]{:S(2)}) %collective-permute-start.29) | collective-permute-done | bytes 95264 | tf_op jit(solution)/shard_map/ppermute | solution.py:717
  200.4 2.1 sum_split.2
  202.5 2.3 collective-permute-start.36
  206.3 2.4 %fold_first.3 = (bf16[2,2,48,768]{3,2,1,0:T(8,128)(2,1)}, bf16[2,2,48,768]{3,2,1,0:T(8,128)(2,1)}) custom-call(bf16[2,4,48,768]{3,2,1,0:T(8,128)(2,1)} %get-tuple-element.171.a_zero, bf16[2,4,48,768]{3,2,1,0:T(8,128)(2,1)} %collective-permute-done.24.a_got, bf16[4,48,768]{2,1,0:T(8,128)(2,1)} %copy-done.11, ...), custom_call_target="tpu_custom_call" | custom-call | flops 517500000 | bytes 1 | tf_op jit(solution)/shard_map/fold_first/pallas_call | solution.py:466
  216.5 4.5 %collective-permute-done.34.refs_1_ = bf16[2,2,48,768]{3,2,1,0:T(8,128)(2,1)S(1)} collective-permute-done((bf16[2,2,48,768]{3,2,1,0:T(8,128)(2,1)}, bf16[2,2,48,768]{3,2,1,0:T(8,128)(2,1)S(1)}, u32[]{:S(2)}, u32[]{:S(2)}) %collective-permute-start.34) | collective-permute-done | bytes 294944 | tf_op jit(solution)/shard_map/ppermute | solution.py:717
  227.6 3.4 %collective-permute-done.38 = bf16[1,2,48,768]{3,2,1,0:T(8,128)(2,1)S(1)} collective-permute-done((bf16[1,2,48,768]{3,2,1,0:T(8,128)(2,1)}, bf16[1,2,48,768]{3,2,1,0:T(8,128)(2,1)S(1)}, u32[]{:S(2)}, u32[]{:S(2)}) %collective-permute-start.38) | collective-permute-done | bytes 147488 | tf_op jit(solution)/shard_map/ppermute | solution.py:717
  (203 shorter events, 69.3 us)
Async XLA Ops:
  9.3 13.1 %collective-permute-start.4 = (bf16[1040,768]{1,0:T(8,128)(2,1)S(1)}, bf16[1040,768]{1,0:T(8,128)(2,1)}, u32[]{:S(2)}, u32[]{:S(2)}) collective-permute-start(bf16[1040,768]{1,0:T(8,128)(2,1)S(1)} %fusion.1.own), channel_id=1, source_target_pairs={{0,1},{1,0},{2,3},{3,2},{4,5},{5,4},{6,7},{7,6},{8,9},{9,8},{10,11... | collective-permute-start | bytes 4792328 | tf_op jit(solution)/shard_map/ppermute | solution.py:717
  25.8 20.5 %collective-permute-start.3 = (bf16[2,1,2,48,768]{4,3,2,1,0:T(8,128)(2,1)S(1)}, bf16[2,1,2,48,768]{4,3,2,1,0:T(8,128)(2,1)S(1)}, u32[]{:S(2)}, u32[]{:S(2)}) collective-permute-start(bf16[2,1,2,48,768]{4,3,2,1,0:T(8,128)(2,1)S(1)} %bitcast.68), channel_id=1, source_target_pairs={{0,16},{1,17},{2,18},{3,19},{4,20},{5,21},{6,22},{7,23},{8,24},{9,... | collective-permute-start | bytes 884744 | tf_op jit(solution)/shard_map/ppermute | solution.py:717
  32.7 13.7 %collective-permute-start.12 = (bf16[4,48,768]{2,1,0:T(8,128)(2,1)S(1)}, bf16[4,48,768]{2,1,0:T(8,128)(2,1)S(1)}, u32[]{:S(2)}, u32[]{:S(2)}) collective-permute-start(bf16[4,48,768]{2,1,0:T(8,128)(2,1)S(1)} %get-tuple-element.247), channel_id=1, source_target_pairs={{0,2},{1,3},{2,0},{3,1},{4,6},{5,7},{6,4},{7,5},{8,10},{9,11},{10,... | collective-permute-start | bytes 884744 | tf_op jit(solution)/shard_map/ppermute | solution.py:717
  46.3 13.9 %collective-permute-start.9 = (bf16[2,2,2,48,768]{4,3,2,1,0:T(8,128)(2,1)S(1)}, bf16[2,2,2,48,768]{4,3,2,1,0:T(8,128)(2,1)S(1)}, u32[]{:S(2)}, u32[]{:S(2)}) collective-permute-start(bf16[2,2,2,48,768]{4,3,2,1,0:T(8,128)(2,1)S(1)} %pad_maximum_fusion.4), channel_id=1, source_target_pairs={{0,8},{1,9},{2,10},{3,11},{4,12},{5,13},{6,14},{7,15},{8,0},{9,1},... | collective-permute-start | bytes 1769480 | tf_op jit(solution)/shard_map/ppermute | solution.py:717
  46.5 15.2 %collective-permute-start.15 = (bf16[2,4,48,768]{3,2,1,0:T(8,128)(2,1)S(1)}, bf16[2,4,48,768]{3,2,1,0:T(8,128)(2,1)S(1)}, u32[]{:S(2)}, u32[]{:S(2)}) collective-permute-start(bf16[2,4,48,768]{3,2,1,0:T(8,128)(2,1)S(1)} %pad_maximum_fusion.6.refs_2_), channel_id=1, source_target_pairs={{0,2},{1,3},{2,0},{3,1},{4,6},{5,7},{6,4},{7,5},{8,10},{9,11},{10,... | collective-permute-start | bytes 1769480 | tf_op jit(solution)/shard_map/ppermute | solution.py:717
  46.7 15.0 %collective-permute-start.14 = (bf16[2,4,48,768]{3,2,1,0:T(8,128)(2,1)S(1)}, bf16[2,4,48,768]{3,2,1,0:T(8,128)(2,1)S(1)}, u32[]{:S(2)}, u32[]{:S(2)}) collective-permute-start(bf16[2,4,48,768]{3,2,1,0:T(8,128)(2,1)S(1)} %pad_maximum_fusion.5.refs_0_), channel_id=1, source_target_pairs={{0,4},{1,5},{2,6},{3,7},{4,0},{5,1},{6,2},{7,3},{8,12},{9,13},{10,... | collective-permute-start | bytes 1769480 | tf_op jit(solution)/shard_map/ppermute | solution.py:717
  60.6 15.8 %collective-permute-start.10 = (bf16[4,2,48,768]{3,2,1,0:T(8,128)(2,1)S(1)}, bf16[4,2,48,768]{3,2,1,0:T(8,128)(2,1)S(1)}, u32[]{:S(2)}, u32[]{:S(2)}) collective-permute-start(bf16[4,2,48,768]{3,2,1,0:T(8,128)(2,1)S(1)} %get-tuple-element.241), channel_id=1, source_target_pairs={{0,2},{1,3},{2,0},{3,1},{4,6},{5,7},{6,4},{7,5},{8,10},{9,11},{10,... | collective-permute-start | bytes 1769480 | tf_op jit(solution)/shard_map/ppermute | solution.py:717
  61.1 15.4 %collective-permute-start.11 = (bf16[4,2,48,768]{3,2,1,0:T(8,128)(2,1)S(1)}, bf16[4,2,48,768]{3,2,1,0:T(8,128)(2,1)S(1)}, u32[]{:S(2)}, u32[]{:S(2)}) collective-permute-start(bf16[4,2,48,768]{3,2,1,0:T(8,128)(2,1)S(1)} %get-tuple-element.242), channel_id=1, source_target_pairs={{0,4},{1,5},{2,6},{3,7},{4,0},{5,1},{6,2},{7,3},{8,12},{9,13},{10,... | collective-permute-start | bytes 1769480 | tf_op jit(solution)/shard_map/ppermute | solution.py:717
  76.6 28.4 %collective-permute-start.18 = (bf16[2,4,2,48,768]{4,3,2,1,0:T(8,128)(2,1)S(1)}, bf16[2,4,2,48,768]{4,3,2,1,0:T(8,128)(2,1)S(1)}, u32[]{:S(2)}, u32[]{:S(2)}) collective-permute-start(bf16[2,4,2,48,768]{4,3,2,1,0:T(8,128)(2,1)S(1)} %pad_maximum_fusion.2), channel_id=1, source_target_pairs={{0,2},{1,3},{2,0},{3,1},{4,6},{5,7},{6,4},{7,5},{8,10},{9,11},{10,... | collective-permute-start | bytes 3538952 | tf_op jit(solution)/shard_map/ppermute | solution.py:717
  78.3 28.2 %collective-permute-start.17 = (bf16[2,4,2,48,768]{4,3,2,1,0:T(8,128)(2,1)S(1)}, bf16[2,4,2,48,768]{4,3,2,1,0:T(8,128)(2,1)}, u32[]{:S(2)}, u32[]{:S(2)}) collective-permute-start(bf16[2,4,2,48,768]{4,3,2,1,0:T(8,128)(2,1)S(1)} %pad_maximum_fusion.1), channel_id=1, source_target_pairs={{0,4},{1,5},{2,6},{3,7},{4,0},{5,1},{6,2},{7,3},{8,12},{9,13},{10,... | collective-permute-start | bytes 3538952 | tf_op jit(solution)/shard_map/ppermute | solution.py:717
  123.0 33.5 %collective-permute-start.23 = (bf16[2,4,2,48,768]{4,3,2,1,0:T(8,128)(2,1)}, bf16[2,4,2,48,768]{4,3,2,1,0:T(8,128)(2,1)}, u32[]{:S(2)}, u32[]{:S(2)}) collective-permute-start(bf16[2,4,2,48,768]{4,3,2,1,0:T(8,128)(2,1)} %bitcast.103), channel_id=1, source_target_pairs={{0,2},{1,3},{2,0},{3,1},{4,6},{5,7},{6,4},{7,5},{8,10},{9,11},{10,... | collective-permute-start | bytes 3538952 | tf_op jit(solution)/shard_map/ppermute | solution.py:717
  124.1 32.4 %collective-permute-start.22 = (bf16[2,4,2,48,768]{4,3,2,1,0:T(8,128)(2,1)}, bf16[2,4,2,48,768]{4,3,2,1,0:T(8,128)(2,1)}, u32[]{:S(2)}, u32[]{:S(2)}) collective-permute-start(bf16[2,4,2,48,768]{4,3,2,1,0:T(8,128)(2,1)} %bitcast.102), channel_id=1, source_target_pairs={{0,4},{1,5},{2,6},{3,7},{4,0},{5,1},{6,2},{7,3},{8,12},{9,13},{10,... | collective-permute-start | bytes 3538952 | tf_op jit(solution)/shard_map/ppermute | solution.py:717
  146.7 15.4 %collective-permute-start.21 = (bf16[1088,768]{1,0:T(8,128)(2,1)}, bf16[1088,768]{1,0:T(8,128)(2,1)}, u32[]{:S(2)}, u32[]{:S(2)}) collective-permute-start(bf16[1088,768]{1,0:T(8,128)(2,1)} %get-tuple-element.163.one), channel_id=1, source_target_pairs={{0,1},{1,0},{2,3},{3,2},{4,5},{5,4},{6,7},{7,6},{8,9},{9,8},{10,11... | collective-permute-start | bytes 5013512 | tf_op jit(solution)/shard_map/ppermute | solution.py:717
  146.9 25.8 %collective-permute-start.20 = (bf16[1088,768]{1,0:T(8,128)(2,1)S(1)}, bf16[1088,768]{1,0:T(8,128)(2,1)S(1)}, u32[]{:S(2)}, u32[]{:S(2)}) collective-permute-start(bf16[1088,768]{1,0:T(8,128)(2,1)S(1)} %copy-done.4), channel_id=1, source_target_pairs={{0,1},{1,0},{2,3},{3,2},{4,5},{5,4},{6,7},{7,6},{8,9},{9,8},{10,11... | collective-permute-start | bytes 5013512 | tf_op jit(solution)/shard_map/ppermute | solution.py:717
  159.0 20.9 %collective-permute-start.28 = (bf16[4,2,48,768]{3,2,1,0:T(8,128)(2,1)}, bf16[4,2,48,768]{3,2,1,0:T(8,128)(2,1)}, u32[]{:S(2)}, u32[]{:S(2)}) collective-permute-start(bf16[4,2,48,768]{3,2,1,0:T(8,128)(2,1)} %get-tuple-element.185), channel_id=1, source_target_pairs={{0,4},{1,5},{2,6},{3,7},{4,0},{5,1},{6,2},{7,3},{8,12},{9,13},{10,... | collective-permute-start | bytes 1769480 | tf_op jit(solution)/shard_map/ppermute | solution.py:717
  160.5 19.4 %collective-permute-start.27 = (bf16[4,2,48,768]{3,2,1,0:T(8,128)(2,1)}, bf16[4,2,48,768]{3,2,1,0:T(8,128)(2,1)}, u32[]{:S(2)}, u32[]{:S(2)}) collective-permute-start(bf16[4,2,48,768]{3,2,1,0:T(8,128)(2,1)} %get-tuple-element.175), channel_id=1, source_target_pairs={{0,2},{1,3},{2,0},{3,1},{4,6},{5,7},{6,4},{7,5},{8,10},{9,11},{10,... | collective-permute-start | bytes 1769480 | tf_op jit(solution)/shard_map/ppermute | solution.py:717
  161.5 25.8 %collective-permute-start.24 = (bf16[2,4,48,768]{3,2,1,0:T(8,128)(2,1)}, bf16[2,4,48,768]{3,2,1,0:T(8,128)(2,1)}, u32[]{:S(2)}, u32[]{:S(2)}) collective-permute-start(bf16[2,4,48,768]{3,2,1,0:T(8,128)(2,1)} %get-tuple-element.183), channel_id=1, source_target_pairs={{0,4},{1,5},{2,6},{3,7},{4,0},{5,1},{6,2},{7,3},{8,12},{9,13},{10,... | collective-permute-start | bytes 1769480 | tf_op jit(solution)/shard_map/ppermute | solution.py:717
  162.1 26.4 %collective-permute-start.25 = (bf16[2,4,48,768]{3,2,1,0:T(8,128)(2,1)}, bf16[2,4,48,768]{3,2,1,0:T(8,128)(2,1)}, u32[]{:S(2)}, u32[]{:S(2)}) collective-permute-start(bf16[2,4,48,768]{3,2,1,0:T(8,128)(2,1)} %get-tuple-element.186), channel_id=1, source_target_pairs={{0,2},{1,3},{2,0},{3,1},{4,6},{5,7},{6,4},{7,5},{8,10},{9,11},{10,... | collective-permute-start | bytes 1769480 | tf_op jit(solution)/shard_map/ppermute | solution.py:717
  183.2 16.4 %collective-permute-start.33 = (bf16[2,2,2,48,768]{4,3,2,1,0:T(8,128)(2,1)}, bf16[2,2,2,48,768]{4,3,2,1,0:T(8,128)(2,1)S(1)}, u32[]{:S(2)}, u32[]{:S(2)}) collective-permute-start(bf16[2,2,2,48,768]{4,3,2,1,0:T(8,128)(2,1)} %get-tuple-element.195), channel_id=1, source_target_pairs={{0,8},{1,9},{2,10},{3,11},{4,12},{5,13},{6,14},{7,15},{8,0},{9,1},... | collective-permute-start | bytes 1769480 | tf_op jit(solution)/shard_map/ppermute | solution.py:717
  190.6 14.2 %collective-permute-start.32 = (bf16[4,48,768]{2,1,0:T(8,128)(2,1)}, bf16[4,48,768]{2,1,0:T(8,128)(2,1)S(1)}, u32[]{:S(2)}, u32[]{:S(2)}) collective-permute-start(bf16[4,48,768]{2,1,0:T(8,128)(2,1)} %get-tuple-element.201), channel_id=1, source_target_pairs={{0,4},{1,5},{2,6},{3,7},{4,0},{5,1},{6,2},{7,3},{8,12},{9,13},{10,... | collective-permute-start | bytes 884744 | tf_op jit(solution)/shard_map/ppermute | solution.py:717
  191.2 13.7 %collective-permute-start.31 = (bf16[4,48,768]{2,1,0:T(8,128)(2,1)}, bf16[4,48,768]{2,1,0:T(8,128)(2,1)S(1)}, u32[]{:S(2)}, u32[]{:S(2)}) collective-permute-start(bf16[4,48,768]{2,1,0:T(8,128)(2,1)} %get-tuple-element.200), channel_id=1, source_target_pairs={{0,2},{1,3},{2,0},{3,1},{4,6},{5,7},{6,4},{7,5},{8,10},{9,11},{10,... | collective-permute-start | bytes 884744 | tf_op jit(solution)/shard_map/ppermute | solution.py:717
  192.2 16.5 %collective-permute-start.30 = (bf16[96,768]{1,0:T(8,128)(2,1)S(1)}, bf16[96,768]{1,0:T(8,128)(2,1)S(1)}, u32[]{:S(2)}, u32[]{:S(2)}) collective-permute-start(bf16[96,768]{1,0:T(8,128)(2,1)S(1)} %pad_maximum_fusion.10), channel_id=1, source_target_pairs={{0,2},{1,3},{2,0},{3,1},{4,6},{5,7},{6,4},{7,5},{8,10},{9,11},{10,... | collective-permute-start | bytes 442376 | tf_op jit(solution)/shard_map/ppermute | solution.py:717
  202.5 18.5 %collective-permute-start.36 = (bf16[1,2,2,48,768]{4,3,2,1,0:T(8,128)(2,1)}, bf16[1,2,2,48,768]{4,3,2,1,0:T(8,128)(2,1)S(1)}, u32[]{:S(2)}, u32[]{:S(2)}) collective-permute-start(bf16[1,2,2,48,768]{4,3,2,1,0:T(8,128)(2,1)} %get-tuple-element.204), channel_id=1, source_target_pairs={{0,16},{1,17},{2,18},{3,19},{4,20},{5,21},{6,22},{7,23},{8,24},{9,... | collective-permute-start | bytes 884744 | tf_op jit(solution)/shard_map/ppermute | solution.py:717
  208.7 12.4 %collective-permute-start.34 = (bf16[2,2,48,768]{3,2,1,0:T(8,128)(2,1)}, bf16[2,2,48,768]{3,2,1,0:T(8,128)(2,1)S(1)}, u32[]{:S(2)}, u32[]{:S(2)}) collective-permute-start(bf16[2,2,48,768]{3,2,1,0:T(8,128)(2,1)} %get-tuple-element.207), channel_id=1, source_target_pairs={{0,8},{1,9},{2,10},{3,11},{4,12},{5,13},{6,14},{7,15},{8,0},{9,1},... | collective-permute-start | bytes 884744 | tf_op jit(solution)/shard_map/ppermute | solution.py:717
  (43 other events, 277.7 us)

commit v6 on v5

--- a/solution.py
+++ b/solution.py
@@ -35,8 +35,8 @@
     return pl.BlockSpec(shape, lambda *_: (0,) * len(shape))
 
 
-def params(**more):
-    return pltpu.CompilerParams(vmem_limit_bytes=VMEM_LIMIT, **more)
+def params(limit=VMEM_LIMIT):
+    return pltpu.CompilerParams(vmem_limit_bytes=limit)
 
 
 SCALE = 0.15
@@ -63,11 +63,43 @@
     return inverse * (inner - first - hat * second)
 
 
+def pick_rows(step, sources, block):
+    total = None
+    for dest, ref in sources:
+        size = dest.shape[1]
+        at = step * SLOT + lax.broadcasted_iota(jnp.int32, (SLOT, size), 0)
+        part = dot((at == dest[...]).astype(BF16), ref[block * size : (block + 1) * size])
+        total = part if total is None else total + part
+    return total
+
+
+def prep_cot_kernel(own, other, halo, dest_own, dest_other, dest_halo, out):
+    sources = ((dest_own, own), (dest_other, other), (dest_halo, halo))
+    out[...] = pick_rows(pl.program_id(0), sources, 0).astype(BF16)
+
+
+def prep_cot(own, other, halo, dest_own, dest_other, dest_halo, slots):
+    count, wide = dest_own.shape[1], own.shape[1]
+    rows = slots * SLOT
+    second = [pl.BlockSpec((size, wide), lambda t: (1, 0)) for size in (count, count, HALO)]
+    dests = (dest_own, dest_other, dest_halo)
+    return pl.pallas_call(
+        prep_cot_kernel,
+        grid=(slots,),
+        in_specs=second + [whole(v.shape) for v in dests],
+        out_specs=pl.BlockSpec((SLOT, wide), lambda t: (t, 0)),
+        out_shape=jax.ShapeDtypeStruct((rows, wide), BF16),
+        compiler_params=params(24 * 1024 * 1024),
+        cost_estimate=cost(5),
+        name="prep_cot",
+    )(own, other, halo, *dests)
+
+
 def prep_kernel(
-    place, own, other, halo, prom, norms, x_out, n_out, cot_out, dest_own, dest_halo, d_oth
+    place, own, other, halo, prom, norms, x_out, n_out, dest_own, dest_other, dest_halo
 ):
     step = pl.program_id(0)
-    count = d_oth.shape[1]
+    count = dest_own.shape[1]
     slots = pl.num_programs(0)
     y_at, c_at = place[2], place[3]
 
@@ -115,22 +147,10 @@
                 dest = jnp.where(live, dest, spare)
             results.append(dest)
         dest_own[...] = results[0]
-        d_oth[...] = results[1]
+        dest_other[...] = results[1]
         dest_halo[...] = results[2]
 
-    rows = step * SLOT
-    tokens = cots = None
-    for dest, ref, size in (
-        (dest_own, own, count),
-        (d_oth, other, count),
-        (dest_halo, halo, HALO),
-    ):
-        at = rows + lax.broadcasted_iota(jnp.int32, (SLOT, size), 0)
-        pick = (at == dest[...]).astype(BF16)
-        one = dot(pick, ref[0:size])
-        two = dot(pick, ref[size : 2 * size])
-        tokens = one if tokens is None else tokens + one
-        cots = two if cots is None else cots + two
+    tokens = pick_rows(step, ((dest_own, own), (dest_other, other), (dest_halo, halo)), 0)
     at = lax.broadcasted_iota(jnp.int32, (SLOT, 1), 0)
     slot_row = lax.broadcasted_iota(jnp.int32, (SLOT, PROMPTS), 0)
     which = lax.broadcasted_iota(jnp.int32, (SLOT, PROMPTS), 1)
@@ -139,7 +159,6 @@
     hat, _ = stats(inputs)
     x_out[...] = inputs.astype(BF16)
     n_out[...] = (hat * norms[0:1] + norms[1:2]).astype(BF16)
-    cot_out[...] = cots.astype(BF16)
 
 
 def prep(place, own, other, halo, prom, norms, slots):
@@ -152,16 +171,10 @@
         prep_kernel,
         grid=(slots,),
         in_specs=[SMEM] + [whole(v.shape) for v in (own, other, halo, prom, norms)],
-        out_specs=[tile, tile, tile, whole((1, count)), whole((1, HALO))],
-        out_shape=[
-            array,
-            array,
-            array,
-            jax.ShapeDtypeStruct((1, count), jnp.int32),
-            jax.ShapeDtypeStruct((1, HALO), jnp.int32),
-        ],
-        scratch_shapes=[pltpu.VMEM((1, count), jnp.int32)],
-        compiler_params=params(),
+        out_specs=[tile, tile] + [whole((1, size)) for size in (count, count, HALO)],
+        out_shape=[array, array]
+        + [jax.ShapeDtypeStruct((1, size), jnp.int32) for size in (count, count, HALO)],
+        compiler_params=params(24 * 1024 * 1024),
         cost_estimate=cost(8),
         name="prep",
     )(place, own, other, halo, prom, norms)
@@ -291,7 +304,7 @@
     step = pl.program_id(0)
     _, pieces, span, wide = weight.shape
     hidden = pieces * span
-    cut = 384
+    cut = 768
     spots = []
     for ref in parts:
         spots.append(sum(size for _, size in spots))
@@ -419,7 +432,7 @@
         in_specs=[block] * 4,
         out_specs=[out] * 2,
         out_shape=[jax.ShapeDtypeStruct(shape, BF16)] * 2,
-        compiler_params=params(),
+        compiler_params=params(24 * 1024 * 1024),
         cost_estimate=cost(time),
         name="add_second",
     )(a_zero, a_got, b_zero, b_got)
@@ -444,7 +457,7 @@
         in_specs=[whole(shape)] * len(values),
         out_specs=[whole(half)] * 2,
         out_shape=[jax.ShapeDtypeStruct(half, BF16)] * 2,
-        compiler_params=params(),
+        compiler_params=params(24 * 1024 * 1024),
         cost_estimate=cost(2),
         name="sum_split",
     )(*values)
@@ -469,7 +482,7 @@
         in_specs=[first, first, whole(shape)] * 2,
         out_specs=[whole(out)] * 2,
         out_shape=[jax.ShapeDtypeStruct(out, BF16)] * 2,
-        compiler_params=params(),
+        compiler_params=params(24 * 1024 * 1024),
         cost_estimate=cost(3),
         name="fold_first",
     )(a_zero, a_got, a_last, b_zero, b_got, b_last)
@@ -506,7 +519,7 @@
             jax.ShapeDtypeStruct((HALO, wide), BF16),
         ],
         scratch_shapes=[pltpu.VMEM((rows, wide), BF16)],
-        compiler_params=params(),
+        compiler_params=params(24 * 1024 * 1024),
         cost_estimate=cost(5),
         name="finish",
     )(middle, one, two, dest_own, dest_halo)
@@ -692,7 +705,7 @@
             jax.ShapeDtypeStruct((8, wide), F32),
         ],
         scratch_shapes=[pltpu.VMEM((rows, wide), BF16)],
-        compiler_params=params(),
+        compiler_params=params(24 * 1024 * 1024),
         cost_estimate=cost(7),
         name="last",
     )(x_in, gm, one, two, norms, dest_own, dest_halo)
@@ -834,12 +847,6 @@
         [up_weight.swapaxes(0, 1).reshape(2, span, wide), down_weight.reshape(2, span, wide)],
         axis=1,
     )
-    bias, first = grid.gather_z(up_bias.reshape(1, hidden), 0)
-    shard = after(shard, first)
-    got, first = grid.gather_z(shard, 1, bias)
-    bias = jnp.stack([bias, grid.by_x(bias)])
-    bias = jnp.stack([bias, grid.by_y(bias)])
-
     code = ((segment % IMGS_ROW) * 2 + live_token).astype(BF16)
     marks = jnp.pad(code[None], ((0, 15), (0, wide - count)))
     own = after(jnp.concatenate([tokens, cotangent, marks]), shard)
@@ -861,12 +868,19 @@
     edge = jnp.concatenate(edge_parts)
     halo = grid.by_y(edge)
 
-    got, bias, halo = tie(got, bias, halo)
+    bias, first = grid.gather_z(up_bias.reshape(1, hidden), 0)
+    got, first = grid.gather_z(after(shard, first), 1, bias, halo)
+    bias = jnp.stack([bias, grid.by_x(bias)])
+    bias = jnp.stack([bias, grid.by_y(bias)])
+    x_in, normed, *dests = prep(place, own, other, halo, prompts, norms, slots)
+    dest_own, _, dest_halo = dests
+    got, bias, _ = tie(got, bias, normed)
     a_zero, b_zero = grid.spread(got[0], got[1])
     a_one, b_one = grid.spread_more(a_zero, b_zero)
-    x_in, normed, cot, dest_own, dest_halo = prep(place, own, other, halo, prompts, norms, slots)
-
-    held, _ = grid.gather_z(after(halves, first)[:, None], 1, normed)
+    cot = prep_cot(own, other, after(halo, a_zero), *dests, slots)
+
+    held, _ = grid.gather_z(after(halves, first)[:, None], 1)
+    held, a_one, b_one = tie(held, a_one, b_one)
     mlp_a, mlp_b = held[0], held[1]
     mlp_a0, mlp_b0 = grid.spread(mlp_a, mlp_b)
     mlp_a1, mlp_b1 = grid.spread_more(mlp_a0, mlp_b0)
@@ -884,6 +898,7 @@
         ).reshape(2, 2, deep, depth, 4 * third)
         blocks = grid.to_absolute(blocks, 2, 1).swapaxes(1, 2)
         weights = [blocks.reshape(2, 2 * deep * depth, 4 * third)]
+    normed, cot = tie(normed, cot)
     qkv, prob, att, part = attend(place, normed, weights, slots)
 
     fine = span % 16 == 0

time: 234 us -> 225 us (0.962)
  Pallas kernels: 112 us -> 98.9 us
  starting transfers between devices: 38 us -> 42.7 us
  local copies, waits for them, and re-layouts: 16.4 us -> 19.9 us
    ppermute x39, starting transfers between devices: 38 us -> 42.7 us  [send(): return lax.ppermute(value, AXES, pairs)]
    pallas_call x1, Pallas kernels: 9.44 us -> 5.1 us  [prep(): pl.pallas_call(prep_kernel, grid=(slots,), in_specs=[SMEM] + [whole(v.sha...]
    unnamed x60 -> x82, local copies, waits for them, and re-layouts: 8.03 us -> 12.3 us
    pallas_call x2, Pallas kernels: 3.93 us -> 0.21 us  [sum_split(): pl.pallas_call(functools.partial(split_kernel, len(values)), grid=(1,), i...]
    pallas_call x0 -> x1, Pallas kernels: none -> 2.95 us  [prep_cot(): pl.pallas_call(prep_cot_kernel, grid=(slots,), in_specs=second + [whole(v...]
    pallas_call x2, Pallas kernels: 5.71 us -> 3.02 us  [fold_first(): pl.pallas_call(fold_kernel, grid=(1,), in_specs=[first, first, whole(shap...]
  transfers between devices with their start and end apart: 39 -> 39, of which waited for: 14 -> 22; matrix products, arithmetic and copies ran while one was open for 10% -> 7% of each run, Pallas kernels for 41% -> 37%
where the time goes in v6:
time: 225 us; the launch traced here: 224 us
  Pallas kernels  98.9 us (44%)
  waiting for transfers between devices  49.7 us (22%)
  starting transfers between devices  42.7 us (19%)
  local copies, waits for them, and re-layouts  19.9 us (9%)
  other arithmetic  11.3 us (5%)
    ppermute x39, waiting for transfers between devices, send(): return lax.ppermute(value, AXES, pairs)  49.7 us
    ppermute x39, starting transfers between devices, send(): return lax.ppermute(value, AXES, pairs)  42.7 us
    pallas_call x2, Pallas kernels, mlp(): pl.pallas_call(functools.partial(mlp_kernel, more, count), grid=(slots,),...  33.2 us
    pallas_call x1, Pallas kernels, back(): pl.pallas_call(functools.partial(back_kernel, len(held)), grid=(slots,),...  18.7 us
    pallas_call x1, Pallas kernels, attend(): pl.pallas_call(functools.partial(attend_kernel, len(held)), grid=(slots,)...  12.8 us
    unnamed x82, local copies, waits for them, and re-layouts  12.3 us
    pallas_call x1, Pallas kernels, weight_grads(): pl.pallas_call(functools.partial(weight_kernel, len(held)), grid=(wide //...  9.25 us
    pallas_call x1, Pallas kernels, finish(): pl.pallas_call(finish_kernel, grid=(slots,), in_specs=[tile, tile, tile,...  5.7 us
  transfers between devices with their start and end apart: 39, of which 22 were waited for; matrix products, arithmetic and copies ran while one was open for 7% of the time, Pallas kernels for 37%

profile of v6, /device:TPU:0, one launch (start us, length us, event | category | flops | bytes accessed | tf_op | source)
XLA Modules:
  0.0 224.0 jit_solution(5607099921995312054)
XLA Ops:
  5.5 3.7 %collective-permute-start = (bf16[1,96]{1,0:T(2,128)(2,1)S(1)}, bf16[1,96]{1,0:T(2,128)(2,1)S(1)}, u32[]{:S(2)}, u32[]{:S(2)}) collective-permute-start(bf16[1,96]{1,0:T(2,128)(2,1)S(1)} %bitcast.96), channel_id=1, source_target_pairs={{0,16},{1,17},{2,18},{3,19},{4,20},{5,21},{6,22},{7,23},{8,24},{9,... | collective-permute-start | bytes 584 | tf_op jit(solution)/shard_map/ppermute | solution.py:730
  12.7 2.6 %collective-permute-start.1 = (bf16[2,1,48,768]{3,2,1,0:T(8,128)(2,1)S(1)}, bf16[2,1,48,768]{3,2,1,0:T(8,128)(2,1)S(1)}, u32[]{:S(2)}, u32[]{:S(2)}) collective-permute-start(bf16[2,1,48,768]{3,2,1,0:T(8,128)(2,1)S(1)} %pad_maximum_fusion.9), channel_id=1, source_target_pairs={{0,16},{1,17},{2,18},{3,19},{4,20},{5,21},{6,22},{7,23},{8,24},{9,... | collective-permute-start | bytes 442376 | tf_op jit(solution)/shard_map/ppermute | solution.py:730
  23.6 2.7 %collective-permute-start.5 = (bf16[2,1,2,48,768]{4,3,2,1,0:T(8,128)(2,1)}, bf16[2,1,2,48,768]{4,3,2,1,0:T(8,128)(2,1)S(1)}, u32[]{:S(2)}, u32[]{:S(2)}) collective-permute-start(bf16[2,1,2,48,768]{4,3,2,1,0:T(8,128)(2,1)} %bitcast.72), channel_id=1, source_target_pairs={{0,16},{1,17},{2,18},{3,19},{4,20},{5,21},{6,22},{7,23},{8,24},{9,... | collective-permute-start | bytes 884744 | tf_op jit(solution)/shard_map/ppermute | solution.py:730
  26.3 5.1 %prep.1 = (bf16[1088,768]{1,0:T(8,128)(2,1)S(1)}, bf16[1088,768]{1,0:T(8,128)(2,1)S(1)}, s32[1,512]{1,0:T(1,128)S(1)}, s32[1,512]{1,0:T(1,128)S(1)}, s32[1,48]{1,0:T(1,128)S(1)}) custom-call(s32[4]{0:T(128)S(1)} %pad_add_fusion.place, bf16[1040,768]{1,0:T(8,128)(2,1)S(1)} %fusion.1.own, bf16[1040,768]{1,0:T(8,128)(2,1)S(1)} %collective-permute-done.3.other, ...), custom_call_target="tpu_custom_call" | custom-call | flops 1380000000 | bytes 1 | tf_op jit(solution)/shard_map/prep/pallas_call | solution.py:170
  31.5 4.1 %collective-permute-done.7 = bf16[2,2,48,768]{3,2,1,0:T(8,128)(2,1)S(1)} collective-permute-done((bf16[2,2,48,768]{3,2,1,0:T(8,128)(2,1)S(1)}, bf16[2,2,48,768]{3,2,1,0:T(8,128)(2,1)S(1)}, u32[]{:S(2)}, u32[]{:S(2)}) %collective-permute-start.7) | collective-permute-done | bytes 294944 | tf_op jit(solution)/shard_map/ppermute | solution.py:730
  39.1 4.5 %collective-permute-done.10 = bf16[4,48,768]{2,1,0:T(8,128)(2,1)S(1)} collective-permute-done((bf16[4,48,768]{2,1,0:T(8,128)(2,1)S(1)}, bf16[4,48,768]{2,1,0:T(8,128)(2,1)S(1)}, u32[]{:S(2)}, u32[]{:S(2)}) %collective-permute-start.10) | collective-permute-done | bytes 294944 | tf_op jit(solution)/shard_map/ppermute | solution.py:730
  47.2 2.9 %prep_cot.1.refs_6_.refs_3_.cot = bf16[1088,768]{1,0:T(8,128)(2,1)S(1)} custom-call(bf16[1040,768]{1,0:T(8,128)(2,1)S(1)} %fusion.1.own, bf16[1040,768]{1,0:T(8,128)(2,1)S(1)} %collective-permute-done.3.other, bf16[112,768]{1,0:T(8,128)(2,1)S(1)} %collective-permute-done.4.halo, s32[1,512]{1,0:T(1,128)S(1)} %get-tuple-element.156.dest_own, ...), custom_call_target="tpu_custom_call" | custom-call | flops 862499968 | bytes 1 | tf_op jit(solution)/shard_map/prep_cot/pallas_call | solution.py:86
  50.1 2.7 %collective-permute-done.6 = bf16[2,2,2,48,768]{4,3,2,1,0:T(8,128)(2,1)S(1)} collective-permute-done((bf16[2,2,2,48,768]{4,3,2,1,0:T(8,128)(2,1)S(1)}, bf16[2,2,2,48,768]{4,3,2,1,0:T(8,128)(2,1)S(1)}, u32[]{:S(2)}, u32[]{:S(2)}) %collective-permute-start.6) | collective-permute-done | bytes 589856 | tf_op jit(solution)/shard_map/ppermute | solution.py:730
  53.0 5.0 %collective-permute-done.13.refs_3_ = bf16[2,4,48,768]{3,2,1,0:T(8,128)(2,1)S(1)} collective-permute-done((bf16[2,4,48,768]{3,2,1,0:T(8,128)(2,1)S(1)}, bf16[2,4,48,768]{3,2,1,0:T(8,128)(2,1)S(1)}, u32[]{:S(2)}, u32[]{:S(2)}) %collective-permute-start.13) | collective-permute-done | bytes 589856 | tf_op jit(solution)/shard_map/ppermute | solution.py:730
  62.5 12.8 %attend.1 = (bf16[2,1088,576]{2,1,0:T(8,128)(2,1)}, bf16[4,2,3,256,256]{4,3,2,1,0:T(8,128)(2,1)}, bf16[2,1088,192]{2,1,0:T(8,128)(2,1)}, bf16[1088,768]{1,0:T(8,128)(2,1)}) custom-call(s32[4]{0:T(128)} %copy-done.23, bf16[1088,768]{1,0:T(8,128)(2,1)} %copy-done.3, bf16[2,4,48,768]{3,2,1,0:T(8,128)(2,1)} %copy-done.27, bf16[2,4,48,768]{3,2,1,0:T(8,128)(2,1)} %copy-done.32, ...), custom_call_target="tpu_custom_call" | custom-call | flops 2242500096 | bytes 1 | tf_op jit(solution)/shard_map/attend/pallas_call | solution.py:270
  79.2 17.3 %mlp.2 = (bf16[1088,768]{1,0:T(8,128)(2,1)}, bf16[1088,768]{1,0:T(8,128)(2,1)}, bf16[1088,768]{1,0:T(8,128)(2,1)}, bf16[1088,768]{1,0:T(8,128)(2,1)}, bf16[8,2,4...) custom-call(bf16[8,2,48,768]{3,2,1,0:T(8,128)(2,1)} %bitcast.78, ...), custom_call_target="tpu_custom_call" | custom-call | flops 2932499968 | bytes 1 | tf_op jit(solution)/shard_map/mlp/pallas_call | solution.py:393
  96.5 7.5 %collective-permute-done.18 = bf16[2,4,2,48,768]{4,3,2,1,0:T(8,128)(2,1)} collective-permute-done((bf16[2,4,2,48,768]{4,3,2,1,0:T(8,128)(2,1)S(1)}, bf16[2,4,2,48,768]{4,3,2,1,0:T(8,128)(2,1)}, u32[]{:S(2)}, u32[]{:S(2)}) %collective-permute-start.18) | collective-permute-done | bytes 1179680 | tf_op jit(solution)/shard_map/ppermute | solution.py:730
  104.5 15.9 %mlp.3 = (bf16[1088,768]{1,0:T(8,128)(2,1)}, bf16[1088,768]{1,0:T(8,128)(2,1)}, bf16[8,2,48,768]{3,2,1,0:T(8,128)(2,1)}, bf16[8,2,48,768]{3,2,1,0:T(8,128)(2,1)}, f32[1,768]{1,0:T(1,128)}) custom-call(bf16[8,2,48,768]{3,2,1,0:T(8,128)(2,1)} %bitcast.29.refs_0_, bf16[8,2,48,768]{3,2,1,0:T(8,128)(2,1)} %bitcast.30.refs_1_, ...), custom_call_target="tpu_custom_call" | custom-call | flops 2932499968 | bytes 1 | tf_op jit(solution)/shard_map/mlp/pallas_call | solution.py:393
  124.3 18.7 %back.1 = (bf16[1088,768]{1,0:T(8,128)(2,1)}, bf16[2,1088,576]{2,1,0:T(8,128)(2,1)}, bf16[1088,768]{1,0:T(8,128)(2,1)}, f32[8,768]{1,0:T(8,128)}) custom-call(s32[4]{0:T(128)} %copy-done.23, bf16[1088,768]{1,0:T(8,128)(2,1)} %get-tuple-element.165.middle, bf16[1088,768]{1,0:T(8,128)(2,1)} %get-tuple-element.170.one, ...), custom_call_target="tpu_custom_call" | custom-call | flops 3277499904 | bytes 1 | tf_op jit(solution)/shard_map/back/pallas_call | solution.py:595
  143.8 9.3 %weight_grads.1 = (bf16[2,4,48,768]{3,2,1,0:T(8,128)(2,1)}, bf16[2,4,48,768]{3,2,1,0:T(8,128)(2,1)}, bf16[2,4,48,768]{3,2,1,0:T(8,128)(2,1)}, bf16[2,4,48,768]{3,2,1,0:T(8,128)(2,1)}) custom-call(s32[4]{0:T(128)} %copy-done.23, bf16[1088,768]{1,0:T(8,128)(2,1)} %copy-done.3, bf16[1088,768]{1,0:T(8,128)(2,1)} %get-tuple-element.175.grad_proj.gm, ...), custom_call_target="tpu_custom_call" | custom-call | flops 1552499968 | bytes 1 | tf_op jit(solution)/shard_map/weight_grads/pallas_call | solution.py:654
  160.6 1.8 collective-permute-start.24
  168.0 5.6 %last.1 = (f32[512,768]{1,0:T(8,128)}, bf16[48,768]{1,0:T(8,128)(2,1)S(1)}, f32[56,768]{1,0:T(8,128)S(1)}, f32[8,768]{1,0:T(8,128)S(1)}) custom-call(bf16[1088,768]{1,0:T(8,128)(2,1)S(1)} %copy-done.5, bf16[1088,768]{1,0:T(8,128)(2,1)S(1)} %copy-done.2, bf16[1088,768]{1,0:T(8,128)(2,1)S(1)} %copy-done.6, bf16[1088,768]{1,0:T(8,128)(2,1)S(1)} %copy-done.8, ...), custom_call_target="tpu_custom_call" | custom-call | flops 1207500032 | bytes 1 | tf_op jit(solution)/shard_map/last/pallas_call | solution.py:696
  173.8 5.7 %finish.1 = (bf16[512,768]{1,0:T(8,128)(2,1)}, bf16[48,768]{1,0:T(8,128)(2,1)S(1)}) custom-call(bf16[1088,768]{1,0:T(8,128)(2,1)S(1)} %copy-done, bf16[1088,768]{1,0:T(8,128)(2,1)} %get-tuple-element.174.one, bf16[1088,768]{1,0:T(8,128)(2,1)} %collective-permute-done.20.two, s32[1,512]{1,0:T(1,128)S(1)} %get-tuple-element.156.dest_own, ...), custom_call_target="tpu_custom_call" | custom-call | flops 862499968 | bytes 1 | tf_op jit(solution)/shard_map/finish/pallas_call | solution.py:512
  179.6 1.8 fold_first.2
  183.0 4.2 %collective-permute-done.24.a_got = bf16[2,4,48,768]{3,2,1,0:T(8,128)(2,1)} collective-permute-done((bf16[2,4,48,768]{3,2,1,0:T(8,128)(2,1)}, bf16[2,4,48,768]{3,2,1,0:T(8,128)(2,1)}, u32[]{:S(2)}, u32[]{:S(2)}) %collective-permute-start.24) | collective-permute-done | bytes 589856 | tf_op jit(solution)/shard_map/ppermute | solution.py:730
  192.3 4.2 %collective-permute-done.29 = bf16[62,768]{1,0:T(8,128)(2,1)S(1)} collective-permute-done((bf16[62,768]{1,0:T(8,128)(2,1)S(1)}, bf16[62,768]{1,0:T(8,128)(2,1)S(1)}, u32[]{:S(2)}, u32[]{:S(2)}) %collective-permute-start.29) | collective-permute-done | bytes 95264 | tf_op jit(solution)/shard_map/ppermute | solution.py:730
  197.9 2.4 %collective-permute-start.36 = (bf16[1,2,2,48,768]{4,3,2,1,0:T(8,128)(2,1)S(1)}, bf16[1,2,2,48,768]{4,3,2,1,0:T(8,128)(2,1)S(1)}, u32[]{:S(2)}, u32[]{:S(2)}) collective-permute-start(bf16[1,2,2,48,768]{4,3,2,1,0:T(8,128)(2,1)S(1)} %get-tuple-element.212), channel_id=1, source_target_pairs={{0,16},{1,17},{2,18},{3,19},{4,20},{5,21},{6,22},{7,23},{8,24},{9,... | collective-permute-start | bytes 884744 | tf_op jit(solution)/shard_map/ppermute | solution.py:730
  209.4 4.5 %collective-permute-done.34.refs_1_ = bf16[2,2,48,768]{3,2,1,0:T(8,128)(2,1)S(1)} collective-permute-done((bf16[2,2,48,768]{3,2,1,0:T(8,128)(2,1)S(1)}, bf16[2,2,48,768]{3,2,1,0:T(8,128)(2,1)S(1)}, u32[]{:S(2)}, u32[]{:S(2)}) %collective-permute-start.34) | collective-permute-done | bytes 294944 | tf_op jit(solution)/shard_map/ppermute | solution.py:730
  216.4 2.1 collective-permute-done.37
  (226 shorter events, 75.6 us)
Async XLA Ops:
  5.0 11.9 %collective-permute-start.3 = (bf16[1040,768]{1,0:T(8,128)(2,1)S(1)}, bf16[1040,768]{1,0:T(8,128)(2,1)S(1)}, u32[]{:S(2)}, u32[]{:S(2)}) collective-permute-start(bf16[1040,768]{1,0:T(8,128)(2,1)S(1)} %fusion.1.own), channel_id=1, source_target_pairs={{0,1},{1,0},{2,3},{3,2},{4,5},{5,4},{6,7},{7,6},{8,9},{9,8},{10,11... | collective-permute-start | bytes 4792328 | tf_op jit(solution)/shard_map/ppermute | solution.py:730
  22.5 13.1 %collective-permute-start.7 = (bf16[2,2,48,768]{3,2,1,0:T(8,128)(2,1)S(1)}, bf16[2,2,48,768]{3,2,1,0:T(8,128)(2,1)S(1)}, u32[]{:S(2)}, u32[]{:S(2)}) collective-permute-start(bf16[2,2,48,768]{3,2,1,0:T(8,128)(2,1)S(1)} %pad_maximum_fusion.8), channel_id=1, source_target_pairs={{0,8},{1,9},{2,10},{3,11},{4,12},{5,13},{6,14},{7,15},{8,0},{9,1},... | collective-permute-start | bytes 884744 | tf_op jit(solution)/shard_map/ppermute | solution.py:730
  23.6 15.3 %collective-permute-start.5 = (bf16[2,1,2,48,768]{4,3,2,1,0:T(8,128)(2,1)}, bf16[2,1,2,48,768]{4,3,2,1,0:T(8,128)(2,1)S(1)}, u32[]{:S(2)}, u32[]{:S(2)}) collective-permute-start(bf16[2,1,2,48,768]{4,3,2,1,0:T(8,128)(2,1)} %bitcast.72), channel_id=1, source_target_pairs={{0,16},{1,17},{2,18},{3,19},{4,20},{5,21},{6,22},{7,23},{8,24},{9,... | collective-permute-start | bytes 884744 | tf_op jit(solution)/shard_map/ppermute | solution.py:730
  39.0 13.8 %collective-permute-start.6 = (bf16[2,2,2,48,768]{4,3,2,1,0:T(8,128)(2,1)S(1)}, bf16[2,2,2,48,768]{4,3,2,1,0:T(8,128)(2,1)S(1)}, u32[]{:S(2)}, u32[]{:S(2)}) collective-permute-start(bf16[2,2,2,48,768]{4,3,2,1,0:T(8,128)(2,1)S(1)} %pad_maximum_fusion.3), channel_id=1, source_target_pairs={{0,8},{1,9},{2,10},{3,11},{4,12},{5,13},{6,14},{7,15},{8,0},{9,1},... | collective-permute-start | bytes 1769480 | tf_op jit(solution)/shard_map/ppermute | solution.py:730
  44.9 13.0 %collective-permute-start.13 = (bf16[2,4,48,768]{3,2,1,0:T(8,128)(2,1)S(1)}, bf16[2,4,48,768]{3,2,1,0:T(8,128)(2,1)S(1)}, u32[]{:S(2)}, u32[]{:S(2)}) collective-permute-start(bf16[2,4,48,768]{3,2,1,0:T(8,128)(2,1)S(1)} %pad_maximum_fusion.6.refs_2_), channel_id=1, source_target_pairs={{0,2},{1,3},{2,0},{3,1},{4,6},{5,7},{6,4},{7,5},{8,10},{9,11},{10,... | collective-permute-start | bytes 1769480 | tf_op jit(solution)/shard_map/ppermute | solution.py:730
  45.6 12.8 %collective-permute-start.12 = (bf16[2,4,48,768]{3,2,1,0:T(8,128)(2,1)S(1)}, bf16[2,4,48,768]{3,2,1,0:T(8,128)(2,1)S(1)}, u32[]{:S(2)}, u32[]{:S(2)}) collective-permute-start(bf16[2,4,48,768]{3,2,1,0:T(8,128)(2,1)S(1)} %pad_maximum_fusion.5.refs_0_), channel_id=1, source_target_pairs={{0,4},{1,5},{2,6},{3,7},{4,0},{5,1},{6,2},{7,3},{8,12},{9,13},{10,... | collective-permute-start | bytes 1769480 | tf_op jit(solution)/shard_map/ppermute | solution.py:730
  59.3 16.1 %collective-permute-start.14 = (bf16[4,2,48,768]{3,2,1,0:T(8,128)(2,1)S(1)}, bf16[4,2,48,768]{3,2,1,0:T(8,128)(2,1)S(1)}, u32[]{:S(2)}, u32[]{:S(2)}) collective-permute-start(bf16[4,2,48,768]{3,2,1,0:T(8,128)(2,1)S(1)} %get-tuple-element.249), channel_id=1, source_target_pairs={{0,2},{1,3},{2,0},{3,1},{4,6},{5,7},{6,4},{7,5},{8,10},{9,11},{10,... | collective-permute-start | bytes 1769480 | tf_op jit(solution)/shard_map/ppermute | solution.py:730
  60.7 14.6 %collective-permute-start.15 = (bf16[4,2,48,768]{3,2,1,0:T(8,128)(2,1)S(1)}, bf16[4,2,48,768]{3,2,1,0:T(8,128)(2,1)S(1)}, u32[]{:S(2)}, u32[]{:S(2)}) collective-permute-start(bf16[4,2,48,768]{3,2,1,0:T(8,128)(2,1)S(1)} %get-tuple-element.250), channel_id=1, source_target_pairs={{0,4},{1,5},{2,6},{3,7},{4,0},{5,1},{6,2},{7,3},{8,12},{9,13},{10,... | collective-permute-start | bytes 1769480 | tf_op jit(solution)/shard_map/ppermute | solution.py:730
  75.5 28.5 %collective-permute-start.18 = (bf16[2,4,2,48,768]{4,3,2,1,0:T(8,128)(2,1)S(1)}, bf16[2,4,2,48,768]{4,3,2,1,0:T(8,128)(2,1)}, u32[]{:S(2)}, u32[]{:S(2)}) collective-permute-start(bf16[2,4,2,48,768]{4,3,2,1,0:T(8,128)(2,1)S(1)} %pad_maximum_fusion.2), channel_id=1, source_target_pairs={{0,2},{1,3},{2,0},{3,1},{4,6},{5,7},{6,4},{7,5},{8,10},{9,11},{10,... | collective-permute-start | bytes 3538952 | tf_op jit(solution)/shard_map/ppermute | solution.py:730
  76.2 28.2 %collective-permute-start.17 = (bf16[2,4,2,48,768]{4,3,2,1,0:T(8,128)(2,1)S(1)}, bf16[2,4,2,48,768]{4,3,2,1,0:T(8,128)(2,1)}, u32[]{:S(2)}, u32[]{:S(2)}) collective-permute-start(bf16[2,4,2,48,768]{4,3,2,1,0:T(8,128)(2,1)S(1)} %pad_maximum_fusion.1), channel_id=1, source_target_pairs={{0,4},{1,5},{2,6},{3,7},{4,0},{5,1},{6,2},{7,3},{8,12},{9,13},{10,... | collective-permute-start | bytes 3538952 | tf_op jit(solution)/shard_map/ppermute | solution.py:730
  120.7 32.3 %collective-permute-start.23 = (bf16[2,4,2,48,768]{4,3,2,1,0:T(8,128)(2,1)}, bf16[2,4,2,48,768]{4,3,2,1,0:T(8,128)(2,1)S(1)}, u32[]{:S(2)}, u32[]{:S(2)}) collective-permute-start(bf16[2,4,2,48,768]{4,3,2,1,0:T(8,128)(2,1)} %bitcast.103), channel_id=1, source_target_pairs={{0,2},{1,3},{2,0},{3,1},{4,6},{5,7},{6,4},{7,5},{8,10},{9,11},{10,... | collective-permute-start | bytes 3538952 | tf_op jit(solution)/shard_map/ppermute | solution.py:730
  122.2 31.9 %collective-permute-start.22 = (bf16[2,4,2,48,768]{4,3,2,1,0:T(8,128)(2,1)}, bf16[2,4,2,48,768]{4,3,2,1,0:T(8,128)(2,1)S(1)}, u32[]{:S(2)}, u32[]{:S(2)}) collective-permute-start(bf16[2,4,2,48,768]{4,3,2,1,0:T(8,128)(2,1)} %bitcast.102), channel_id=1, source_target_pairs={{0,4},{1,5},{2,6},{3,7},{4,0},{5,1},{6,2},{7,3},{8,12},{9,13},{10,... | collective-permute-start | bytes 3538952 | tf_op jit(solution)/shard_map/ppermute | solution.py:730
  143.1 19.3 %collective-permute-start.21 = (bf16[1088,768]{1,0:T(8,128)(2,1)}, bf16[1088,768]{1,0:T(8,128)(2,1)S(1)}, u32[]{:S(2)}, u32[]{:S(2)}) collective-permute-start(bf16[1088,768]{1,0:T(8,128)(2,1)} %get-tuple-element.173.one), channel_id=1, source_target_pairs={{0,1},{1,0},{2,3},{3,2},{4,5},{5,4},{6,7},{7,6},{8,9},{9,8},{10,11... | collective-permute-start | bytes 5013512 | tf_op jit(solution)/shard_map/ppermute | solution.py:730
  143.3 30.3 %collective-permute-start.20 = (bf16[1088,768]{1,0:T(8,128)(2,1)}, bf16[1088,768]{1,0:T(8,128)(2,1)}, u32[]{:S(2)}, u32[]{:S(2)}) collective-permute-start(bf16[1088,768]{1,0:T(8,128)(2,1)} %get-tuple-element.174.one), channel_id=1, source_target_pairs={{0,1},{1,0},{2,3},{3,2},{4,5},{5,4},{6,7},{7,6},{8,9},{9,8},{10,11... | collective-permute-start | bytes 5013512 | tf_op jit(solution)/shard_map/ppermute | solution.py:730
  158.8 20.7 %collective-permute-start.28 = (bf16[4,2,48,768]{3,2,1,0:T(8,128)(2,1)}, bf16[4,2,48,768]{3,2,1,0:T(8,128)(2,1)}, u32[]{:S(2)}, u32[]{:S(2)}) collective-permute-start(bf16[4,2,48,768]{3,2,1,0:T(8,128)(2,1)} %get-tuple-element.193), channel_id=1, source_target_pairs={{0,4},{1,5},{2,6},{3,7},{4,0},{5,1},{6,2},{7,3},{8,12},{9,13},{10,... | collective-permute-start | bytes 1769480 | tf_op jit(solution)/shard_map/ppermute | solution.py:730
  159.6 19.9 %collective-permute-start.27 = (bf16[4,2,48,768]{3,2,1,0:T(8,128)(2,1)}, bf16[4,2,48,768]{3,2,1,0:T(8,128)(2,1)}, u32[]{:S(2)}, u32[]{:S(2)}) collective-permute-start(bf16[4,2,48,768]{3,2,1,0:T(8,128)(2,1)} %get-tuple-element.185), channel_id=1, source_target_pairs={{0,2},{1,3},{2,0},{3,1},{4,6},{5,7},{6,4},{7,5},{8,10},{9,11},{10,... | collective-permute-start | bytes 1769480 | tf_op jit(solution)/shard_map/ppermute | solution.py:730
  160.6 26.5 %collective-permute-start.24 = (bf16[2,4,48,768]{3,2,1,0:T(8,128)(2,1)}, bf16[2,4,48,768]{3,2,1,0:T(8,128)(2,1)}, u32[]{:S(2)}, u32[]{:S(2)}) collective-permute-start(bf16[2,4,48,768]{3,2,1,0:T(8,128)(2,1)} %get-tuple-element.191), channel_id=1, source_target_pairs={{0,4},{1,5},{2,6},{3,7},{4,0},{5,1},{6,2},{7,3},{8,12},{9,13},{10,... | collective-permute-start | bytes 1769480 | tf_op jit(solution)/shard_map/ppermute | solution.py:730
  163.7 23.9 %collective-permute-start.25 = (bf16[2,4,48,768]{3,2,1,0:T(8,128)(2,1)}, bf16[2,4,48,768]{3,2,1,0:T(8,128)(2,1)}, u32[]{:S(2)}, u32[]{:S(2)}) collective-permute-start(bf16[2,4,48,768]{3,2,1,0:T(8,128)(2,1)} %get-tuple-element.194), channel_id=1, source_target_pairs={{0,2},{1,3},{2,0},{3,1},{4,6},{5,7},{6,4},{7,5},{8,10},{9,11},{10,... | collective-permute-start | bytes 1769480 | tf_op jit(solution)/shard_map/ppermute | solution.py:730
  181.3 16.4 %collective-permute-start.33 = (bf16[2,2,2,48,768]{4,3,2,1,0:T(8,128)(2,1)S(1)}, bf16[2,2,2,48,768]{4,3,2,1,0:T(8,128)(2,1)S(1)}, u32[]{:S(2)}, u32[]{:S(2)}) collective-permute-start(bf16[2,2,2,48,768]{4,3,2,1,0:T(8,128)(2,1)S(1)} %get-tuple-element.203), channel_id=1, source_target_pairs={{0,8},{1,9},{2,10},{3,11},{4,12},{5,13},{6,14},{7,15},{8,0},{9,1},... | collective-permute-start | bytes 1769480 | tf_op jit(solution)/shard_map/ppermute | solution.py:730
  188.8 11.4 %collective-permute-start.32 = (bf16[4,48,768]{2,1,0:T(8,128)(2,1)S(1)}, bf16[4,48,768]{2,1,0:T(8,128)(2,1)S(1)}, u32[]{:S(2)}, u32[]{:S(2)}) collective-permute-start(bf16[4,48,768]{2,1,0:T(8,128)(2,1)S(1)} %get-tuple-element.209), channel_id=1, source_target_pairs={{0,4},{1,5},{2,6},{3,7},{4,0},{5,1},{6,2},{7,3},{8,12},{9,13},{10,... | collective-permute-start | bytes 884744 | tf_op jit(solution)/shard_map/ppermute | solution.py:730
  190.2 10.0 %collective-permute-start.31 = (bf16[4,48,768]{2,1,0:T(8,128)(2,1)S(1)}, bf16[4,48,768]{2,1,0:T(8,128)(2,1)S(1)}, u32[]{:S(2)}, u32[]{:S(2)}) collective-permute-start(bf16[4,48,768]{2,1,0:T(8,128)(2,1)S(1)} %get-tuple-element.208), channel_id=1, source_target_pairs={{0,2},{1,3},{2,0},{3,1},{4,6},{5,7},{6,4},{7,5},{8,10},{9,11},{10,... | collective-permute-start | bytes 884744 | tf_op jit(solution)/shard_map/ppermute | solution.py:730
  191.7 9.9 %collective-permute-start.30 = (bf16[96,768]{1,0:T(8,128)(2,1)S(1)}, bf16[96,768]{1,0:T(8,128)(2,1)S(1)}, u32[]{:S(2)}, u32[]{:S(2)}) collective-permute-start(bf16[96,768]{1,0:T(8,128)(2,1)S(1)} %pad_maximum_fusion.10), channel_id=1, source_target_pairs={{0,2},{1,3},{2,0},{3,1},{4,6},{5,7},{6,4},{7,5},{8,10},{9,11},{10,... | collective-permute-start | bytes 442376 | tf_op jit(solution)/shard_map/ppermute | solution.py:730
  197.9 16.0 %collective-permute-start.36 = (bf16[1,2,2,48,768]{4,3,2,1,0:T(8,128)(2,1)S(1)}, bf16[1,2,2,48,768]{4,3,2,1,0:T(8,128)(2,1)S(1)}, u32[]{:S(2)}, u32[]{:S(2)}) collective-permute-start(bf16[1,2,2,48,768]{4,3,2,1,0:T(8,128)(2,1)S(1)} %get-tuple-element.212), channel_id=1, source_target_pairs={{0,16},{1,17},{2,18},{3,19},{4,20},{5,21},{6,22},{7,23},{8,24},{9,... | collective-permute-start | bytes 884744 | tf_op jit(solution)/shard_map/ppermute | solution.py:730
  201.5 12.3 %collective-permute-start.34 = (bf16[2,2,48,768]{3,2,1,0:T(8,128)(2,1)S(1)}, bf16[2,2,48,768]{3,2,1,0:T(8,128)(2,1)S(1)}, u32[]{:S(2)}, u32[]{:S(2)}) collective-permute-start(bf16[2,2,48,768]{3,2,1,0:T(8,128)(2,1)S(1)} %get-tuple-element.215), channel_id=1, source_target_pairs={{0,8},{1,9},{2,10},{3,11},{4,12},{5,13},{6,14},{7,15},{8,0},{9,1},... | collective-permute-start | bytes 884744 | tf_op jit(solution)/shard_map/ppermute | solution.py:730
  (54 other events, 333.1 us)
